TPU v7x, 256 devices: a whole 4x4x8 slice. The times are simulated.
256 devices in a mesh: seq: 32 (over x, z), ch: 8 (over y, core).
Axes of the slice: x: 4, y: 4, z: 8, core: 2. Of those that a mesh axis runs over, the one named last changes fastest.
Arguments:
- outer_gate: bfloat16 [8192, 4096], P('seq', 'ch'), may hold values from -6 to 6
- inner_gate: bfloat16 [8192, 4096], P('seq', 'ch'), may hold values from -6 to 6
- values: bfloat16 [8192, 4096], P('seq', 'ch'), may hold values from -6 to 6
- filter_taps: float32 [8192, 4096], P('seq', 'ch'), may hold values from -2 to 2, as said below
- skip_scale: float32 [4096], P('ch'), may hold values from 0.5 to 1.5
- out_weight: bfloat16 [4096, 8192], P(None, 'ch'), may hold values from -0.09375 to 0.09375
- out_grad: bfloat16 [8192, 8192], P('seq', 'ch'), may hold values from -6 to 6
Outputs:
- mixed: bfloat16 [8192, 8192], P('seq', 'ch')
- outer_grad: bfloat16 [8192, 4096], P('seq', 'ch')
- inner_grad: bfloat16 [8192, 4096], P('seq', 'ch')
- values_grad: bfloat16 [8192, 4096], P('seq', 'ch')
- taps_grad: float32 [8192, 4096], P('seq', 'ch')
Inputs may be any that keep to these rules, and one draw needn't show every extreme that they name: `filter_taps`: taps of each channel's long filter.
All inputs are finite; a program needn't handle non-finite values.
Results may differ from a plain program's by a relative error of at most 0.015.
Values may be sent and summed in bfloat16 or wider, within the bound.
No kernel may reach another device: no remote copies, remote signals or barrier semaphores. Data moves between devices by JAX's collectives and lax.ppermute only.
A program may use at most 128 MiB of HBM per device.

v0:
```python
import math

import jax
import jax.numpy as jnp
import numpy as np
from jax import lax
from jax.experimental import pallas as pl
from jax.experimental.pallas import tpu as pltpu
from jax.sharding import PartitionSpec as P

SEQ_PARTS = 32
ROWS = 256
WIDTH = 512
LANE_CH = WIDTH // SEQ_PARTS
COLUMNS = 1024
SLOTS = 32
PADDED = 2 * SEQ_PARTS * ROWS
VMEM_LIMIT = 48 * 1024 * 1024


def transform_tables():
    q = np.arange(SLOTS) + 0.5
    p = np.arange(SEQ_PARTS)
    r = np.arange(ROWS)
    coarse = 2.0 * math.pi * np.outer(q, p) / (2 * SEQ_PARTS)
    eye = np.eye(LANE_CH)
    gather = np.concatenate([np.kron(np.cos(coarse), eye), np.kron(-np.sin(coarse), eye)], 0)
    spread = gather.T * (2.0 / PADDED)
    fine = 2.0 * math.pi * (np.outer(r, r) % ROWS) / ROWS
    cos, sin = np.cos(fine), np.sin(fine)
    turn = np.block([[cos, -sin], [sin, cos]])
    twist = 2.0 * math.pi * np.outer(q, r) / PADDED
    twist = np.repeat(twist, LANE_CH, 0)

    def half(a):
        return jnp.asarray(a, jnp.float32).astype(jnp.bfloat16)

    return (
        half(gather),
        half(spread),
        half(turn),
        jnp.asarray(np.cos(twist), jnp.float32),
        jnp.asarray(np.sin(twist), jnp.float32),
    )


def dot(a, b, contract=((1,), (0,))):
    return lax.dot_general(a, b, (contract, ((), ())), preferred_element_type=jnp.float32)


def bf16(a):
    return a.astype(jnp.bfloat16)


def forward(x, gather, turn, cos, sin):
    count = SLOTS * LANE_CH
    a = dot(gather[...], x)
    real, imag = a[:count], a[count:]
    c, s = cos[...], sin[...]
    b = jnp.concatenate([bf16(real * c + imag * s), bf16(imag * c - real * s)], 1)
    spec = dot(b, turn[...])
    return spec[:, :ROWS], spec[:, ROWS:]


def inverse(real, imag, spread, turn, cos, sin):
    y = jnp.concatenate([bf16(real), bf16(imag)], 1)
    z = dot(y, turn[...], ((1,), (1,)))
    real, imag = z[:, :ROWS], z[:, ROWS:]
    c, s = cos[...], sin[...]
    b = jnp.concatenate([bf16(real * c - imag * s), bf16(imag * c + real * s)], 0)
    return dot(spread[...], b)


def chunks(a):
    return bf16(a).reshape(SEQ_PARTS, LANE_CH, ROWS)


def flat(a):
    return a.reshape(WIDTH, ROWS)


def prepare_kernel(inner, values, taps, out):
    product = inner[...].astype(jnp.float32) * values[...].astype(jnp.float32)
    out[:, :LANE_CH, :] = chunks(product.T)
    out[:, LANE_CH:, :] = chunks(taps[...].T)


def gates_kernel(inner, values, outer, skip, outer_t, outer_skip_t, skip_product_t):
    product = inner[...].astype(jnp.float32) * values[...].astype(jnp.float32)
    out = outer[...].astype(jnp.float32)
    scale = skip[...]
    outer_t[...] = bf16(out.T)
    outer_skip_t[...] = (out * scale).T
    skip_product_t[...] = (product * scale).T


def project_kernel(order, weight, grad, out):
    out[...] = bf16(dot(weight[...], grad[...], ((1,), (1,))))


def project_add_kernel(order, weight, grad, other, out0, out1, out2, out3):
    step = pl.program_id(0)
    total = bf16(dot(weight[...], grad[...], ((1,), (1,))) + other[...].astype(jnp.float32))
    for i, out in enumerate((out0, out1, out2, out3)):

        @pl.when(step == i)
        def _():
            out[...] = total


def first_kernel(got, gather, spread, turn, cos, sin, conv, sr, si, tr, ti):
    x_real, x_imag = forward(flat(got[:, :LANE_CH, :]), gather, turn, cos, sin)
    sr[...] = x_real
    si[...] = x_imag
    t_real, t_imag = forward(flat(got[:, LANE_CH:, :]), gather, turn, cos, sin)
    tr[...] = t_real
    ti[...] = t_imag
    y = inverse(
        x_real * t_real - x_imag * t_imag, x_real * t_imag + x_imag * t_real, spread, turn, cos, sin
    )
    conv[...] = chunks(y)


def middle_kernel(own, a, b, c, outer_t, outer_skip_t, conv, out, hidden_grad_t, skip_grad_t):
    total = (own[...].astype(jnp.float32) + a[...].astype(jnp.float32)) + (
        b[...].astype(jnp.float32) + c[...].astype(jnp.float32)
    )
    hidden_grad_t[...] = total
    skip_grad_t[...] = total * outer_skip_t[...]
    out[:, :LANE_CH, :] = chunks(total * outer_t[...].astype(jnp.float32))
    out[:, LANE_CH:, :] = conv[...]


def second_kernel(got, sr, si, tr, ti, gather, spread, turn, cos, sin, out):
    g_real, g_imag = forward(flat(got[:, :LANE_CH, :]), gather, turn, cos, sin)
    t_real, t_imag = tr[...], ti[...]
    corr = inverse(
        t_real * g_real + t_imag * g_imag, t_real * g_imag - t_imag * g_real, spread, turn, cos, sin
    )
    out[:, :LANE_CH, :] = chunks(corr)
    x_real, x_imag = sr[...], si[...]
    lag = inverse(
        x_real * g_real + x_imag * g_imag, x_real * g_imag - x_imag * g_real, spread, turn, cos, sin
    )
    out[:, LANE_CH:, :] = chunks(lag)


def mix_kernel(got, skip_product_t, outer_t, hidden_grad_t, hidden_t, outer_grad):
    mixed_pre = flat(got[:, LANE_CH:, :]).astype(jnp.float32) + skip_product_t[...]
    hidden_t[...] = bf16(outer_t[...].astype(jnp.float32) * mixed_pre)
    outer_grad[...] = bf16((hidden_grad_t[...] * mixed_pre).T)


def final_kernel(got, skip_grad_t, inner, values, inner_grad, values_grad, taps_grad):
    total = (flat(got[:, :LANE_CH, :]).astype(jnp.float32) + skip_grad_t[...]).T
    inner_grad[...] = bf16(total * values[...].astype(jnp.float32))
    values_grad[...] = bf16(total * inner[...].astype(jnp.float32))
    taps_grad[...] = flat(got[:, LANE_CH:, :]).astype(jnp.float32).T


def blocks_kernel(n, has_base, last, order, *refs):
    parts = refs[:n]
    weight = refs[n]
    out = refs[-2]
    total = refs[-1]
    step = pl.program_id(0)

    @pl.when(step == 0)
    def _():
        total[...] = refs[n + 1][...] if has_base else jnp.zeros_like(total)

    for i in range(n):

        @pl.when(step == i)
        def _():
            total[...] += dot(parts[i][...], weight[...], ((0,), (0,)))

    @pl.when(step == n - 1)
    def _():
        out[...] = total[...].astype(out.dtype)


def shape(dims, dtype):
    return jax.ShapeDtypeStruct(dims, dtype)


def local(kernel, outs, *args, flops=0):
    moved = sum(math.prod(a.shape) * a.dtype.itemsize for a in (*args, *outs))
    return pl.pallas_call(
        kernel,
        out_shape=outs,
        in_specs=[pl.BlockSpec(memory_space=pltpu.VMEM)] * len(args),
        out_specs=tuple(pl.BlockSpec(memory_space=pltpu.VMEM) for _ in outs),
        compiler_params=pltpu.CompilerParams(vmem_limit_bytes=VMEM_LIMIT),
        cost_estimate=pl.CostEstimate(flops=flops, bytes_accessed=moved, transcendentals=0),
    )(*args)


def project(order, weight, grad, other=None):
    block = pl.BlockSpec((WIDTH, ROWS), lambda i, o: (i, 0))
    whole = pl.BlockSpec((WIDTH, ROWS), lambda i, o: (0, 0))
    specs = [
        pl.BlockSpec((WIDTH, COLUMNS), lambda i, o: (o[i], 0)),
        pl.BlockSpec((ROWS, COLUMNS), lambda i, o: (0, 0)),
    ]
    if other is None:
        kernel, outs, out_specs = project_kernel, shape((4 * WIDTH, ROWS), jnp.bfloat16), block
        args = (order, weight, grad)
    else:
        kernel = project_add_kernel
        outs = (shape((WIDTH, ROWS), jnp.bfloat16),) * 4
        out_specs = (whole,) * 4
        specs.append(block)
        args = (order, weight, grad, other)
    return pl.pallas_call(
        kernel,
        out_shape=outs,
        grid_spec=pltpu.PrefetchScalarGridSpec(
            num_scalar_prefetch=1, grid=(4,), in_specs=specs, out_specs=out_specs
        ),
        compiler_params=pltpu.CompilerParams(vmem_limit_bytes=VMEM_LIMIT),
        cost_estimate=pl.CostEstimate(
            flops=2 * 4 * WIDTH * ROWS * COLUMNS, bytes_accessed=6 << 20, transcendentals=0
        ),
    )(*args)


def blocks(order, parts, weight, base=None):
    n = len(parts)
    last = base is not None
    specs = [pl.BlockSpec((WIDTH, ROWS), lambda i, o: (0, 0))] * n
    specs.append(pl.BlockSpec((WIDTH, COLUMNS), lambda i, o: (o[i], 0)))
    args = (order, *parts, weight)
    if last:
        specs.append(pl.BlockSpec((ROWS, COLUMNS), lambda i, o: (0, 0)))
        args = (*args, base)

    def kernel(*refs):
        blocks_kernel(n, last, last, *refs)

    return pl.pallas_call(
        kernel,
        out_shape=shape((ROWS, COLUMNS), jnp.bfloat16 if last else jnp.float32),
        grid_spec=pltpu.PrefetchScalarGridSpec(
            num_scalar_prefetch=1,
            grid=(n,),
            in_specs=specs,
            out_specs=pl.BlockSpec((ROWS, COLUMNS), lambda i, o: (0, 0)),
            scratch_shapes=[pltpu.VMEM((ROWS, COLUMNS), jnp.float32)],
        ),
        compiler_params=pltpu.CompilerParams(vmem_limit_bytes=VMEM_LIMIT),
        cost_estimate=pl.CostEstimate(
            flops=2 * n * WIDTH * ROWS * COLUMNS, bytes_accessed=(n + 2) << 20, transcendentals=0
        ),
    )(*args)


def exchange(a):
    return lax.all_to_all(a, "seq", split_axis=0, concat_axis=0, tiled=True)


def to_partner(a):
    return lax.ppermute(a, "ch", [(i, i ^ 1) for i in range(8)])


def along(a, shift):
    return lax.ppermute(a, "ch", [(i, (i + 2 * shift) % 8) for i in range(8)])


def on_device(outer_gate, inner_gate, values, filter_taps, skip_scale, out_weight, out_grad):
    tables = transform_tables()
    me = lax.axis_index("ch").astype(jnp.int32)
    row, core = me // 2, me % 2
    steps = jnp.arange(4, dtype=jnp.int32)
    ahead = 2 * ((row + steps) % 4)
    behind = 2 * ((row - steps + 4) % 4)
    pass_flops = 2 * 1024 * 512 * 256

    sent = local(
        prepare_kernel, (shape((SEQ_PARTS, 2 * LANE_CH, ROWS), jnp.bfloat16),), inner_gate, values, filter_taps
    )[0]
    got = exchange(sent)

    given = project(ahead + (1 - core), out_weight, out_grad)
    own = project(ahead + core, out_weight, out_grad, to_partner(given))
    sums = [own[0], along(own[2], 2), along(own[1], 1), along(own[3], 3)]

    full = shape((WIDTH, ROWS), jnp.float32)
    outer_t, outer_skip_t, skip_product_t = local(
        gates_kernel,
        (shape((WIDTH, ROWS), jnp.bfloat16), full, full),
        inner_gate,
        values,
        outer_gate,
        skip_scale.reshape(1, WIDTH),
    )
    spectrum = shape((SLOTS * LANE_CH, ROWS), jnp.float32)
    conv, *spectra = local(
        first_kernel,
        (shape((SEQ_PARTS, LANE_CH, ROWS), jnp.bfloat16),) + (spectrum,) * 4,
        got,
        *tables,
        flops=6 * pass_flops,
    )
    sent, hidden_grad_t, skip_grad_t = local(
        middle_kernel,
        (shape((SEQ_PARTS, 2 * LANE_CH, ROWS), jnp.bfloat16), full, full),
        *sums,
        outer_t,
        outer_skip_t,
        conv,
    )
    got = exchange(sent)
    sent = local(
        second_kernel,
        (shape((SEQ_PARTS, 2 * LANE_CH, ROWS), jnp.bfloat16),),
        got,
        *spectra,
        *tables,
        flops=6 * pass_flops,
    )[0]
    returned = exchange(sent)
    hidden_t, outer_grad = local(
        mix_kernel,
        (shape((WIDTH, ROWS), jnp.bfloat16), shape((ROWS, WIDTH), jnp.bfloat16)),
        got,
        skip_product_t,
        outer_t,
        hidden_grad_t,
    )
    near = [hidden_t, along(hidden_t, 1), along(hidden_t, 2), along(hidden_t, 3)]
    far = [to_partner(a) for a in near]
    near_order = jnp.concatenate([behind + core, behind[:1] + (1 - core)])
    part = blocks(near_order, near + far[:1], out_weight)
    mixed = blocks(behind[1:] + (1 - core), far[1:], out_weight, part)
    inner_grad, values_grad, taps_grad = local(
        final_kernel,
        (
            shape((ROWS, WIDTH), jnp.bfloat16),
            shape((ROWS, WIDTH), jnp.bfloat16),
            shape((ROWS, WIDTH), jnp.float32),
        ),
        returned,
        skip_grad_t,
        inner_gate,
        values,
    )
    return (mixed, outer_grad, inner_grad, values_grad, taps_grad)


def solution(mesh):
    placed = (
        P("seq", "ch"),
        P("seq", "ch"),
        P("seq", "ch"),
        P("seq", "ch"),
        P("ch"),
        P(None, "ch"),
        P("seq", "ch"),
    )
    return jax.shard_map(
        on_device,
        mesh=mesh,
        in_specs=placed,
        out_specs=(P("seq", "ch"), P("seq", "ch"), P("seq", "ch"), P("seq", "ch"), P("seq", "ch")),
        check_vma=False,
    )
```

profile of v0, /device:TPU:1, one launch (start us, length us, event | category | flops | bytes accessed | tf_op | source)
XLA Modules:
  0.0 115.9 jit_solution(1196623293060340306)
XLA Ops:
  0.7 1.1 copy-done.2
  1.8 4.5 %shard_map.155 = bf16[2048,256]{1,0:T(8,128)(2,1)S(1)} custom-call(s32[4]{0:T(128)S(1)} %broadcast_add_fusion.order, bf16[4096,1024]{1,0:T(8,128)(2,1)} %refs_4_.1, bf16[256,1024]{1,0:T(8,128)(2,1)S(1)} %copy-done.2), custom_call_target="tpu_custom_call" | custom-call | flops 1073741824 | bytes 6291456 | tf_op jit(solution)/shard_map/pallas_call | solution.py:215
  6.4 3.3 %collective-permute-start = (bf16[2048,256]{1,0:T(8,128)(2,1)S(1)}, bf16[2048,256]{1,0:T(8,128)(2,1)S(1)}, u32[]{:S(2)}, u32[]{:S(2)}) collective-permute-start(bf16[2048,256]{1,0:T(8,128)(2,1)S(1)} %shard_map.155), channel_id=1, source_target_pairs={{0,1},{1,0},{2,3},{3,2},{4,5},{5,4},{6,7},{7,6},{8,9},{9,8},{10,11... | collective-permute-start | bytes 3145736 | tf_op jit(solution)/shard_map/ppermute | solution.py:263
  9.7 1.0 shard_map.158
  10.7 9.4 %all-to-all-start = ((bf16[32,32,256]{2,1,0:T(8,128)(2,1)}), bf16[32,32,256]{2,1,0:T(8,128)(2,1)}, u32[]{:S(2)}, u32[]{:S(2)}) async-start(bf16[32,32,256]{2,1,0:T(8,128)(2,1)} %shard_map.158), calls=%async_computation | async-start | bytes 1048576 | tf_op jit(solution)/shard_map/all_to_all | solution.py:259
  20.2 5.5 %shard_map.156 = (bf16[512,256]{1,0:T(8,128)(2,1)S(1)}, bf16[512,256]{1,0:T(8,128)(2,1)}, bf16[512,256]{1,0:T(8,128)(2,1)}, bf16[512,256]{1,0:T(8,128)(2,1)}) custom-call(s32[4]{0:T(128)S(1)} %broadcast_add_fusion.2.order, bf16[4096,1024]{1,0:T(8,128)(2,1)} %refs_4_.1, bf16[256,1024]{1,0:T(8,128)(2,1)S(1)} %copy-done.3, ...), custom_call_target="tpu_custom_call" | custom-call | flops 1073741824 | bytes 6291456 | tf_op jit(solution)/shard_map/pallas_call | solution.py:215
  26.4 2.9 %collective-permute-start.1 = (bf16[512,256]{1,0:T(8,128)(2,1)}, bf16[512,256]{1,0:T(8,128)(2,1)S(1)}, u32[]{:S(2)}, u32[]{:S(2)}) collective-permute-start(bf16[512,256]{1,0:T(8,128)(2,1)} %get-tuple-element.26), channel_id=1, source_target_pairs={{0,4},{1,5},{2,6},{3,7},{4,0},{5,1},{6,2},{7,3},{8,12},{9,13},{10,... | collective-permute-start | bytes 786440 | tf_op jit(solution)/shard_map/ppermute | solution.py:267
  29.7 2.3 %collective-permute-start.3 = (bf16[512,256]{1,0:T(8,128)(2,1)}, bf16[512,256]{1,0:T(8,128)(2,1)}, u32[]{:S(2)}, u32[]{:S(2)}) collective-permute-start(bf16[512,256]{1,0:T(8,128)(2,1)} %get-tuple-element.28), channel_id=1, source_target_pairs={{0,6},{1,7},{2,0},{3,1},{4,2},{5,3},{6,4},{7,5},{8,14},{9,15},{10,... | collective-permute-start | bytes 786440 | tf_op jit(solution)/shard_map/ppermute | solution.py:267
  32.4 0.8 copy-done.8
  33.2 1.7 %all-to-all-done.got = bf16[32,32,256]{2,1,0:T(8,128)(2,1)} async-done(((bf16[32,32,256]{2,1,0:T(8,128)(2,1)}), bf16[32,32,256]{2,1,0:T(8,128)(2,1)}, u32[]{:S(2)}, u32[]{:S(2)}) %all-to-all-start) | async-done | bytes 524320 | tf_op jit(solution)/shard_map/all_to_all | solution.py:259
  35.0 1.0 copy-done.12
  36.0 1.0 copy-done.14
  37.0 1.0 copy-done.16
  38.1 3.8 %shard_map.159 = (bf16[32,16,256]{2,1,0:T(8,128)(2,1)S(1)}, f32[512,256]{1,0:T(8,128)S(1)}, f32[512,256]{1,0:T(8,128)S(1)}, f32[512,256]{1,0:T(8,128)S(1)}, f32[512,256]{1,0:T(8,128)S(1)}) custom-call(bf16[32,32,256]{2,1,0:T(8,128)(2,1)} %all-to-all-done.got, bf16[1024,512]{1,0:T(8,128)(2,1)S(1)} %copy-done.4, bf16[512,1024]{1,0:T(8,128)(2,1)} %constant.66.spread, ...), custom_call_target="tpu_custom_call" | custom-call | flops 1610612736 | bytes 6553600 | tf_op jit(solution)/shard_map/pallas_call | solution.py:189
  42.1 0.9 copy-done.19
  43.0 1.3 %shard_map.160 = (bf16[32,32,256]{2,1,0:T(8,128)(2,1)S(1)}, f32[512,256]{1,0:T(8,128)S(1)}, f32[512,256]{1,0:T(8,128)S(1)}) custom-call(bf16[512,256]{1,0:T(8,128)(2,1)S(1)} %copy-done.19, bf16[512,256]{1,0:T(8,128)(2,1)S(1)} %collective-permute-done.1.a, bf16[512,256]{1,0:T(8,128)(2,1)} %collective-permute-done.2.b, ...), custom_call_target="tpu_custom_call" | custom-call | bytes 3670016 | tf_op jit(solution)/shard_map/pallas_call | solution.py:189
  45.1 23.0 %all_to_all.15.got = bf16[32,32,256]{2,1,0:T(8,128)(2,1)S(1)} all-to-all(bf16[32,32,256]{2,1,0:T(8,128)(2,1)S(1)} %get-tuple-element.32), channel_id=1, replica_groups=mesh['seq'=32,'ch'=8] {'seq'}, dimensions={0} | all-to-all | bytes 1048576 | tf_op jit(solution)/shard_map/all_to_all | solution.py:259
  68.1 1.0 copy-done.13
  69.1 1.0 copy-done.15
  70.2 4.6 %shard_map.164 = bf16[32,32,256]{2,1,0:T(8,128)(2,1)} custom-call(bf16[32,32,256]{2,1,0:T(8,128)(2,1)S(1)} %all_to_all.15.got, f32[512,256]{1,0:T(8,128)S(1)} %get-tuple-element.37.sr, f32[512,256]{1,0:T(8,128)S(1)} %get-tuple-element.38.si, f32[512,256]{1,0:T(8,128)S(1)} %get-tuple-element.39.tr, f32[512,256]{1,0:T(8,128)S(1)} %get-tuple-element.40.ti, ...), custom_call_target="tpu_custom_call" | custom-call | flops 1610612736 | bytes 6815744 | tf_op jit(solution)/shard_map/pallas_call | solution.py:189
  74.7 7.8 %all-to-all-start.2 = ((bf16[32,32,256]{2,1,0:T(8,128)(2,1)}), bf16[32,32,256]{2,1,0:T(8,128)(2,1)S(1)}, u32[]{:S(2)}, u32[]{:S(2)}) async-start(bf16[32,32,256]{2,1,0:T(8,128)(2,1)} %shard_map.164), calls=%async_computation.2 | async-start | bytes 1048576 | tf_op jit(solution)/shard_map/all_to_all | solution.py:259
  82.5 1.0 copy-done.9
  83.6 1.0 copy-done.11
  84.6 0.9 shard_map.161
  85.5 2.7 %collective-permute-start.8 = (bf16[512,256]{1,0:T(8,128)(2,1)S(1)}, bf16[512,256]{1,0:T(8,128)(2,1)S(1)}, u32[]{:S(2)}, u32[]{:S(2)}) collective-permute-start(bf16[512,256]{1,0:T(8,128)(2,1)S(1)} %get-tuple-element.35.refs_1_), channel_id=1, source_target_pairs={{0,6},{1,7},{2,0},{3,1},{4,2},{5,3},{6,4},{7,5},{8,14},{9,15},{10,... | collective-permute-start | bytes 786440 | tf_op jit(solution)/shard_map/ppermute | solution.py:267
  88.8 2.5 %collective-permute-start.10 = (bf16[512,256]{1,0:T(8,128)(2,1)S(1)}, bf16[512,256]{1,0:T(8,128)(2,1)S(1)}, u32[]{:S(2)}, u32[]{:S(2)}) collective-permute-start(bf16[512,256]{1,0:T(8,128)(2,1)S(1)} %get-tuple-element.35.refs_1_), channel_id=1, source_target_pairs={{0,1},{1,0},{2,3},{3,2},{4,5},{5,4},{6,7},{7,6},{8,9},{9,8},{10,11... | collective-permute-start | bytes 786440 | tf_op jit(solution)/shard_map/ppermute | solution.py:263
  91.3 2.1 %collective-permute-done.8.refs_4_ = bf16[512,256]{1,0:T(8,128)(2,1)S(1)} collective-permute-done((bf16[512,256]{1,0:T(8,128)(2,1)S(1)}, bf16[512,256]{1,0:T(8,128)(2,1)S(1)}, u32[]{:S(2)}, u32[]{:S(2)}) %collective-permute-start.8) | collective-permute-done | bytes 262176 | tf_op jit(solution)/shard_map/ppermute | solution.py:267
  93.4 6.9 %collective-permute-start.9 = (bf16[512,256]{1,0:T(8,128)(2,1)S(1)}, bf16[512,256]{1,0:T(8,128)(2,1)S(1)}, u32[]{:S(2)}, u32[]{:S(2)}) collective-permute-start(bf16[512,256]{1,0:T(8,128)(2,1)S(1)} %collective-permute-done.8.refs_4_), channel_id=1, source_target_pairs={{0,1},{1,0},{2,3},{3,2},{4,5},{5,4},{6,7},{7,6},{8,9},{9,8},{10,11... | collective-permute-start | bytes 786440 | tf_op jit(solution)/shard_map/ppermute | solution.py:263
  100.9 2.7 %collective-permute-done.4.refs_2_ = bf16[512,256]{1,0:T(8,128)(2,1)S(1)} collective-permute-done((bf16[512,256]{1,0:T(8,128)(2,1)S(1)}, bf16[512,256]{1,0:T(8,128)(2,1)S(1)}, u32[]{:S(2)}, u32[]{:S(2)}) %collective-permute-start.4) | collective-permute-done | bytes 262176 | tf_op jit(solution)/shard_map/ppermute | solution.py:267
  104.2 5.7 %shard_map.162.refs_5_ = f32[256,1024]{1,0:T(8,128)S(1)} custom-call(s32[5]{0:T(128)S(1)} %pad_add_fusion.refs_0_, bf16[512,256]{1,0:T(8,128)(2,1)S(1)} %get-tuple-element.35.refs_1_, bf16[512,256]{1,0:T(8,128)(2,1)S(1)} %collective-permute-done.4.refs_2_, bf16[512,256]{1,0:T(8,128)(2,1)S(1)} %collective-permute-done.6.refs_3_, ...), custom_call_target="tpu_custom_call" | custom-call | flops 1342177280 | bytes 7340032 | tf_op jit(solution)/shard_map/pallas_call | solution.py:241
  109.9 4.8 %shard_map.163 = bf16[256,1024]{1,0:T(8,128)(2,1)} custom-call(s32[3]{0:T(128)S(1)} %slice_add_fusion.refs_0_, bf16[512,256]{1,0:T(8,128)(2,1)S(1)} %collective-permute-done.5.refs_1_, bf16[512,256]{1,0:T(8,128)(2,1)S(1)} %collective-permute-done.7.refs_2_, bf16[512,256]{1,0:T(8,128)(2,1)S(1)} %collective-permute-done.9.refs_3_, bf16[4096,1024]{1,0:T(8,128)(2,1)} %refs_4_.1, ...), custom_call_target="tpu_custom_call" | custom-call | flops 805306368 | bytes 5242880 | tf_op jit(solution)/shard_map/pallas_call | solution.py:241
  114.7 1.2 %shard_map.165 = (bf16[256,512]{1,0:T(8,128)(2,1)}, bf16[256,512]{1,0:T(8,128)(2,1)}, f32[256,512]{1,0:T(8,128)}) custom-call(bf16[32,32,256]{2,1,0:T(8,128)(2,1)S(1)} %all-to-all-done.2.got, f32[512,256]{1,0:T(8,128)S(1)} %copy-done.7, bf16[256,512]{1,0:T(8,128)(2,1)S(1)} %copy-done, bf16[256,512]{1,0:T(8,128)(2,1)S(1)} %copy-done.1), custom_call_target="tpu_custom_call" | custom-call | bytes 2621440 | tf_op jit(solution)/shard_map/pallas_call | solution.py:189
  (54 shorter events, 4.3 us)
Async XLA Ops:
  0.6 9.1 %copy-start.1 = (bf16[256,512]{1,0:T(8,128)(2,1)S(1)}, bf16[256,512]{1,0:T(8,128)(2,1)}, u32[]{:S(2)}) copy-start(bf16[256,512]{1,0:T(8,128)(2,1)} %values.5) | copy-start | bytes 786436
  0.6 9.0 %copy-start = (bf16[256,512]{1,0:T(8,128)(2,1)S(1)}, bf16[256,512]{1,0:T(8,128)(2,1)}, u32[]{:S(2)}) copy-start(bf16[256,512]{1,0:T(8,128)(2,1)} %inner.5) | copy-start | bytes 786436
  0.7 1.1 copy-start.2
  1.8 7.9 %copy-start.5 = (f32[256,512]{1,0:T(8,128)S(1)}, f32[256,512]{1,0:T(8,128)}, u32[]{:S(2)}) copy-start(f32[256,512]{1,0:T(8,128)} %taps.1) | copy-start | bytes 1572868
  1.8 18.4 %copy-start.3 = (bf16[256,1024]{1,0:T(8,128)(2,1)S(1)}, bf16[256,1024]{1,0:T(8,128)(2,1)}, u32[]{:S(2)}) copy-start(bf16[256,1024]{1,0:T(8,128)(2,1)} %grad.3) | copy-start | bytes 1572868
  6.3 25.7 %copy-start.17 = (bf16[256,512]{1,0:T(8,128)(2,1)S(1)}, bf16[256,512]{1,0:T(8,128)(2,1)}, u32[]{:S(2)}) copy-start(bf16[256,512]{1,0:T(8,128)(2,1)} %outer.1) | copy-start | bytes 786436
  6.3 25.7 %copy-start.20 = (f32[512]{0:T(512)S(1)}, f32[512]{0:T(512)}, u32[]{:S(2)}) copy-start(f32[512]{0:T(512)} %param.16) | copy-start | bytes 6148
  6.4 13.8 %collective-permute-start = (bf16[2048,256]{1,0:T(8,128)(2,1)S(1)}, bf16[2048,256]{1,0:T(8,128)(2,1)S(1)}, u32[]{:S(2)}, u32[]{:S(2)}) collective-permute-start(bf16[2048,256]{1,0:T(8,128)(2,1)S(1)} %shard_map.155), channel_id=1, source_target_pairs={{0,1},{1,0},{2,3},{3,2},{4,5},{5,4},{6,7},{7,6},{8,9},{9,8},{10,11... | collective-permute-start | bytes 3145736 | tf_op jit(solution)/shard_map/ppermute | solution.py:263
  10.7 24.3 %all-to-all-start = ((bf16[32,32,256]{2,1,0:T(8,128)(2,1)}), bf16[32,32,256]{2,1,0:T(8,128)(2,1)}, u32[]{:S(2)}, u32[]{:S(2)}) async-start(bf16[32,32,256]{2,1,0:T(8,128)(2,1)} %shard_map.158), calls=%async_computation | async-start | bytes 1048576 | tf_op jit(solution)/shard_map/all_to_all | solution.py:259
  20.2 14.8 %copy-start.4 = (bf16[1024,512]{1,0:T(8,128)(2,1)S(1)}, bf16[1024,512]{1,0:T(8,128)(2,1)}, u32[]{:S(2)}) copy-start(bf16[1024,512]{1,0:T(8,128)(2,1)} %constant.65.gather) | copy-start | bytes 3145732
  26.4 15.5 %collective-permute-start.1 = (bf16[512,256]{1,0:T(8,128)(2,1)}, bf16[512,256]{1,0:T(8,128)(2,1)S(1)}, u32[]{:S(2)}, u32[]{:S(2)}) collective-permute-start(bf16[512,256]{1,0:T(8,128)(2,1)} %get-tuple-element.26), channel_id=1, source_target_pairs={{0,4},{1,5},{2,6},{3,7},{4,0},{5,1},{6,2},{7,3},{8,12},{9,13},{10,... | collective-permute-start | bytes 786440 | tf_op jit(solution)/shard_map/ppermute | solution.py:267
  29.3 12.8 %collective-permute-start.2 = (bf16[512,256]{1,0:T(8,128)(2,1)}, bf16[512,256]{1,0:T(8,128)(2,1)}, u32[]{:S(2)}, u32[]{:S(2)}) collective-permute-start(bf16[512,256]{1,0:T(8,128)(2,1)} %get-tuple-element.27), channel_id=1, source_target_pairs={{0,2},{1,3},{2,4},{3,5},{4,6},{5,7},{6,0},{7,1},{8,10},{9,11},{10,... | collective-permute-start | bytes 786440 | tf_op jit(solution)/shard_map/ppermute | solution.py:267
  29.7 12.4 %collective-permute-start.3 = (bf16[512,256]{1,0:T(8,128)(2,1)}, bf16[512,256]{1,0:T(8,128)(2,1)}, u32[]{:S(2)}, u32[]{:S(2)}) collective-permute-start(bf16[512,256]{1,0:T(8,128)(2,1)} %get-tuple-element.28), channel_id=1, source_target_pairs={{0,6},{1,7},{2,0},{3,1},{4,2},{5,3},{6,4},{7,5},{8,14},{9,15},{10,... | collective-permute-start | bytes 786440 | tf_op jit(solution)/shard_map/ppermute | solution.py:267
  32.4 0.8 copy-start.8
  35.0 1.0 copy-start.12
  36.0 1.0 copy-start.14
  37.0 1.0 copy-start.16
  42.1 1.0 copy-start.19
  45.1 29.6 %copy-start.6 = (f32[512,256]{1,0:T(8,128)}, f32[512,256]{1,0:T(8,128)S(1)}, u32[]{:S(2)}) copy-start(f32[512,256]{1,0:T(8,128)S(1)} %get-tuple-element.41.skip_grad_t) | copy-start | bytes 1572868
  68.1 1.0 copy-start.13
  69.1 1.0 copy-start.15
  74.7 40.0 %all-to-all-start.2 = ((bf16[32,32,256]{2,1,0:T(8,128)(2,1)}), bf16[32,32,256]{2,1,0:T(8,128)(2,1)S(1)}, u32[]{:S(2)}, u32[]{:S(2)}) async-start(bf16[32,32,256]{2,1,0:T(8,128)(2,1)} %shard_map.164), calls=%async_computation.2 | async-start | bytes 1048576 | tf_op jit(solution)/shard_map/all_to_all | solution.py:259
  82.5 1.0 copy-start.9
  83.6 1.0 copy-start.11
  85.5 8.0 %collective-permute-start.8 = (bf16[512,256]{1,0:T(8,128)(2,1)S(1)}, bf16[512,256]{1,0:T(8,128)(2,1)S(1)}, u32[]{:S(2)}, u32[]{:S(2)}) collective-permute-start(bf16[512,256]{1,0:T(8,128)(2,1)S(1)} %get-tuple-element.35.refs_1_), channel_id=1, source_target_pairs={{0,6},{1,7},{2,0},{3,1},{4,2},{5,3},{6,4},{7,5},{8,14},{9,15},{10,... | collective-permute-start | bytes 786440 | tf_op jit(solution)/shard_map/ppermute | solution.py:267
  88.2 12.1 %collective-permute-start.6 = (bf16[512,256]{1,0:T(8,128)(2,1)S(1)}, bf16[512,256]{1,0:T(8,128)(2,1)S(1)}, u32[]{:S(2)}, u32[]{:S(2)}) collective-permute-start(bf16[512,256]{1,0:T(8,128)(2,1)S(1)} %get-tuple-element.35.refs_1_), channel_id=1, source_target_pairs={{0,4},{1,5},{2,6},{3,7},{4,0},{5,1},{6,2},{7,3},{8,12},{9,13},{10,... | collective-permute-start | bytes 786440 | tf_op jit(solution)/shard_map/ppermute | solution.py:267
  88.5 15.0 %collective-permute-start.4 = (bf16[512,256]{1,0:T(8,128)(2,1)S(1)}, bf16[512,256]{1,0:T(8,128)(2,1)S(1)}, u32[]{:S(2)}, u32[]{:S(2)}) collective-permute-start(bf16[512,256]{1,0:T(8,128)(2,1)S(1)} %get-tuple-element.35.refs_1_), channel_id=1, source_target_pairs={{0,2},{1,3},{2,4},{3,5},{4,6},{5,7},{6,0},{7,1},{8,10},{9,11},{10,... | collective-permute-start | bytes 786440 | tf_op jit(solution)/shard_map/ppermute | solution.py:267
  88.8 15.4 %collective-permute-start.10 = (bf16[512,256]{1,0:T(8,128)(2,1)S(1)}, bf16[512,256]{1,0:T(8,128)(2,1)S(1)}, u32[]{:S(2)}, u32[]{:S(2)}) collective-permute-start(bf16[512,256]{1,0:T(8,128)(2,1)S(1)} %get-tuple-element.35.refs_1_), channel_id=1, source_target_pairs={{0,1},{1,0},{2,3},{3,2},{4,5},{5,4},{6,7},{7,6},{8,9},{9,8},{10,11... | collective-permute-start | bytes 786440 | tf_op jit(solution)/shard_map/ppermute | solution.py:263
  93.4 16.5 %collective-permute-start.9 = (bf16[512,256]{1,0:T(8,128)(2,1)S(1)}, bf16[512,256]{1,0:T(8,128)(2,1)S(1)}, u32[]{:S(2)}, u32[]{:S(2)}) collective-permute-start(bf16[512,256]{1,0:T(8,128)(2,1)S(1)} %collective-permute-done.8.refs_4_), channel_id=1, source_target_pairs={{0,1},{1,0},{2,3},{3,2},{4,5},{5,4},{6,7},{7,6},{8,9},{9,8},{10,11... | collective-permute-start | bytes 786440 | tf_op jit(solution)/shard_map/ppermute | solution.py:263
  100.4 9.6 %collective-permute-start.7 = (bf16[512,256]{1,0:T(8,128)(2,1)S(1)}, bf16[512,256]{1,0:T(8,128)(2,1)S(1)}, u32[]{:S(2)}, u32[]{:S(2)}) collective-permute-start(bf16[512,256]{1,0:T(8,128)(2,1)S(1)} %collective-permute-done.6.refs_3_), channel_id=1, source_target_pairs={{0,1},{1,0},{2,3},{3,2},{4,5},{5,4},{6,7},{7,6},{8,9},{9,8},{10,11... | collective-permute-start | bytes 786440 | tf_op jit(solution)/shard_map/ppermute | solution.py:263
  103.6 6.4 %collective-permute-start.5 = (bf16[512,256]{1,0:T(8,128)(2,1)S(1)}, bf16[512,256]{1,0:T(8,128)(2,1)S(1)}, u32[]{:S(2)}, u32[]{:S(2)}) collective-permute-start(bf16[512,256]{1,0:T(8,128)(2,1)S(1)} %collective-permute-done.4.refs_2_), channel_id=1, source_target_pairs={{0,1},{1,0},{2,3},{3,2},{4,5},{5,4},{6,7},{7,6},{8,9},{9,8},{10,11... | collective-permute-start | bytes 786440 | tf_op jit(solution)/shard_map/ppermute | solution.py:263
  104.2 10.5 %copy-start.7 = (f32[512,256]{1,0:T(8,128)S(1)}, f32[512,256]{1,0:T(8,128)}, u32[]{:S(2)}) copy-start(f32[512,256]{1,0:T(8,128)} %copy-done.6) | copy-start | bytes 1572868
  (2 other events, 1.5 us)
where the time goes:
time: 117 us; the launch traced here: 116 us
  starting transfers between devices  39.8 us (34%)
  Pallas kernels  33.6 us (29%)
  blocking collectives  23 us (20%)
  local copies, waits for them, and re-layouts  11.7 us (10%)
  waiting for transfers between devices  6.72 us (6%)
    all_to_all x1, blocking collectives, exchange(): return lax.all_to_all(a, 'seq', split_axis=0, concat_axis=0, tiled=True)  23 us
    all_to_all x2, starting transfers between devices, exchange(): return lax.all_to_all(a, 'seq', split_axis=0, concat_axis=0, tiled=True)  17.2 us
    ppermute x5, starting transfers between devices, to_partner(): return lax.ppermute(a, 'ch', [(i, i ^ 1) for i in range(8)])  13.7 us
    pallas_call x7, Pallas kernels, local(): pl.pallas_call(kernel, out_shape=outs, in_specs=[pl.BlockSpec(memory_spac...  13.1 us
    unnamed x42, local copies, waits for them, and re-layouts  11.7 us
    pallas_call x2, Pallas kernels, blocks(): pl.pallas_call(kernel, out_shape=shape((ROWS, COLUMNS), jnp.bfloat16 if l...  10.5 us
    pallas_call x2, Pallas kernels, project(): pl.pallas_call(kernel, out_shape=outs, grid_spec=pltpu.PrefetchScalarGrid...  10.1 us
    ppermute x6, starting transfers between devices, along(): return lax.ppermute(a, 'ch', [(i, (i + 2 * shift) % 8) for i in range(8)])  8.9 us
  transfers between devices with their start and end apart: 13, of which 4 were waited for; matrix products, arithmetic and copies ran while one was open for 0% of the time, Pallas kernels for 19%

commit v1 on v0

v1 whole, which is shorter than its diff:
```python
import math

import jax
import jax.numpy as jnp
import numpy as np
from jax import lax
from jax.experimental import pallas as pl
from jax.experimental.pallas import tpu as pltpu
from jax.sharding import PartitionSpec as P

SEQ_PARTS = 32
ROWS = 256
WIDTH = 512
LANE_CH = WIDTH // SEQ_PARTS
COLUMNS = 1024
SLOTS = 32
PADDED = 2 * SEQ_PARTS * ROWS
AHEAD = 3
COSTS = (0.0, 10.0, 2.0, 10.0, 2.0, 1.0, 10.0)


def transform_tables():
    q = np.arange(SLOTS) + 0.5
    p = np.arange(SEQ_PARTS)
    r = np.arange(ROWS)
    coarse = 2.0 * math.pi * np.outer(q, p) / (2 * SEQ_PARTS)
    eye = np.eye(LANE_CH)
    gather = np.concatenate([np.kron(np.cos(coarse), eye), np.kron(-np.sin(coarse), eye)], 0)
    spread = gather.T * (2.0 / PADDED)
    fine = 2.0 * math.pi * (np.outer(r, r) % ROWS) / ROWS
    cos, sin = np.cos(fine), np.sin(fine)
    turn = np.block([[cos, -sin], [sin, cos]])
    twist = 2.0 * math.pi * np.outer(q, r) / PADDED
    twist = np.repeat(twist, LANE_CH, 0)

    def half(a):
        return jnp.asarray(a, jnp.float32).astype(jnp.bfloat16)

    return (
        half(gather),
        half(spread),
        half(turn),
        jnp.asarray(np.cos(twist), jnp.float32),
        jnp.asarray(np.sin(twist), jnp.float32),
    )


def dot(a, b, contract=((1,), (0,))):
    return lax.dot_general(a, b, (contract, ((), ())), preferred_element_type=jnp.float32)


def bf16(a):
    return a.astype(jnp.bfloat16)


def turned(real, imag, cos, sin):
    c, s = cos[...], sin[...]
    return bf16(real * c + imag * s), bf16(imag * c - real * s)


def forward(a, tables):
    count = SLOTS * LANE_CH
    b = turned(a[:count], a[count:], tables["cos"], tables["sin"])
    spec = dot(jnp.concatenate(b, 1), tables["turn"][...])
    return spec[:, :ROWS], spec[:, ROWS:]


def inverse(real, imag, tables):
    y = jnp.concatenate([bf16(real), bf16(imag)], 1)
    z = dot(y, tables["turn"][...], ((1,), (1,)))
    imag, real = turned(z[:, ROWS:], z[:, :ROWS], tables["cos"], tables["sin"])
    return dot(tables["spread"][...], jnp.concatenate([real, imag], 0))


TABLES = ("gather", "cos", "sin", "turn", "spread")


class Fetch:
    def __init__(self, far, near, sems):
        self.near = dict(zip(TABLES, near))
        self.copies = {
            n: pltpu.make_async_copy(f, t, sems.at[i]) for i, (n, f, t) in enumerate(zip(TABLES, far, near))
        }

    def start(self, *names):
        for name in names:
            self.copies[name].start()

    def wait(self, *names):
        for name in names:
            self.copies[name].wait()


def chunks(a):
    return bf16(a).reshape(SEQ_PARTS, LANE_CH, ROWS)


def flat(a):
    return a.reshape(WIDTH, ROWS)


def prepare_kernel(inner, values, taps, skip, out):
    product = inner[...].astype(jnp.float32) * values[...].astype(jnp.float32)
    out[:, :LANE_CH, :] = chunks(product.T)
    first = lax.broadcasted_iota(jnp.int32, (ROWS, WIDTH), 0) == 0
    out[:, LANE_CH:, :] = chunks((taps[...] + jnp.where(first, skip[...], 0.0)).T)


def project_kernel(where, weight, grad, *refs):
    out, blocks, sems = refs[-3:]

    def copy(i):
        return pltpu.make_async_copy(weight.at[2 * i + where[1]], blocks.at[i], sems.at[i])

    @pl.loop(0, AHEAD)
    def _(i):
        copy(i).start()

    if len(refs) == 4:
        far_grad, grad = grad, refs[0]
        load = pltpu.make_async_copy(far_grad, grad, sems.at[4])
        load.start()
        load.wait()

    @pl.loop(0, 4)
    def _(i):
        copy(i).wait()

        @pl.when(i + AHEAD < 4)
        def _():
            copy(i + AHEAD).start()

        out[(i - where[0]) & 3] = bf16(dot(blocks[i], grad[...], ((1,), (1,))))


def add_kernel(where, kept, other, *outs):
    ahead = 1 + 2 * where[1]
    for slot, out in zip((2, 4 - ahead, ahead, 0), outs):
        out[...] = bf16(kept[slot].astype(jnp.float32) + other[slot].astype(jnp.float32))


def add_two_kernel(a, b, out):
    out[...] = bf16(a[...].astype(jnp.float32) + b[...].astype(jnp.float32))


def turn_kernel(outer, after, out):
    out[...] = bf16(outer[...].astype(jnp.float32).T)


def first_kernel(go, got, *refs):
    (conv, sr, si, tr, ti), kept, (sems, first) = refs[5:10], refs[10:15], refs[15:]
    fetch = Fetch(refs[:5], kept, sems)

    @pl.when(go[0] >= 0)
    def _():
        fetch.start("gather")
        fetch.wait("gather")
        fetch.start("cos", "sin", "turn", "spread")

    @pl.when(go[0] >= 0)
    def _():
        first[0] = dot(fetch.near["gather"][...], flat(got[:, :LANE_CH, :]))
        first[1] = dot(fetch.near["gather"][...], flat(got[:, LANE_CH:, :]))
        fetch.wait("cos", "sin", "turn")

    @pl.when(go[0] >= 0)
    def _():
        sr[...], si[...] = forward(first[0], fetch.near)
        tr[...], ti[...] = forward(first[1], fetch.near)
        fetch.wait("spread")

    x_real, x_imag, t_real, t_imag = sr[...], si[...], tr[...], ti[...]
    y = inverse(x_real * t_real - x_imag * t_imag, x_real * t_imag + x_imag * t_real, fetch.near)
    conv[...] = chunks(y)


def middle_kernel(own, a, b, outer_t, conv, out, hidden_grad_t):
    total = own[...].astype(jnp.float32) + (a[...].astype(jnp.float32) + b[...].astype(jnp.float32))
    hidden_grad_t[...] = total
    out[:, :LANE_CH, :] = chunks(total * outer_t[...].astype(jnp.float32))
    out[:, LANE_CH:, :] = conv[...]


def second_kernel(got, sr, si, tr, ti, *refs):
    tables, out = dict(zip(TABLES, refs)), refs[5]
    g_real, g_imag = forward(dot(tables["gather"][...], flat(got[:, :LANE_CH, :])), tables)
    t_real, t_imag = tr[...], ti[...]
    corr = inverse(t_real * g_real + t_imag * g_imag, t_real * g_imag - t_imag * g_real, tables)
    out[:, :LANE_CH, :] = chunks(corr)
    x_real, x_imag = sr[...], si[...]
    lag = inverse(x_real * g_real + x_imag * g_imag, x_real * g_imag - x_imag * g_real, tables)
    out[:, LANE_CH:, :] = chunks(lag)


def gate_kernel(got, outer, hidden_grad_t, hidden, outer_grad):
    mixed_pre = flat(got[:, LANE_CH:, :]).astype(jnp.float32)
    hidden[...] = bf16(outer[...].astype(jnp.float32) * mixed_pre.T)
    outer_grad[...] = bf16((hidden_grad_t[...] * mixed_pre).T)


def final_kernel(got, inner, values, inner_grad, values_grad, taps_grad):
    total = flat(got[:, :LANE_CH, :]).astype(jnp.float32).T
    inner_grad[...] = bf16(total * values[...].astype(jnp.float32))
    values_grad[...] = bf16(total * inner[...].astype(jnp.float32))
    taps_grad[...] = flat(got[:, LANE_CH:, :]).astype(jnp.float32).T


def fetch_kernel(weight, hidden, sent, out, sems):
    @pl.loop(0, 8)
    def _(i):
        pltpu.make_async_copy(weight.at[i], out.at[i], sems.at[i]).start()

    @pl.loop(0, 8)
    def _(i):
        pltpu.make_async_copy(weight.at[i], out.at[i], sems.at[i]).wait()


def mixed_kernel(where, *refs):
    parts, weight = refs[:4], refs[4]
    base = refs[5] if len(refs) == 7 else None
    out = refs[-1]
    for c in range(0, COLUMNS, 256):
        columns = slice(c, c + 256)
        total = None if base is None else base[:, columns]
        for i, part in enumerate(parts):
            slot = 2 * ((where[0] - i) & 3) + where[1]
            term = dot(part[...], weight[slot, :, columns])
            total = term if total is None else total + term
        out[:, columns] = total.astype(out.dtype)


def shape(dims, dtype):
    return jax.ShapeDtypeStruct(dims, dtype)


def inside(dims, dtype):
    return pltpu.VMEM(dims, dtype)


def outside(dims, dtype):
    return pltpu.HBM(dims, dtype)


VMEM = pl.BlockSpec(memory_space=pltpu.VMEM)
HBM = pl.BlockSpec(memory_space=pltpu.HBM)
SMEM = pl.BlockSpec(memory_space=pltpu.SMEM)


def local(kernel, outs, *args, limit=16, specs=None, scratch=(), hold=(), cost=0.0):
    n = len(args)

    def body(*refs):
        kernel(*refs[:n], *refs[n + len(hold) :])

    return pl.pallas_call(
        body,
        out_shape=outs,
        in_specs=list(specs or [VMEM] * n) + [VMEM] * len(hold),
        out_specs=tuple(VMEM for _ in outs),
        scratch_shapes=scratch,
        compiler_params=pltpu.CompilerParams(vmem_limit_bytes=limit << 20),
        cost_estimate=pl.CostEstimate(flops=int(cost * 1.15e9), bytes_accessed=1 << 16, transcendentals=0),
    )(*args, *map(near_memory, hold))


def far_memory(a):
    return pltpu.with_memory_space_constraint(a, pltpu.HBM)


def near_memory(a):
    return pltpu.with_memory_space_constraint(a, pltpu.VMEM)


def project(where, weight, grad, cost, load):
    out = inside((4, WIDTH, ROWS), jnp.bfloat16)
    return local(
        project_kernel,
        (inside(grad.shape, grad.dtype), out) if load else (out,),
        where,
        weight,
        far_memory(grad) if load else near_memory(grad),
        specs=[SMEM, HBM, HBM if load else VMEM],
        scratch=[pltpu.VMEM((4, WIDTH, COLUMNS), jnp.bfloat16), pltpu.SemaphoreType.DMA((5,))],
        cost=cost,
    )


def mix(where, parts, weight, extra, out):
    return local(
        mixed_kernel,
        (out((ROWS, COLUMNS), jnp.float32 if out is inside else jnp.bfloat16),),
        where,
        *parts,
        weight,
        *extra,
        specs=[SMEM] + [VMEM] * (5 + len(extra)),
        cost=COSTS[3] if out is inside else COSTS[4],
    )[0]


def exchange(a):
    return lax.all_to_all(a, "seq", split_axis=0, concat_axis=0, tiled=True)


def to_partner(a):
    return lax.ppermute(a, "ch", [(i, i ^ 1) for i in range(8)])


def along(a, way):
    pairs = [(2 * y + c, 2 * ((y + way * (1 - 2 * c)) % 4) + c) for y in range(4) for c in range(2)]
    return lax.ppermute(a, "ch", pairs)


def shifted(a, rows):
    return lax.ppermute(a, "ch", [(i, (i + 2 * rows) % 8) for i in range(8)])


def on_device(outer_gate, inner_gate, values, filter_taps, skip_scale, out_weight, out_grad):
    tables = [far_memory(transform_tables()[i]) for i in (0, 3, 4, 2, 1)]
    me = lax.axis_index("ch").astype(jnp.int32)
    row, core = me // 2, me % 2
    near_half, far_half = jnp.stack([row, core]), jnp.stack([row, 1 - core])
    block = (WIDTH, ROWS)
    block_row = (ROWS, WIDTH)
    sending = (SEQ_PARTS, 2 * LANE_CH, ROWS)
    weight = far_memory(out_weight.reshape(8, WIDTH, COLUMNS))

    skip = jnp.where(lax.axis_index("seq") == 0, skip_scale, 0.0).reshape(1, WIDTH)
    sent = local(
        prepare_kernel,
        (inside(sending, jnp.bfloat16),),
        *map(far_memory, (inner_gate, values, filter_taps)),
        skip,
        limit=8,
    )[0]
    sent, far_half, near_half = lax.optimization_barrier((sent, far_half, near_half))
    got = near_memory(exchange(sent))
    grad, given = project(far_half, weight, out_grad, COSTS[0], True)
    given, near_half = lax.optimization_barrier((given, near_half))
    kept = project(near_half, weight, grad, COSTS[1], False)[0]
    across, back, ahead, own = local(
        add_kernel,
        (inside(block, jnp.bfloat16),) * 3 + (outside(block, jnp.bfloat16),),
        near_half,
        kept,
        to_partner(given),
        specs=[SMEM, VMEM, VMEM],
    )
    passed = along(across, 1)
    back = along(back, -1)

    spectrum = inside((SLOTS * LANE_CH, ROWS), jnp.float32)
    conv, *kept = local(
        first_kernel,
        (
            inside((SEQ_PARTS, LANE_CH, ROWS), jnp.bfloat16),
            *(spectrum,) * 4,
            *(inside(t.shape, t.dtype) for t in tables),
        ),
        near_half,
        got,
        *tables,
        specs=[SMEM, VMEM] + [HBM] * len(tables),
        scratch=[
            pltpu.SemaphoreType.DMA((len(tables),)),
            pltpu.VMEM((2, 2 * SLOTS * LANE_CH, ROWS), jnp.float32),
        ],
        cost=COSTS[6],
    )
    ahead, conv = lax.optimization_barrier((ahead, conv))
    ahead = local(add_two_kernel, (inside(block, jnp.bfloat16),), ahead, passed)[0]
    outer_t = local(
        turn_kernel,
        (inside(block, jnp.bfloat16),),
        far_memory(outer_gate),
        ahead,
        cost=COSTS[5],
    )[0]
    sums = [far_memory(own), back, along(ahead, 1)]
    sent, hidden_grad_t = local(
        middle_kernel,
        (inside(sending, jnp.bfloat16), inside(block, jnp.float32)),
        *sums,
        outer_t,
        conv,
        hold=kept,
    )
    got = near_memory(exchange(sent))
    hidden, outer_grad = local(
        gate_kernel,
        (inside(block_row, jnp.bfloat16), outside(block_row, jnp.bfloat16)),
        got,
        far_memory(outer_gate),
        near_memory(hidden_grad_t),
        hold=kept,
    )
    sent = local(
        second_kernel,
        (outside(sending, jnp.bfloat16),),
        got,
        *map(near_memory, kept),
        hold=(hidden,),
    )[0]
    returned = near_memory(exchange(sent))
    near = [hidden, shifted(hidden, 1), shifted(hidden, 2), shifted(hidden, 3)]
    kept_weight = local(
        fetch_kernel,
        (inside(weight.shape, weight.dtype),),
        weight,
        hidden,
        far_memory(sent),
        specs=[HBM, VMEM, HBM],
        scratch=[pltpu.SemaphoreType.DMA((8,))],
        cost=COSTS[2],
    )[0]
    *waited, kept_weight = lax.optimization_barrier((*near, kept_weight))
    far = [to_partner(a) for a in waited]
    part = mix(near_half, near, kept_weight, (), inside)
    mixed = mix(far_half, far, kept_weight, (part,), outside)
    inner_grad, values_grad, taps_grad = local(
        final_kernel,
        (
            outside(block_row, jnp.bfloat16),
            outside(block_row, jnp.bfloat16),
            outside(block_row, jnp.float32),
        ),
        returned,
        inner_gate,
        values,
    )
    return (mixed, outer_grad, inner_grad, values_grad, taps_grad)


def solution(mesh):
    placed = (
        P("seq", "ch"),
        P("seq", "ch"),
        P("seq", "ch"),
        P("seq", "ch"),
        P("ch"),
        P(None, "ch"),
        P("seq", "ch"),
    )
    return jax.shard_map(
        on_device,
        mesh=mesh,
        in_specs=placed,
        out_specs=(P("seq", "ch"), P("seq", "ch"), P("seq", "ch"), P("seq", "ch"), P("seq", "ch")),
        check_vma=False,
    )
```

time: 117 us -> 103 us (0.88)
  the two profiles are of different devices: /device:TPU:1 before, /device:TPU:32 now
where the time goes in v1:
time: 103 us; the launch traced here: 102 us
  Pallas kernels  33.5 us (33%)
  starting transfers between devices  27.6 us (27%)
  blocking collectives  20.7 us (20%)
  waiting for transfers between devices  19.6 us (19%)
    pallas_call x14, Pallas kernels, local(): pl.pallas_call(body, out_shape=outs, in_specs=list(specs or [VMEM] * n) +...  33.5 us
    all_to_all x1, blocking collectives, exchange(): return lax.all_to_all(a, 'seq', split_axis=0, concat_axis=0, tiled=True)  20.7 us
    all_to_all x2, starting transfers between devices, exchange(): return lax.all_to_all(a, 'seq', split_axis=0, concat_axis=0, tiled=True)  16 us
    all_to_all x2, waiting for transfers between devices, exchange(): return lax.all_to_all(a, 'seq', split_axis=0, concat_axis=0, tiled=True)  13.1 us
    ppermute x3, waiting for transfers between devices, along(): return lax.ppermute(a, 'ch', pairs)  6.48 us
    ppermute x3, starting transfers between devices, shifted(): return lax.ppermute(a, 'ch', [(i, (i + 2 * rows) % 8) for i in range(8)])  5.42 us
    ppermute x3, starting transfers between devices, along(): return lax.ppermute(a, 'ch', pairs)  4.76 us
  transfers between devices with their start and end apart: 13, of which 4 were waited for; matrix products, arithmetic and copies ran while one was open for 0% of the time, Pallas kernels for 27%

profile of v1, /device:TPU:32, one launch (start us, length us, event | category | flops | bytes accessed | tf_op | source)
XLA Modules:
  0.0 102.3 jit_solution(11837783701296876009)
XLA Ops:
  0.7 0.1 pad_add_fusion
  0.8 2.2 %shard_map.155 = bf16[32,32,256]{2,1,0:T(8,128)(2,1)} custom-call(bf16[256,512]{1,0:T(8,128)(2,1)} %refs_1_.5, bf16[256,512]{1,0:T(8,128)(2,1)} %refs_2_.5, f32[256,512]{1,0:T(8,128)} %refs_2_.3, f32[1,512]{1,0:T(1,128)S(1)} %bitcast.5), custom_call_target="tpu_custom_call" | custom-call | bytes 65536 | tf_op jit(solution)/shard_map/pallas_call | solution.py:255
  3.0 11.2 %all-to-all-start = ((bf16[32,32,256]{2,1,0:T(8,128)(2,1)}), bf16[32,32,256]{2,1,0:T(8,128)(2,1)S(1)}, u32[]{:S(2)}, u32[]{:S(2)}) async-start(bf16[32,32,256]{2,1,0:T(8,128)(2,1)} %shard_map.155), calls=%async_computation | async-start | bytes 1048576 | tf_op jit(solution)/shard_map/all_to_all | solution.py:302
  14.2 4.5 %shard_map.156 = (bf16[256,1024]{1,0:T(8,128)(2,1)S(1)}, bf16[4,512,256]{2,1,0:T(8,128)(2,1)S(1)}) custom-call(s32[2]{0:T(128)S(1)} %get-tuple-element.40.refs_0_, bf16[8,512,1024]{2,1,0:T(8,128)(2,1)} %bitcast.6, bf16[256,1024]{1,0:T(8,128)(2,1)} %refs_2_.4), custom_call_target="tpu_custom_call" | custom-call | bytes 65536 | tf_op jit(solution)/shard_map/pallas_call | solution.py:255
  18.6 0.1 collective-permute-start
  18.7 3.7 %shard_map.157.refs_1_ = bf16[4,512,256]{2,1,0:T(8,128)(2,1)S(1)} custom-call(s32[2]{0:T(128)S(1)} %get-tuple-element.43.refs_0_, bf16[8,512,1024]{2,1,0:T(8,128)(2,1)} %bitcast.7, bf16[256,1024]{1,0:T(8,128)(2,1)S(1)} %get-tuple-element.44.refs_2_), custom_call_target="tpu_custom_call" | custom-call | flops 11500000256 | bytes 65536 | tf_op jit(solution)/shard_map/pallas_call | solution.py:255
  22.5 1.4 %shard_map.158 = (bf16[512,256]{1,0:T(8,128)(2,1)S(1)}, bf16[512,256]{1,0:T(8,128)(2,1)S(1)}, bf16[512,256]{1,0:T(8,128)(2,1)S(1)}, bf16[512,256]{1,0:T(8,128)(2,1)}) custom-call(s32[2]{0:T(128)S(1)} %get-tuple-element.43.refs_0_, bf16[4,512,256]{2,1,0:T(8,128)(2,1)S(1)} %shard_map.157.refs_1_, bf16[4,512,256]{2,1,0:T(8,128)(2,1)S(1)} %collective-permute-done.refs_2_), custom_call_target="tpu_custom_call" | custom-call | bytes 65536 | tf_op jit(solution)/shard_map/pallas_call | solution.py:255
  23.9 1.6 %collective-permute-start.2 = (bf16[512,256]{1,0:T(8,128)(2,1)S(1)}, bf16[512,256]{1,0:T(8,128)(2,1)S(1)}, u32[]{:S(2)}, u32[]{:S(2)}) collective-permute-start(bf16[512,256]{1,0:T(8,128)(2,1)S(1)} %get-tuple-element.52), channel_id=1, source_target_pairs={{0,2},{1,7},{2,4},{3,1},{4,6},{5,3},{6,0},{7,5},{8,10},{9,15},{10,... | collective-permute-start | bytes 786440 | tf_op jit(solution)/shard_map/ppermute | solution.py:311
  25.5 6.3 %all-to-all-done.refs_1_ = bf16[32,32,256]{2,1,0:T(8,128)(2,1)S(1)} async-done(((bf16[32,32,256]{2,1,0:T(8,128)(2,1)}), bf16[32,32,256]{2,1,0:T(8,128)(2,1)S(1)}, u32[]{:S(2)}, u32[]{:S(2)}) %all-to-all-start) | async-done | bytes 524320 | tf_op jit(solution)/shard_map/all_to_all | solution.py:302
  31.8 5.2 %shard_map.159 = (bf16[32,16,256]{2,1,0:T(8,128)(2,1)S(1)}, f32[512,256]{1,0:T(8,128)S(1)}, f32[512,256]{1,0:T(8,128)S(1)}, f32[512,256]{1,0:T(8,128)S(1)}, f32[...) custom-call(s32[2]{0:T(128)S(1)} %get-tuple-element.43.refs_0_, ...), custom_call_target="tpu_custom_call" | custom-call | flops 11500000256 | bytes 65536 | tf_op jit(solution)/shard_map/pallas_call | solution.py:255
  37.0 3.1 %collective-permute-start.1 = (bf16[512,256]{1,0:T(8,128)(2,1)S(1)}, bf16[512,256]{1,0:T(8,128)(2,1)S(1)}, u32[]{:S(2)}, u32[]{:S(2)}) collective-permute-start(bf16[512,256]{1,0:T(8,128)(2,1)S(1)} %get-tuple-element.47), channel_id=1, source_target_pairs={{0,6},{1,3},{2,0},{3,5},{4,2},{5,7},{6,4},{7,1},{8,14},{9,11},{10,... | collective-permute-start | bytes 786440 | tf_op jit(solution)/shard_map/ppermute | solution.py:311
  40.1 0.1 collective-permute-start.3
  40.2 1.1 %shard_map.161.refs_3_ = bf16[512,256]{1,0:T(8,128)(2,1)S(1)} custom-call(bf16[256,512]{1,0:T(8,128)(2,1)} %refs_1_.4, bf16[512,256]{1,0:T(8,128)(2,1)S(1)} %shard_map.160.refs_1_), custom_call_target="tpu_custom_call" | custom-call | flops 1150000000 | bytes 65536 | tf_op jit(solution)/shard_map/pallas_call | solution.py:255
  41.3 3.1 %collective-permute-done.1.refs_1_ = bf16[512,256]{1,0:T(8,128)(2,1)S(1)} collective-permute-done((bf16[512,256]{1,0:T(8,128)(2,1)S(1)}, bf16[512,256]{1,0:T(8,128)(2,1)S(1)}, u32[]{:S(2)}, u32[]{:S(2)}) %collective-permute-start.1) | collective-permute-done | bytes 262176 | tf_op jit(solution)/shard_map/ppermute | solution.py:311
  44.4 3.4 %collective-permute-done.3.refs_2_ = bf16[512,256]{1,0:T(8,128)(2,1)S(1)} collective-permute-done((bf16[512,256]{1,0:T(8,128)(2,1)S(1)}, bf16[512,256]{1,0:T(8,128)(2,1)S(1)}, u32[]{:S(2)}, u32[]{:S(2)}) %collective-permute-start.3) | collective-permute-done | bytes 262176 | tf_op jit(solution)/shard_map/ppermute | solution.py:311
  47.8 1.1 %shard_map.162 = (bf16[32,32,256]{2,1,0:T(8,128)(2,1)S(1)}, f32[512,256]{1,0:T(8,128)S(1)}) custom-call(bf16[512,256]{1,0:T(8,128)(2,1)} %get-tuple-element.46.refs_0_, bf16[512,256]{1,0:T(8,128)(2,1)S(1)} %collective-permute-done.1.refs_1_, bf16[512,256]{1,0:T(8,128)(2,1)S(1)} %collective-permute-done.3.refs_2_, bf16[512,256]{1,0:T(8,128)(2,1)S(1)} %shard_map.161.refs_3_, ...), custom_call_target="tpu_custom_call" | custom-call | bytes 65536 | tf_op jit(solution)/shard_map/pallas_call | solution.py:255
  48.9 20.7 %all_to_all.15.refs_0_ = bf16[32,32,256]{2,1,0:T(8,128)(2,1)S(1)} all-to-all(bf16[32,32,256]{2,1,0:T(8,128)(2,1)S(1)} %get-tuple-element.63), channel_id=1, replica_groups=mesh['seq'=32,'ch'=8] {'seq'}, dimensions={0} | all-to-all | bytes 1048576 | tf_op jit(solution)/shard_map/all_to_all | solution.py:302
  69.6 1.9 %shard_map.163 = (bf16[256,512]{1,0:T(8,128)(2,1)S(1)}, bf16[256,512]{1,0:T(8,128)(2,1)}) custom-call(bf16[32,32,256]{2,1,0:T(8,128)(2,1)S(1)} %all_to_all.15.refs_0_, bf16[256,512]{1,0:T(8,128)(2,1)} %refs_1_.4, f32[512,256]{1,0:T(8,128)S(1)} %get-tuple-element.64.refs_2_, f32[512,256]{1,0:T(8,128)S(1)} %get-tuple-element.54.refs_5_.refs_3_.refs_1_, ...), custom_call_target="tpu_custom_call" | custom-call | bytes 65536 | tf_op jit(solution)/shard_map/pallas_call | solution.py:255
  71.4 1.4 %collective-permute-start.4 = (bf16[256,512]{1,0:T(8,128)(2,1)S(1)}, bf16[256,512]{1,0:T(8,128)(2,1)S(1)}, u32[]{:S(2)}, u32[]{:S(2)}) collective-permute-start(bf16[256,512]{1,0:T(8,128)(2,1)S(1)} %get-tuple-element.66.refs_10_.refs_1_), channel_id=1, source_target_pairs={{0,2},{1,3},{2,4},{3,5},{4,6},{5,7},{6,0},{7,1},{8,10},{9,11},{10,... | collective-permute-start | bytes 786440 | tf_op jit(solution)/shard_map/ppermute | solution.py:315
  72.9 3.7 %collective-permute-start.5 = (bf16[256,512]{1,0:T(8,128)(2,1)S(1)}, bf16[256,512]{1,0:T(8,128)(2,1)S(1)}, u32[]{:S(2)}, u32[]{:S(2)}) collective-permute-start(bf16[256,512]{1,0:T(8,128)(2,1)S(1)} %get-tuple-element.66.refs_10_.refs_1_), channel_id=1, source_target_pairs={{0,4},{1,5},{2,6},{3,7},{4,0},{5,1},{6,2},{7,3},{8,12},{9,13},{10,... | collective-permute-start | bytes 786440 | tf_op jit(solution)/shard_map/ppermute | solution.py:315
  76.6 0.3 collective-permute-start.6
  76.9 3.3 %shard_map.164.refs_2_ = bf16[32,32,256]{2,1,0:T(8,128)(2,1)} custom-call(bf16[32,32,256]{2,1,0:T(8,128)(2,1)S(1)} %all_to_all.15.refs_0_, f32[512,256]{1,0:T(8,128)S(1)} %get-tuple-element.54.refs_5_.refs_3_.refs_1_, f32[512,256]{1,0:T(8,128)S(1)} %get-tuple-element.55.refs_6_.refs_4_.refs_2_, f32[512,256]{1,0:T(8,128)S(1)} %get-tuple-element.56.refs_7_.refs_5_.refs_3_, ...), custom_call_target="tpu_custom_call" | custom-call | bytes 65536 | tf_op jit(solution)/shard_map/pallas_call | solution.py:255
  80.2 4.8 %all-to-all-start.2 = ((bf16[32,32,256]{2,1,0:T(8,128)(2,1)}), bf16[32,32,256]{2,1,0:T(8,128)(2,1)S(1)}, u32[]{:S(2)}, u32[]{:S(2)}) async-start(bf16[32,32,256]{2,1,0:T(8,128)(2,1)} %shard_map.164.refs_2_), calls=%async_computation.2 | async-start | bytes 1048576 | tf_op jit(solution)/shard_map/all_to_all | solution.py:302
  85.1 3.5 %shard_map.165.refs_5_ = bf16[8,512,1024]{2,1,0:T(8,128)(2,1)S(1)} custom-call(bf16[8,512,1024]{2,1,0:T(8,128)(2,1)} %bitcast.8, bf16[256,512]{1,0:T(8,128)(2,1)S(1)} %get-tuple-element.66.refs_10_.refs_1_, bf16[32,32,256]{2,1,0:T(8,128)(2,1)} %shard_map.164.refs_2_), custom_call_target="tpu_custom_call" | custom-call | flops 2300000000 | bytes 65536 | tf_op jit(solution)/shard_map/pallas_call | solution.py:255
  88.6 0.3 collective-permute-start.10
  88.9 0.5 collective-permute-start.7
  89.4 0.1 collective-permute-start.8
  89.5 0.4 collective-permute-start.9
  89.9 1.8 %shard_map.166.refs_6_ = f32[256,1024]{1,0:T(8,128)S(1)} custom-call(s32[2]{0:T(128)S(1)} %get-tuple-element.43.refs_0_, bf16[256,512]{1,0:T(8,128)(2,1)S(1)} %get-tuple-element.66.refs_10_.refs_1_, bf16[256,512]{1,0:T(8,128)(2,1)S(1)} %collective-permute-done.4.refs_2_, bf16[256,512]{1,0:T(8,128)(2,1)S(1)} %collective-permute-done.5.refs_3_, ...), custom_call_target="tpu_custom_call" | custom-call | flops 11500000256 | bytes 65536 | tf_op jit(solution)/shard_map/pallas_call | solution.py:255
  91.7 2.6 %shard_map.167 = bf16[256,1024]{1,0:T(8,128)(2,1)} custom-call(s32[2]{0:T(128)S(1)} %get-tuple-element.40.refs_0_, bf16[256,512]{1,0:T(8,128)(2,1)S(1)} %collective-permute-done.7.refs_1_, bf16[256,512]{1,0:T(8,128)(2,1)S(1)} %collective-permute-done.8.refs_2_, bf16[256,512]{1,0:T(8,128)(2,1)S(1)} %collective-permute-done.9.refs_3_, ...), custom_call_target="tpu_custom_call" | custom-call | flops 2300000000 | bytes 65536 | tf_op jit(solution)/shard_map/pallas_call | solution.py:255
  94.3 6.9 %all-to-all-done.2.refs_0_ = bf16[32,32,256]{2,1,0:T(8,128)(2,1)S(1)} async-done(((bf16[32,32,256]{2,1,0:T(8,128)(2,1)}), bf16[32,32,256]{2,1,0:T(8,128)(2,1)S(1)}, u32[]{:S(2)}, u32[]{:S(2)}) %all-to-all-start.2) | async-done | bytes 524320 | tf_op jit(solution)/shard_map/all_to_all | solution.py:302
  101.2 1.1 %shard_map.168 = (bf16[256,512]{1,0:T(8,128)(2,1)}, bf16[256,512]{1,0:T(8,128)(2,1)}, f32[256,512]{1,0:T(8,128)}) custom-call(bf16[32,32,256]{2,1,0:T(8,128)(2,1)S(1)} %all-to-all-done.2.refs_0_, bf16[256,512]{1,0:T(8,128)(2,1)S(1)} %copy-done, bf16[256,512]{1,0:T(8,128)(2,1)S(1)} %copy-done.1), custom_call_target="tpu_custom_call" | custom-call | bytes 65536 | tf_op jit(solution)/shard_map/pallas_call | solution.py:255
  (15 shorter events, 0.1 us)
Async XLA Ops:
  3.0 28.8 %all-to-all-start = ((bf16[32,32,256]{2,1,0:T(8,128)(2,1)}), bf16[32,32,256]{2,1,0:T(8,128)(2,1)S(1)}, u32[]{:S(2)}, u32[]{:S(2)}) async-start(bf16[32,32,256]{2,1,0:T(8,128)(2,1)} %shard_map.155), calls=%async_computation | async-start | bytes 1048576 | tf_op jit(solution)/shard_map/all_to_all | solution.py:302
  18.6 3.8 %collective-permute-start = (bf16[4,512,256]{2,1,0:T(8,128)(2,1)S(1)}, bf16[4,512,256]{2,1,0:T(8,128)(2,1)S(1)}, u32[]{:S(2)}, u32[]{:S(2)}) collective-permute-start(bf16[4,512,256]{2,1,0:T(8,128)(2,1)S(1)} %get-tuple-element.45), channel_id=1, source_target_pairs={{0,1},{1,0},{2,3},{3,2},{4,5},{5,4},{6,7},{7,6},{8,9},{9,8},{10,11... | collective-permute-start | bytes 3145736 | tf_op jit(solution)/shard_map/ppermute | solution.py:306
  23.9 16.2 %collective-permute-start.2 = (bf16[512,256]{1,0:T(8,128)(2,1)S(1)}, bf16[512,256]{1,0:T(8,128)(2,1)S(1)}, u32[]{:S(2)}, u32[]{:S(2)}) collective-permute-start(bf16[512,256]{1,0:T(8,128)(2,1)S(1)} %get-tuple-element.52), channel_id=1, source_target_pairs={{0,2},{1,7},{2,4},{3,1},{4,6},{5,3},{6,0},{7,5},{8,10},{9,15},{10,... | collective-permute-start | bytes 786440 | tf_op jit(solution)/shard_map/ppermute | solution.py:311
  37.0 7.4 %collective-permute-start.1 = (bf16[512,256]{1,0:T(8,128)(2,1)S(1)}, bf16[512,256]{1,0:T(8,128)(2,1)S(1)}, u32[]{:S(2)}, u32[]{:S(2)}) collective-permute-start(bf16[512,256]{1,0:T(8,128)(2,1)S(1)} %get-tuple-element.47), channel_id=1, source_target_pairs={{0,6},{1,3},{2,0},{3,5},{4,2},{5,7},{6,4},{7,1},{8,14},{9,11},{10,... | collective-permute-start | bytes 786440 | tf_op jit(solution)/shard_map/ppermute | solution.py:311
  40.1 7.7 %collective-permute-start.3 = (bf16[512,256]{1,0:T(8,128)(2,1)S(1)}, bf16[512,256]{1,0:T(8,128)(2,1)S(1)}, u32[]{:S(2)}, u32[]{:S(2)}) collective-permute-start(bf16[512,256]{1,0:T(8,128)(2,1)S(1)} %shard_map.160.refs_1_), channel_id=1, source_target_pairs={{0,2},{1,7},{2,4},{3,1},{4,6},{5,3},{6,0},{7,5},{8,10},{9,15},{10,... | collective-permute-start | bytes 786440 | tf_op jit(solution)/shard_map/ppermute | solution.py:311
  71.4 17.1 %collective-permute-start.4 = (bf16[256,512]{1,0:T(8,128)(2,1)S(1)}, bf16[256,512]{1,0:T(8,128)(2,1)S(1)}, u32[]{:S(2)}, u32[]{:S(2)}) collective-permute-start(bf16[256,512]{1,0:T(8,128)(2,1)S(1)} %get-tuple-element.66.refs_10_.refs_1_), channel_id=1, source_target_pairs={{0,2},{1,3},{2,4},{3,5},{4,6},{5,7},{6,0},{7,1},{8,10},{9,11},{10,... | collective-permute-start | bytes 786440 | tf_op jit(solution)/shard_map/ppermute | solution.py:315
  72.9 15.7 %collective-permute-start.5 = (bf16[256,512]{1,0:T(8,128)(2,1)S(1)}, bf16[256,512]{1,0:T(8,128)(2,1)S(1)}, u32[]{:S(2)}, u32[]{:S(2)}) collective-permute-start(bf16[256,512]{1,0:T(8,128)(2,1)S(1)} %get-tuple-element.66.refs_10_.refs_1_), channel_id=1, source_target_pairs={{0,4},{1,5},{2,6},{3,7},{4,0},{5,1},{6,2},{7,3},{8,12},{9,13},{10,... | collective-permute-start | bytes 786440 | tf_op jit(solution)/shard_map/ppermute | solution.py:315
  76.6 12.0 %collective-permute-start.6 = (bf16[256,512]{1,0:T(8,128)(2,1)S(1)}, bf16[256,512]{1,0:T(8,128)(2,1)S(1)}, u32[]{:S(2)}, u32[]{:S(2)}) collective-permute-start(bf16[256,512]{1,0:T(8,128)(2,1)S(1)} %get-tuple-element.66.refs_10_.refs_1_), channel_id=1, source_target_pairs={{0,6},{1,7},{2,0},{3,1},{4,2},{5,3},{6,4},{7,5},{8,14},{9,15},{10,... | collective-permute-start | bytes 786440 | tf_op jit(solution)/shard_map/ppermute | solution.py:315
  80.2 21.0 %all-to-all-start.2 = ((bf16[32,32,256]{2,1,0:T(8,128)(2,1)}), bf16[32,32,256]{2,1,0:T(8,128)(2,1)S(1)}, u32[]{:S(2)}, u32[]{:S(2)}) async-start(bf16[32,32,256]{2,1,0:T(8,128)(2,1)} %shard_map.164.refs_2_), calls=%async_computation.2 | async-start | bytes 1048576 | tf_op jit(solution)/shard_map/all_to_all | solution.py:302
  88.6 3.1 %collective-permute-start.10 = (bf16[256,512]{1,0:T(8,128)(2,1)S(1)}, bf16[256,512]{1,0:T(8,128)(2,1)S(1)}, u32[]{:S(2)}, u32[]{:S(2)}) collective-permute-start(bf16[256,512]{1,0:T(8,128)(2,1)S(1)} %collective-permute-done.6.refs_4_), channel_id=1, source_target_pairs={{0,1},{1,0},{2,3},{3,2},{4,5},{5,4},{6,7},{7,6},{8,9},{9,8},{10,11... | collective-permute-start | bytes 786440 | tf_op jit(solution)/shard_map/ppermute | solution.py:306
  88.9 2.8 %collective-permute-start.7 = (bf16[256,512]{1,0:T(8,128)(2,1)S(1)}, bf16[256,512]{1,0:T(8,128)(2,1)S(1)}, u32[]{:S(2)}, u32[]{:S(2)}) collective-permute-start(bf16[256,512]{1,0:T(8,128)(2,1)S(1)} %get-tuple-element.66.refs_10_.refs_1_), channel_id=1, source_target_pairs={{0,1},{1,0},{2,3},{3,2},{4,5},{5,4},{6,7},{7,6},{8,9},{9,8},{10,11... | collective-permute-start | bytes 786440 | tf_op jit(solution)/shard_map/ppermute | solution.py:306
  89.4 2.4 %collective-permute-start.8 = (bf16[256,512]{1,0:T(8,128)(2,1)S(1)}, bf16[256,512]{1,0:T(8,128)(2,1)S(1)}, u32[]{:S(2)}, u32[]{:S(2)}) collective-permute-start(bf16[256,512]{1,0:T(8,128)(2,1)S(1)} %collective-permute-done.4.refs_2_), channel_id=1, source_target_pairs={{0,1},{1,0},{2,3},{3,2},{4,5},{5,4},{6,7},{7,6},{8,9},{9,8},{10,11... | collective-permute-start | bytes 786440 | tf_op jit(solution)/shard_map/ppermute | solution.py:306
  89.5 2.3 %collective-permute-start.9 = (bf16[256,512]{1,0:T(8,128)(2,1)S(1)}, bf16[256,512]{1,0:T(8,128)(2,1)S(1)}, u32[]{:S(2)}, u32[]{:S(2)}) collective-permute-start(bf16[256,512]{1,0:T(8,128)(2,1)S(1)} %collective-permute-done.5.refs_3_), channel_id=1, source_target_pairs={{0,1},{1,0},{2,3},{3,2},{4,5},{5,4},{6,7},{7,6},{8,9},{9,8},{10,11... | collective-permute-start | bytes 786440 | tf_op jit(solution)/shard_map/ppermute | solution.py:306
  91.7 9.5 %copy-start = (bf16[256,512]{1,0:T(8,128)(2,1)S(1)}, bf16[256,512]{1,0:T(8,128)(2,1)}, u32[]{:S(2)}) copy-start(bf16[256,512]{1,0:T(8,128)(2,1)} %refs_1_.5) | copy-start | bytes 786436
  91.7 9.5 %copy-start.1 = (bf16[256,512]{1,0:T(8,128)(2,1)S(1)}, bf16[256,512]{1,0:T(8,128)(2,1)}, u32[]{:S(2)}) copy-start(bf16[256,512]{1,0:T(8,128)(2,1)} %refs_2_.5) | copy-start | bytes 786436

commit v2 on v1

v2 whole, which is shorter than its diff:
```python
import math

import jax
import jax.numpy as jnp
import numpy as np
from jax import lax
from jax.experimental import pallas as pl
from jax.experimental.pallas import tpu as pltpu
from jax.sharding import PartitionSpec as P

SEQ_PARTS = 32
ROWS = 256
WIDTH = 512
LANE_CH = WIDTH // SEQ_PARTS
COLUMNS = 1024
SLOTS = 32
PADDED = 2 * SEQ_PARTS * ROWS
AHEAD = 3
GROUP = 8
LINES = SLOTS * GROUP
LATE = False
COSTS = (0.0, 10.0, 2.0, 5.0, 0.0, 0.0, 0.0, 0.0, 20.0)


def transform_tables():
    q = np.arange(SLOTS) + 0.5
    p = np.arange(SEQ_PARTS)
    r = np.arange(ROWS)
    coarse = 2.0 * math.pi * np.outer(q, p) / (2 * SEQ_PARTS)
    eye = np.eye(GROUP)
    gather = np.concatenate([np.kron(np.cos(coarse), eye), np.kron(-np.sin(coarse), eye)], 0)
    spread = gather.T * (2.0 / PADDED)
    fine = 2.0 * math.pi * (np.outer(r, r) % ROWS) / ROWS
    cos, sin = np.cos(fine), np.sin(fine)
    turn = np.block([[cos, -sin], [sin, cos]])
    twist = 2.0 * math.pi * np.outer(q, r) / PADDED
    twist = np.repeat(twist, GROUP, 0)

    def half(a):
        return jnp.asarray(a, jnp.float32).astype(jnp.bfloat16)

    return (
        half(gather),
        half(spread),
        half(turn),
        jnp.asarray(np.cos(twist), jnp.float32),
        jnp.asarray(np.sin(twist), jnp.float32),
    )


def dot(a, b, contract=((1,), (0,))):
    return lax.dot_general(a, b, (contract, ((), ())), preferred_element_type=jnp.float32)


def bf16(a):
    return a.astype(jnp.bfloat16)


def turned(real, imag, cos, sin):
    c, s = cos[...], sin[...]
    return bf16(real * c + imag * s), bf16(imag * c - real * s)


def forward(x, tables):
    c, s = tables["cos"], tables["sin"]
    x = x.astype(jnp.float32)
    b = []
    for g in range(0, LANE_CH, GROUP):
        a = dot(tables["gather"][...], bf16(x[:, g : g + GROUP].reshape(SEQ_PARTS * GROUP, ROWS)))
        b.append(jnp.concatenate(turned(a[:LINES], a[LINES:], c, s), 1))
    spec = dot(jnp.concatenate(b, 0), tables["turn"][...])
    return spec[:, :ROWS], spec[:, ROWS:]


def inverse(real, imag, tables):
    c, s = tables["cos"], tables["sin"]
    y = jnp.concatenate([bf16(real), bf16(imag)], 1)
    z = dot(y, tables["turn"][...], ((1,), (1,)))
    out = []
    for g in range(0, 2 * LINES, LINES):
        imag, real = turned(z[g : g + LINES, ROWS:], z[g : g + LINES, :ROWS], c, s)
        y = dot(tables["spread"][...], jnp.concatenate([real, imag], 0))
        out.append(y.reshape(SEQ_PARTS, GROUP, ROWS))
    return bf16(jnp.concatenate(out, 1))


TABLES = ("gather", "cos", "sin", "turn", "spread")


class Fetch:
    def __init__(self, far, near, sems):
        self.near = dict(zip(TABLES, near))
        self.copies = {
            n: pltpu.make_async_copy(f, t, sems.at[i]) for i, (n, f, t) in enumerate(zip(TABLES, far, near))
        }

    def start(self, *names):
        for name in names:
            self.copies[name].start()

    def wait(self, *names):
        for name in names:
            self.copies[name].wait()


def chunks(a):
    return bf16(a).reshape(SEQ_PARTS, LANE_CH, ROWS)


def flat(a):
    return a.reshape(WIDTH, ROWS)


def prepare_kernel(inner, values, taps, skip, out):
    product = inner[...].astype(jnp.float32) * values[...].astype(jnp.float32)
    out[:, :LANE_CH, :] = chunks(product.T)
    first = lax.broadcasted_iota(jnp.int32, (ROWS, WIDTH), 0) == 0
    out[:, LANE_CH:, :] = chunks((taps[...] + jnp.where(first, skip[...], 0.0)).T)


def project_kernel(where, weight, grad, out, blocks, sems):

    def copy(i):
        return pltpu.make_async_copy(weight.at[2 * i + where[1]], blocks.at[i], sems.at[i])

    @pl.loop(0, AHEAD)
    def _(i):
        copy(i).start()

    @pl.loop(0, 4)
    def _(i):
        copy(i).wait()

        @pl.when(i + AHEAD < 4)
        def _():
            copy(i + AHEAD).start()

        out[(i - where[0]) & 3] = bf16(dot(blocks[i], grad[...], ((1,), (1,))))


def add_kernel(where, kept, other, *outs):
    ahead = 1 + 2 * where[1]
    for slot, out in zip((2, 4 - ahead, ahead, 0), outs):
        out[...] = bf16(kept[slot].astype(jnp.float32) + other[slot].astype(jnp.float32))


def add_two_kernel(ahead, passed, own, back, out, total):
    out[...] = bf16(ahead[...].astype(jnp.float32) + passed[...].astype(jnp.float32))
    total[...] = own[...].astype(jnp.float32) + back[...].astype(jnp.float32)


def turn_kernel(outer, after, out):
    out[...] = bf16(outer[...].astype(jnp.float32).T)


def first_kernel(go, got, *refs):
    (sr, si, tr, ti), kept, sems = refs[5:9], refs[9:14], refs[14]
    fetch = Fetch(refs[:5], kept, sems)

    @pl.when(go[0] >= 0)
    def _():
        fetch.start(*TABLES)
        fetch.wait("gather", "cos", "sin", "turn")

    @pl.when(go[0] >= 0)
    def _():
        sr[...], si[...] = forward(got[:, :LANE_CH, :], fetch.near)
        tr[...], ti[...] = forward(got[:, LANE_CH:, :], fetch.near)
        fetch.wait("spread")


def conv_kernel(sr, si, tr, ti, *refs):
    tables, conv = dict(zip(TABLES, refs)), refs[-1]
    x_real, x_imag, t_real, t_imag = sr[...], si[...], tr[...], ti[...]
    conv[...] = inverse(x_real * t_real - x_imag * t_imag, x_real * t_imag + x_imag * t_real, tables)


def middle_kernel(own, last, outer_t, conv, out, hidden_grad_t):
    total = own[...] + last[...].astype(jnp.float32)
    hidden_grad_t[...] = total
    out[:, :LANE_CH, :] = chunks(total * outer_t[...].astype(jnp.float32))
    out[:, LANE_CH:, :] = conv[...]


def second_kernel(got, sr, si, tr, ti, *refs):
    tables, out = dict(zip(TABLES, refs)), refs[-1]
    g_real, g_imag = forward(got[:, :LANE_CH, :], tables)
    t_real, t_imag = tr[...], ti[...]
    out[:, :LANE_CH, :] = inverse(
        t_real * g_real + t_imag * g_imag, t_real * g_imag - t_imag * g_real, tables
    )
    x_real, x_imag = sr[...], si[...]
    out[:, LANE_CH:, :] = inverse(
        x_real * g_real + x_imag * g_imag, x_real * g_imag - x_imag * g_real, tables
    )


def gate_kernel(where, got, outer, hidden_grad_t, hidden, outer_grad, staged, sem):
    copy = pltpu.make_async_copy(staged, outer_grad, sem)
    mixed_pre = flat(got[:, LANE_CH:, :]).astype(jnp.float32)

    @pl.when(where[0] >= 0)
    def _():
        staged[...] = bf16((hidden_grad_t[...] * mixed_pre).T)
        copy.start()

    hidden[...] = bf16(outer[...].astype(jnp.float32) * mixed_pre.T)
    copy.wait()


def final_kernel(got, inner, values, inner_grad, values_grad, taps_grad):
    total = flat(got[:, :LANE_CH, :]).astype(jnp.float32).T
    inner_grad[...] = bf16(total * values[...].astype(jnp.float32))
    values_grad[...] = bf16(total * inner[...].astype(jnp.float32))
    taps_grad[...] = flat(got[:, LANE_CH:, :]).astype(jnp.float32).T


def token_kernel(sent, hidden, out):
    out[...] = hidden[:8, :128]


def fetch_kernel(weight, hidden, sent, out, sems):
    @pl.loop(0, 8)
    def _(i):
        pltpu.make_async_copy(weight.at[i], out.at[i], sems.at[i]).start()

    @pl.loop(0, 8)
    def _(i):
        pltpu.make_async_copy(weight.at[i], out.at[i], sems.at[i]).wait()


def mixed_kernel(where, weight, *refs):
    parts, base, out = refs[:-2], refs[-2], refs[-1]
    blocks = (0, 1 - 2 * where[1], 2 * where[1] - 1) if len(parts) == 6 else (2,)
    blocks = [2 * ((where[0] + b) & 3) + where[1] for b in blocks]
    mirror = (0, 2 * where[1] - 1, 1 - 2 * where[1]) if len(parts) == 6 else (2,)
    blocks += [2 * ((where[0] + b) & 3) + 1 - where[1] for b in mirror]
    for c in range(0, COLUMNS, 256):
        columns = slice(c, c + 256)
        total = base[:, columns] if len(parts) == 2 else None
        for part, block in zip(parts, blocks):
            term = dot(part[...], weight[block, :, columns])
            total = term if total is None else total + term
        out[:, columns] = total.astype(out.dtype)


def shape(dims, dtype):
    return jax.ShapeDtypeStruct(dims, dtype)


def inside(dims, dtype):
    return pltpu.VMEM(dims, dtype)


def outside(dims, dtype):
    return pltpu.HBM(dims, dtype)


VMEM = pl.BlockSpec(memory_space=pltpu.VMEM)
HBM = pl.BlockSpec(memory_space=pltpu.HBM)
SMEM = pl.BlockSpec(memory_space=pltpu.SMEM)


def local(kernel, outs, *args, limit=16, specs=None, out_specs=None, scratch=(), hold=(), cost=0.0):
    n = len(args)

    def body(*refs):
        kernel(*refs[:n], *refs[n + len(hold) :])

    return pl.pallas_call(
        body,
        out_shape=outs,
        in_specs=list(specs or [VMEM] * n) + [VMEM] * len(hold),
        out_specs=out_specs or tuple(VMEM for _ in outs),
        scratch_shapes=scratch,
        compiler_params=pltpu.CompilerParams(vmem_limit_bytes=limit << 20),
        cost_estimate=pl.CostEstimate(flops=int(cost * 1.15e9), bytes_accessed=1 << 16, transcendentals=0),
    )(*args, *map(near_memory, hold))


def far_memory(a):
    return pltpu.with_memory_space_constraint(a, pltpu.HBM)


def near_memory(a):
    return pltpu.with_memory_space_constraint(a, pltpu.VMEM)


def project(where, weight, grad, cost):
    return local(
        project_kernel,
        (inside((4, WIDTH, ROWS), jnp.bfloat16),),
        where,
        weight,
        grad,
        specs=[SMEM, HBM, VMEM],
        scratch=[pltpu.VMEM((4, WIDTH, COLUMNS), jnp.bfloat16), pltpu.SemaphoreType.DMA((4,))],
        cost=cost,
    )[0]


def mix(where, weight, parts, base, out):
    return local(
        mixed_kernel,
        (out((ROWS, COLUMNS), jnp.float32 if out is inside else jnp.bfloat16),),
        where,
        weight,
        *parts,
        base,
        specs=[SMEM] + [VMEM] * (2 + len(parts)),
        cost=COSTS[3] if out is inside else COSTS[4],
    )[0]


def exchange(a):
    return lax.all_to_all(a, "seq", split_axis=0, concat_axis=0, tiled=True)


def to_partner(a):
    return lax.ppermute(a, "ch", [(i, i ^ 1) for i in range(8)])


def along(a, way):
    pairs = [(2 * y + c, 2 * ((y + way * (1 - 2 * c)) % 4) + c) for y in range(4) for c in range(2)]
    return lax.ppermute(a, "ch", pairs)


def on_device(outer_gate, inner_gate, values, filter_taps, skip_scale, out_weight, out_grad):
    tables = [far_memory(transform_tables()[i]) for i in (0, 3, 4, 2, 1)]
    me = lax.axis_index("ch").astype(jnp.int32)
    row, core = me // 2, me % 2
    near_half, far_half = jnp.stack([row, core]), jnp.stack([row, 1 - core])
    block = (WIDTH, ROWS)
    block_row = (ROWS, WIDTH)
    sending = (SEQ_PARTS, 2 * LANE_CH, ROWS)
    weight = far_memory(out_weight.reshape(8, WIDTH, COLUMNS))

    skip = jnp.where(lax.axis_index("seq") == 0, skip_scale, 0.0).reshape(1, WIDTH)
    sent = local(
        prepare_kernel,
        (inside(sending, jnp.bfloat16),),
        *map(far_memory, (inner_gate, values, filter_taps)),
        skip,
        limit=8,
        cost=COSTS[8],
    )[0]
    sent, far_half, near_half = lax.optimization_barrier((sent, far_half, near_half))
    got = near_memory(exchange(sent))
    given = project(far_half, weight, out_grad, COSTS[0])
    given, near_half = lax.optimization_barrier((given, near_half))
    kept = project(near_half, weight, out_grad, COSTS[1])
    across, back, ahead, own = local(
        add_kernel,
        (inside(block, jnp.bfloat16),) * 3 + (outside(block, jnp.bfloat16),),
        near_half,
        kept,
        to_partner(given),
        specs=[SMEM, VMEM, VMEM],
    )
    passed = along(across, 1)
    back = along(back, -1)

    spectrum = inside((SLOTS * LANE_CH, ROWS), jnp.float32)
    kept = local(
        first_kernel,
        (*(spectrum,) * 4, *(inside(t.shape, t.dtype) for t in tables)),
        near_half,
        got,
        *tables,
        specs=[SMEM, VMEM] + [HBM] * len(tables),
        scratch=[pltpu.SemaphoreType.DMA((len(tables),))],
        cost=COSTS[6],
    )
    ahead, total = local(
        add_two_kernel,
        (inside(block, jnp.bfloat16), inside(block, jnp.float32)),
        ahead,
        passed,
        far_memory(own),
        back,
        hold=kept[:1],
    )
    conv = local(
        conv_kernel,
        (inside((SEQ_PARTS, LANE_CH, ROWS), jnp.bfloat16),),
        *map(near_memory, kept),
        hold=(ahead,),
        cost=COSTS[7],
    )[0]
    outer_t = local(
        turn_kernel,
        (inside(block, jnp.bfloat16),),
        far_memory(outer_gate),
        ahead,
        cost=COSTS[5],
    )[0]
    sums = [near_memory(total), along(ahead, 1)]
    sent, hidden_grad_t = local(
        middle_kernel,
        (inside(sending, jnp.bfloat16), inside(block, jnp.float32)),
        *sums,
        outer_t,
        conv,
        hold=kept,
    )
    got = near_memory(exchange(sent))
    hidden, outer_grad = local(
        gate_kernel,
        (inside(block_row, jnp.bfloat16), outside(block_row, jnp.bfloat16)),
        near_half,
        got,
        outer_gate,
        near_memory(hidden_grad_t),
        specs=[SMEM, VMEM, VMEM, VMEM],
        out_specs=(VMEM, HBM),
        scratch=[pltpu.VMEM(block_row, jnp.bfloat16), pltpu.SemaphoreType.DMA],
        hold=kept,
    )
    sent = local(
        second_kernel,
        (outside(sending, jnp.bfloat16),),
        got,
        *map(near_memory, kept),
        hold=(hidden,),
    )[0]
    returned = near_memory(exchange(sent))
    before = along(hidden, 1)
    if LATE:
        after = None
    else:
        after = along(hidden, -1)
    token = local(
        token_kernel,
        (inside((8, 128), jnp.bfloat16),),
        far_memory(sent),
        hidden,
        specs=[HBM, VMEM],
    )[0]
    passed, turned_back, token = lax.optimization_barrier((before, hidden, token))
    if LATE:
        after = along(turned_back, -1)
    kept_weight = local(
        fetch_kernel,
        (inside(weight.shape, weight.dtype),),
        weight,
        token,
        far_memory(sent),
        specs=[HBM, VMEM, HBM],
        scratch=[pltpu.SemaphoreType.DMA((8,))],
        cost=COSTS[2],
    )[0]
    across = along(passed, 1)
    near = [hidden, after, before]
    far = [to_partner(a) for a in near]
    part = mix(near_half, kept_weight, near + far, hidden, inside)
    mixed = mix(near_half, kept_weight, [across, to_partner(across)], part, outside)
    inner_grad, values_grad, taps_grad = local(
        final_kernel,
        (
            outside(block_row, jnp.bfloat16),
            outside(block_row, jnp.bfloat16),
            outside(block_row, jnp.float32),
        ),
        returned,
        inner_gate,
        values,
    )
    return (mixed, outer_grad, inner_grad, values_grad, taps_grad)


def solution(mesh):
    placed = (
        P("seq", "ch"),
        P("seq", "ch"),
        P("seq", "ch"),
        P("seq", "ch"),
        P("ch"),
        P(None, "ch"),
        P("seq", "ch"),
    )
    return jax.shard_map(
        on_device,
        mesh=mesh,
        in_specs=placed,
        out_specs=(P("seq", "ch"), P("seq", "ch"), P("seq", "ch"), P("seq", "ch"), P("seq", "ch")),
        check_vma=False,
    )
```

time: 103 us -> 98.3 us (0.954)
  Pallas kernels: 33.5 us -> 30.4 us
  blocking collectives: 20.7 us -> 23.7 us
  waiting for transfers between devices: 19.6 us -> 16.7 us
  starting transfers between devices: 27.6 us -> 26 us
    ppermute x3 -> x0, starting transfers between devices: 5.42 us -> none  [shifted(): return lax.ppermute(a, 'ch', [(i, (i + 2 * rows) % 8) for i in range(8)])]
    ppermute x3 -> x6, starting transfers between devices: 4.76 us -> 8.29 us  [along(): return lax.ppermute(a, 'ch', pairs)]
    all_to_all x2, waiting for transfers between devices: 13.1 us -> 10 us  [exchange(): return lax.all_to_all(a, 'seq', split_axis=0, concat_axis=0, tiled=True)]
    pallas_call x14 -> x16, Pallas kernels: 33.5 us -> 30.4 us  [local(): pl.pallas_call(body, out_shape=outs, in_specs=list(specs or [VMEM] * n) +...]
    all_to_all x1, blocking collectives: 20.7 us -> 23.7 us  [exchange(): return lax.all_to_all(a, 'seq', split_axis=0, concat_axis=0, tiled=True)]
    ppermute x3 -> x6, waiting for transfers between devices: 6.48 us -> 6.68 us  [along(): return lax.ppermute(a, 'ch', pairs)]
  transfers between devices with their start and end apart: 13 -> 13, of which waited for: 4 -> 4; matrix products, arithmetic and copies ran while one was open for 0% -> 0% of each run, Pallas kernels for 27% -> 25%
where the time goes in v2:
time: 98.3 us; the launch traced here: 97.8 us
  Pallas kernels  30.4 us (31%)
  starting transfers between devices  26 us (26%)
  blocking collectives  23.7 us (24%)
  waiting for transfers between devices  16.7 us (17%)
    pallas_call x16, Pallas kernels, local(): pl.pallas_call(body, out_shape=outs, in_specs=list(specs or [VMEM] * n) +...  30.4 us
    all_to_all x1, blocking collectives, exchange(): return lax.all_to_all(a, 'seq', split_axis=0, concat_axis=0, tiled=True)  23.7 us
    all_to_all x2, starting transfers between devices, exchange(): return lax.all_to_all(a, 'seq', split_axis=0, concat_axis=0, tiled=True)  16 us
    all_to_all x2, waiting for transfers between devices, exchange(): return lax.all_to_all(a, 'seq', split_axis=0, concat_axis=0, tiled=True)  10 us
    ppermute x6, starting transfers between devices, along(): return lax.ppermute(a, 'ch', pairs)  8.29 us
    ppermute x6, waiting for transfers between devices, along(): return lax.ppermute(a, 'ch', pairs)  6.68 us
  transfers between devices with their start and end apart: 13, of which 4 were waited for; matrix products, arithmetic and copies ran while one was open for 0% of the time, Pallas kernels for 25%

profile of v2, /device:TPU:32, one launch (start us, length us, event | category | flops | bytes accessed | tf_op | source)
XLA Modules:
  0.0 97.8 jit_solution(13354849429757088751)
XLA Ops:
  0.7 0.1 pad_add_fusion
  0.8 2.3 %shard_map.155 = bf16[32,32,256]{2,1,0:T(8,128)(2,1)} custom-call(bf16[256,512]{1,0:T(8,128)(2,1)} %refs_1_.3, bf16[256,512]{1,0:T(8,128)(2,1)} %refs_2_.9, f32[256,512]{1,0:T(8,128)} %refs_2_.5, f32[1,512]{1,0:T(1,128)S(1)} %bitcast.5), custom_call_target="tpu_custom_call" | custom-call | flops 23000000512 | bytes 65536 | tf_op jit(solution)/shard_map/pallas_call | solution.py:270
  3.0 11.2 %all-to-all-start = ((bf16[32,32,256]{2,1,0:T(8,128)(2,1)}), bf16[32,32,256]{2,1,0:T(8,128)(2,1)S(1)}, u32[]{:S(2)}, u32[]{:S(2)}) async-start(bf16[32,32,256]{2,1,0:T(8,128)(2,1)} %shard_map.155), calls=%async_computation | async-start | bytes 1048576 | tf_op jit(solution)/shard_map/all_to_all | solution.py:316
  14.2 3.7 %shard_map.156 = bf16[4,512,256]{2,1,0:T(8,128)(2,1)S(1)} custom-call(s32[2]{0:T(128)S(1)} %get-tuple-element.34.refs_0_, bf16[8,512,1024]{2,1,0:T(8,128)(2,1)} %bitcast.6, bf16[256,1024]{1,0:T(8,128)(2,1)S(1)} %copy-done.1), custom_call_target="tpu_custom_call" | custom-call | bytes 65536 | tf_op jit(solution)/shard_map/pallas_call | solution.py:270
  17.9 0.1 collective-permute-start
  18.0 3.7 %shard_map.157.refs_1_ = bf16[4,512,256]{2,1,0:T(8,128)(2,1)S(1)} custom-call(s32[2]{0:T(128)S(1)} %get-tuple-element.36.refs_0_, bf16[8,512,1024]{2,1,0:T(8,128)(2,1)} %bitcast.7, bf16[256,1024]{1,0:T(8,128)(2,1)S(1)} %copy-done.1), custom_call_target="tpu_custom_call" | custom-call | flops 11500000256 | bytes 65536 | tf_op jit(solution)/shard_map/pallas_call | solution.py:270
  21.8 1.4 %shard_map.158 = (bf16[512,256]{1,0:T(8,128)(2,1)S(1)}, bf16[512,256]{1,0:T(8,128)(2,1)S(1)}, bf16[512,256]{1,0:T(8,128)(2,1)S(1)}, bf16[512,256]{1,0:T(8,128)(2,1)}) custom-call(s32[2]{0:T(128)S(1)} %get-tuple-element.36.refs_0_, bf16[4,512,256]{2,1,0:T(8,128)(2,1)S(1)} %shard_map.157.refs_1_, bf16[4,512,256]{2,1,0:T(8,128)(2,1)S(1)} %collective-permute-done.refs_2_), custom_call_target="tpu_custom_call" | custom-call | bytes 65536 | tf_op jit(solution)/shard_map/pallas_call | solution.py:270
  23.2 1.6 %collective-permute-start.1 = (bf16[512,256]{1,0:T(8,128)(2,1)S(1)}, bf16[512,256]{1,0:T(8,128)(2,1)S(1)}, u32[]{:S(2)}, u32[]{:S(2)}) collective-permute-start(bf16[512,256]{1,0:T(8,128)(2,1)S(1)} %get-tuple-element.39), channel_id=1, source_target_pairs={{0,2},{1,7},{2,4},{3,1},{4,6},{5,3},{6,0},{7,5},{8,10},{9,15},{10,... | collective-permute-start | bytes 786440 | tf_op jit(solution)/shard_map/ppermute | solution.py:325
  24.8 1.7 %collective-permute-start.2 = (bf16[512,256]{1,0:T(8,128)(2,1)S(1)}, bf16[512,256]{1,0:T(8,128)(2,1)S(1)}, u32[]{:S(2)}, u32[]{:S(2)}) collective-permute-start(bf16[512,256]{1,0:T(8,128)(2,1)S(1)} %get-tuple-element.41), channel_id=1, source_target_pairs={{0,6},{1,3},{2,0},{3,5},{4,2},{5,7},{6,4},{7,1},{8,14},{9,11},{10,... | collective-permute-start | bytes 786440 | tf_op jit(solution)/shard_map/ppermute | solution.py:325
  26.4 5.4 %all-to-all-done.refs_1_ = bf16[32,32,256]{2,1,0:T(8,128)(2,1)S(1)} async-done(((bf16[32,32,256]{2,1,0:T(8,128)(2,1)}), bf16[32,32,256]{2,1,0:T(8,128)(2,1)S(1)}, u32[]{:S(2)}, u32[]{:S(2)}) %all-to-all-start) | async-done | bytes 524320 | tf_op jit(solution)/shard_map/all_to_all | solution.py:316
  31.8 3.2 %shard_map.159 = (f32[512,256]{1,0:T(8,128)S(1)}, f32[512,256]{1,0:T(8,128)S(1)}, f32[512,256]{1,0:T(8,128)S(1)}, f32[512,256]{1,0:T(8,128)S(1)}, bf16[512,256]{...) custom-call(s32[2]{0:T(128)S(1)} %get-tuple-element.36.refs_0_, ...), custom_call_target="tpu_custom_call" | custom-call | bytes 65536 | tf_op jit(solution)/shard_map/pallas_call | solution.py:270
  35.0 1.1 %shard_map.160 = (bf16[512,256]{1,0:T(8,128)(2,1)S(1)}, f32[512,256]{1,0:T(8,128)S(1)}) custom-call(bf16[512,256]{1,0:T(8,128)(2,1)S(1)} %get-tuple-element.38.refs_0_, bf16[512,256]{1,0:T(8,128)(2,1)S(1)} %collective-permute-done.1.refs_1_, bf16[512,256]{1,0:T(8,128)(2,1)} %get-tuple-element.40.refs_2_, ...), custom_call_target="tpu_custom_call" | custom-call | bytes 65536 | tf_op jit(solution)/shard_map/pallas_call | solution.py:270
  36.1 1.7 %collective-permute-start.3 = (bf16[512,256]{1,0:T(8,128)(2,1)S(1)}, bf16[512,256]{1,0:T(8,128)(2,1)S(1)}, u32[]{:S(2)}, u32[]{:S(2)}) collective-permute-start(bf16[512,256]{1,0:T(8,128)(2,1)S(1)} %get-tuple-element.45.refs_1_.refs_9_), channel_id=1, source_target_pairs={{0,2},{1,7},{2,4},{3,1},{4,6},{5,3},{6,0},{7,5},{8,10},{9,15},{10,... | collective-permute-start | bytes 786440 | tf_op jit(solution)/shard_map/ppermute | solution.py:325
  37.8 1.1 %shard_map.161.refs_2_ = bf16[512,256]{1,0:T(8,128)(2,1)S(1)} custom-call(bf16[256,512]{1,0:T(8,128)(2,1)} %refs_2_.8, bf16[512,256]{1,0:T(8,128)(2,1)S(1)} %get-tuple-element.45.refs_1_.refs_9_), custom_call_target="tpu_custom_call" | custom-call | bytes 65536 | tf_op jit(solution)/shard_map/pallas_call | solution.py:270
  38.9 0.7 shard_map.162.refs_3_
  39.6 4.2 %collective-permute-done.3.refs_1_ = bf16[512,256]{1,0:T(8,128)(2,1)S(1)} collective-permute-done((bf16[512,256]{1,0:T(8,128)(2,1)S(1)}, bf16[512,256]{1,0:T(8,128)(2,1)S(1)}, u32[]{:S(2)}, u32[]{:S(2)}) %collective-permute-start.3) | collective-permute-done | bytes 262176 | tf_op jit(solution)/shard_map/ppermute | solution.py:325
  43.8 0.1 shard_map.163
  43.9 23.7 %all_to_all.15.refs_1_.refs_0_ = bf16[32,32,256]{2,1,0:T(8,128)(2,1)S(1)} all-to-all(bf16[32,32,256]{2,1,0:T(8,128)(2,1)S(1)} %get-tuple-element.54), channel_id=1, replica_groups=mesh['seq'=32,'ch'=8] {'seq'}, dimensions={0} | all-to-all | bytes 1048576 | tf_op jit(solution)/shard_map/all_to_all | solution.py:316
  67.6 1.4 %shard_map.164 = (bf16[256,512]{1,0:T(8,128)(2,1)S(1)}, bf16[256,512]{1,0:T(8,128)(2,1)}) custom-call(s32[2]{0:T(128)S(1)} %get-tuple-element.36.refs_0_, bf16[32,32,256]{2,1,0:T(8,128)(2,1)S(1)} %all_to_all.15.refs_1_.refs_0_, bf16[256,512]{1,0:T(8,128)(2,1)S(1)} %copy-done, f32[512,256]{1,0:T(8,128)S(1)} %get-tuple-element.55.refs_3_, ...), custom_call_target="tpu_custom_call" | custom-call | bytes 65536 | tf_op jit(solution)/shard_map/pallas_call | solution.py:270
  69.0 0.4 collective-permute-start.4
  69.4 2.9 %collective-permute-start.7 = (bf16[256,512]{1,0:T(8,128)(2,1)S(1)}, bf16[256,512]{1,0:T(8,128)(2,1)S(1)}, u32[]{:S(2)}, u32[]{:S(2)}) collective-permute-start(bf16[256,512]{1,0:T(8,128)(2,1)S(1)} %get-tuple-element.56.refs_10_.refs_1_.refs_2_.refs_8_), channel_id=1, source_target_pairs={{0,6},{1,3},{2,0},{3,5},{4,2},{5,7},{6,4},{7,1},{8,14},{9,11},{10,... | collective-permute-start | bytes 786440 | tf_op jit(solution)/shard_map/ppermute | solution.py:325
  72.3 2.8 %shard_map.165.refs_0_.refs_2_ = bf16[32,32,256]{2,1,0:T(8,128)(2,1)} custom-call(bf16[32,32,256]{2,1,0:T(8,128)(2,1)S(1)} %all_to_all.15.refs_1_.refs_0_, f32[512,256]{1,0:T(8,128)S(1)} %get-tuple-element.43.refs_4_.refs_0_.refs_1_, f32[512,256]{1,0:T(8,128)S(1)} %get-tuple-element.46.refs_1_.refs_5_.refs_2_, ...), custom_call_target="tpu_custom_call" | custom-call | bytes 65536 | tf_op jit(solution)/shard_map/pallas_call | solution.py:270
  75.1 4.8 %all-to-all-start.2 = ((bf16[32,32,256]{2,1,0:T(8,128)(2,1)}), bf16[32,32,256]{2,1,0:T(8,128)(2,1)S(1)}, u32[]{:S(2)}, u32[]{:S(2)}) async-start(bf16[32,32,256]{2,1,0:T(8,128)(2,1)} %shard_map.165.refs_0_.refs_2_), calls=%async_computation.2 | async-start | bytes 1048576 | tf_op jit(solution)/shard_map/all_to_all | solution.py:316
  79.9 0.1 collective-permute-start.5
  80.0 1.1 %collective-permute-start.8 = (bf16[256,512]{1,0:T(8,128)(2,1)S(1)}, bf16[256,512]{1,0:T(8,128)(2,1)S(1)}, u32[]{:S(2)}, u32[]{:S(2)}) collective-permute-start(bf16[256,512]{1,0:T(8,128)(2,1)S(1)} %get-tuple-element.56.refs_10_.refs_1_.refs_2_.refs_8_), channel_id=1, source_target_pairs={{0,1},{1,0},{2,3},{3,2},{4,5},{5,4},{6,7},{7,6},{8,9},{9,8},{10,11... | collective-permute-start | bytes 786440 | tf_op jit(solution)/shard_map/ppermute | solution.py:320
  81.1 0.5 collective-permute-start.9
  81.6 3.5 %shard_map.167.refs_1_ = bf16[8,512,1024]{2,1,0:T(8,128)(2,1)S(1)} custom-call(bf16[8,512,1024]{2,1,0:T(8,128)(2,1)} %bitcast.8, bf16[8,128]{1,0:T(8,128)(2,1)S(1)} %shard_map.166.refs_1_, bf16[32,32,256]{2,1,0:T(8,128)(2,1)} %shard_map.165.refs_0_.refs_2_), custom_call_target="tpu_custom_call" | custom-call | flops 2300000000 | bytes 65536 | tf_op jit(solution)/shard_map/pallas_call | solution.py:270
  85.1 2.5 %collective-permute-done.5.refs_2_ = bf16[256,512]{1,0:T(8,128)(2,1)S(1)} collective-permute-done((bf16[256,512]{1,0:T(8,128)(2,1)S(1)}, bf16[256,512]{1,0:T(8,128)(2,1)S(1)}, u32[]{:S(2)}, u32[]{:S(2)}) %collective-permute-start.5) | collective-permute-done | bytes 262176 | tf_op jit(solution)/shard_map/ppermute | solution.py:325
  87.6 2.3 %shard_map.168.refs_4_ = f32[256,1024]{1,0:T(8,128)S(1)} custom-call(s32[2]{0:T(128)S(1)} %get-tuple-element.36.refs_0_, bf16[8,512,1024]{2,1,0:T(8,128)(2,1)S(1)} %shard_map.167.refs_1_, bf16[256,512]{1,0:T(8,128)(2,1)S(1)} %get-tuple-element.56.refs_10_.refs_1_.refs_2_.refs_8_, bf16[256,512]{1,0:T(8,128)(2,1)S(1)} %collective-permute-done.7.refs_3_, ...), custom_call_target="tpu_custom_call" | custom-call | flops 5750000128 | bytes 65536 | tf_op jit(solution)/shard_map/pallas_call | solution.py:270
  90.0 2.1 %shard_map.169 = bf16[256,1024]{1,0:T(8,128)(2,1)} custom-call(s32[2]{0:T(128)S(1)} %get-tuple-element.36.refs_0_, bf16[8,512,1024]{2,1,0:T(8,128)(2,1)S(1)} %shard_map.167.refs_1_, bf16[256,512]{1,0:T(8,128)(2,1)S(1)} %collective-permute-done.5.refs_2_, bf16[256,512]{1,0:T(8,128)(2,1)S(1)} %collective-permute-done.6.refs_3_, f32[256,1024]{1,0:T(8,128)S(1)} %shard_map.168.refs_4_), custom_call_target="tpu_custom_call" | custom-call | bytes 65536 | tf_op jit(solution)/shard_map/pallas_call | solution.py:270
  92.0 4.7 %all-to-all-done.2.refs_0_ = bf16[32,32,256]{2,1,0:T(8,128)(2,1)S(1)} async-done(((bf16[32,32,256]{2,1,0:T(8,128)(2,1)}), bf16[32,32,256]{2,1,0:T(8,128)(2,1)S(1)}, u32[]{:S(2)}, u32[]{:S(2)}) %all-to-all-start.2) | async-done | bytes 524320 | tf_op jit(solution)/shard_map/all_to_all | solution.py:316
  96.7 1.1 %shard_map.170 = (bf16[256,512]{1,0:T(8,128)(2,1)}, bf16[256,512]{1,0:T(8,128)(2,1)}, f32[256,512]{1,0:T(8,128)}) custom-call(bf16[32,32,256]{2,1,0:T(8,128)(2,1)S(1)} %all-to-all-done.2.refs_0_, bf16[256,512]{1,0:T(8,128)(2,1)S(1)} %copy-done.2, bf16[256,512]{1,0:T(8,128)(2,1)S(1)} %copy-done.3), custom_call_target="tpu_custom_call" | custom-call | bytes 65536 | tf_op jit(solution)/shard_map/pallas_call | solution.py:270
  (21 shorter events, 0.1 us)
Async XLA Ops:
  0.8 13.5 %copy-start.1 = (bf16[256,1024]{1,0:T(8,128)(2,1)S(1)}, bf16[256,1024]{1,0:T(8,128)(2,1)}, u32[]{:S(2)}) copy-start(bf16[256,1024]{1,0:T(8,128)(2,1)} %refs_2_.7) | copy-start | bytes 1572868
  3.0 28.8 %all-to-all-start = ((bf16[32,32,256]{2,1,0:T(8,128)(2,1)}), bf16[32,32,256]{2,1,0:T(8,128)(2,1)S(1)}, u32[]{:S(2)}, u32[]{:S(2)}) async-start(bf16[32,32,256]{2,1,0:T(8,128)(2,1)} %shard_map.155), calls=%async_computation | async-start | bytes 1048576 | tf_op jit(solution)/shard_map/all_to_all | solution.py:316
  17.9 3.8 %collective-permute-start = (bf16[4,512,256]{2,1,0:T(8,128)(2,1)S(1)}, bf16[4,512,256]{2,1,0:T(8,128)(2,1)S(1)}, u32[]{:S(2)}, u32[]{:S(2)}) collective-permute-start(bf16[4,512,256]{2,1,0:T(8,128)(2,1)S(1)} %shard_map.156), channel_id=1, source_target_pairs={{0,1},{1,0},{2,3},{3,2},{4,5},{5,4},{6,7},{7,6},{8,9},{9,8},{10,11... | collective-permute-start | bytes 3145736 | tf_op jit(solution)/shard_map/ppermute | solution.py:320
  21.8 45.8 %copy-start = (bf16[256,512]{1,0:T(8,128)(2,1)S(1)}, bf16[256,512]{1,0:T(8,128)(2,1)}, u32[]{:S(2)}) copy-start(bf16[256,512]{1,0:T(8,128)(2,1)} %refs_2_.8) | copy-start | bytes 786436
  23.2 11.8 %collective-permute-start.1 = (bf16[512,256]{1,0:T(8,128)(2,1)S(1)}, bf16[512,256]{1,0:T(8,128)(2,1)S(1)}, u32[]{:S(2)}, u32[]{:S(2)}) collective-permute-start(bf16[512,256]{1,0:T(8,128)(2,1)S(1)} %get-tuple-element.39), channel_id=1, source_target_pairs={{0,2},{1,7},{2,4},{3,1},{4,6},{5,3},{6,0},{7,5},{8,10},{9,15},{10,... | collective-permute-start | bytes 786440 | tf_op jit(solution)/shard_map/ppermute | solution.py:325
  24.8 10.2 %collective-permute-start.2 = (bf16[512,256]{1,0:T(8,128)(2,1)S(1)}, bf16[512,256]{1,0:T(8,128)(2,1)S(1)}, u32[]{:S(2)}, u32[]{:S(2)}) collective-permute-start(bf16[512,256]{1,0:T(8,128)(2,1)S(1)} %get-tuple-element.41), channel_id=1, source_target_pairs={{0,6},{1,3},{2,0},{3,5},{4,2},{5,7},{6,4},{7,1},{8,14},{9,11},{10,... | collective-permute-start | bytes 786440 | tf_op jit(solution)/shard_map/ppermute | solution.py:325
  36.1 7.7 %collective-permute-start.3 = (bf16[512,256]{1,0:T(8,128)(2,1)S(1)}, bf16[512,256]{1,0:T(8,128)(2,1)S(1)}, u32[]{:S(2)}, u32[]{:S(2)}) collective-permute-start(bf16[512,256]{1,0:T(8,128)(2,1)S(1)} %get-tuple-element.45.refs_1_.refs_9_), channel_id=1, source_target_pairs={{0,2},{1,7},{2,4},{3,1},{4,6},{5,3},{6,0},{7,5},{8,10},{9,15},{10,... | collective-permute-start | bytes 786440 | tf_op jit(solution)/shard_map/ppermute | solution.py:325
  69.0 10.9 %collective-permute-start.4 = (bf16[256,512]{1,0:T(8,128)(2,1)S(1)}, bf16[256,512]{1,0:T(8,128)(2,1)S(1)}, u32[]{:S(2)}, u32[]{:S(2)}) collective-permute-start(bf16[256,512]{1,0:T(8,128)(2,1)S(1)} %get-tuple-element.56.refs_10_.refs_1_.refs_2_.refs_8_), channel_id=1, source_target_pairs={{0,2},{1,7},{2,4},{3,1},{4,6},{5,3},{6,0},{7,5},{8,10},{9,15},{10,... | collective-permute-start | bytes 786440 | tf_op jit(solution)/shard_map/ppermute | solution.py:325
  69.4 11.7 %collective-permute-start.7 = (bf16[256,512]{1,0:T(8,128)(2,1)S(1)}, bf16[256,512]{1,0:T(8,128)(2,1)S(1)}, u32[]{:S(2)}, u32[]{:S(2)}) collective-permute-start(bf16[256,512]{1,0:T(8,128)(2,1)S(1)} %get-tuple-element.56.refs_10_.refs_1_.refs_2_.refs_8_), channel_id=1, source_target_pairs={{0,6},{1,3},{2,0},{3,5},{4,2},{5,7},{6,4},{7,1},{8,14},{9,11},{10,... | collective-permute-start | bytes 786440 | tf_op jit(solution)/shard_map/ppermute | solution.py:325
  75.1 21.6 %all-to-all-start.2 = ((bf16[32,32,256]{2,1,0:T(8,128)(2,1)}), bf16[32,32,256]{2,1,0:T(8,128)(2,1)S(1)}, u32[]{:S(2)}, u32[]{:S(2)}) async-start(bf16[32,32,256]{2,1,0:T(8,128)(2,1)} %shard_map.165.refs_0_.refs_2_), calls=%async_computation.2 | async-start | bytes 1048576 | tf_op jit(solution)/shard_map/all_to_all | solution.py:316
  79.9 7.7 %collective-permute-start.5 = (bf16[256,512]{1,0:T(8,128)(2,1)S(1)}, bf16[256,512]{1,0:T(8,128)(2,1)S(1)}, u32[]{:S(2)}, u32[]{:S(2)}) collective-permute-start(bf16[256,512]{1,0:T(8,128)(2,1)S(1)} %collective-permute-done.4.refs_4_), channel_id=1, source_target_pairs={{0,2},{1,7},{2,4},{3,1},{4,6},{5,3},{6,0},{7,5},{8,10},{9,15},{10,... | collective-permute-start | bytes 786440 | tf_op jit(solution)/shard_map/ppermute | solution.py:325
  80.0 7.6 %collective-permute-start.8 = (bf16[256,512]{1,0:T(8,128)(2,1)S(1)}, bf16[256,512]{1,0:T(8,128)(2,1)S(1)}, u32[]{:S(2)}, u32[]{:S(2)}) collective-permute-start(bf16[256,512]{1,0:T(8,128)(2,1)S(1)} %get-tuple-element.56.refs_10_.refs_1_.refs_2_.refs_8_), channel_id=1, source_target_pairs={{0,1},{1,0},{2,3},{3,2},{4,5},{5,4},{6,7},{7,6},{8,9},{9,8},{10,11... | collective-permute-start | bytes 786440 | tf_op jit(solution)/shard_map/ppermute | solution.py:320
  81.1 6.5 %collective-permute-start.10 = (bf16[256,512]{1,0:T(8,128)(2,1)S(1)}, bf16[256,512]{1,0:T(8,128)(2,1)S(1)}, u32[]{:S(2)}, u32[]{:S(2)}) collective-permute-start(bf16[256,512]{1,0:T(8,128)(2,1)S(1)} %collective-permute-done.4.refs_4_), channel_id=1, source_target_pairs={{0,1},{1,0},{2,3},{3,2},{4,5},{5,4},{6,7},{7,6},{8,9},{9,8},{10,11... | collective-permute-start | bytes 786440 | tf_op jit(solution)/shard_map/ppermute | solution.py:320
  81.1 6.5 %collective-permute-start.9 = (bf16[256,512]{1,0:T(8,128)(2,1)S(1)}, bf16[256,512]{1,0:T(8,128)(2,1)S(1)}, u32[]{:S(2)}, u32[]{:S(2)}) collective-permute-start(bf16[256,512]{1,0:T(8,128)(2,1)S(1)} %collective-permute-done.7.refs_3_), channel_id=1, source_target_pairs={{0,1},{1,0},{2,3},{3,2},{4,5},{5,4},{6,7},{7,6},{8,9},{9,8},{10,11... | collective-permute-start | bytes 786440 | tf_op jit(solution)/shard_map/ppermute | solution.py:320
  87.6 2.4 %collective-permute-start.6 = (bf16[256,512]{1,0:T(8,128)(2,1)S(1)}, bf16[256,512]{1,0:T(8,128)(2,1)S(1)}, u32[]{:S(2)}, u32[]{:S(2)}) collective-permute-start(bf16[256,512]{1,0:T(8,128)(2,1)S(1)} %collective-permute-done.5.refs_2_), channel_id=1, source_target_pairs={{0,1},{1,0},{2,3},{3,2},{4,5},{5,4},{6,7},{7,6},{8,9},{9,8},{10,11... | collective-permute-start | bytes 786440 | tf_op jit(solution)/shard_map/ppermute | solution.py:320
  90.0 6.7 %copy-start.2 = (bf16[256,512]{1,0:T(8,128)(2,1)S(1)}, bf16[256,512]{1,0:T(8,128)(2,1)}, u32[]{:S(2)}) copy-start(bf16[256,512]{1,0:T(8,128)(2,1)} %refs_1_.3) | copy-start | bytes 786436
  90.0 6.7 %copy-start.3 = (bf16[256,512]{1,0:T(8,128)(2,1)S(1)}, bf16[256,512]{1,0:T(8,128)(2,1)}, u32[]{:S(2)}) copy-start(bf16[256,512]{1,0:T(8,128)(2,1)} %refs_2_.9) | copy-start | bytes 786436

commit v3 on v2

--- a/solution.py
+++ b/solution.py
@@ -61,15 +61,21 @@
     return bf16(real * c + imag * s), bf16(imag * c - real * s)
 
 
-def forward(x, tables):
+def gathered(x, tables):
+    x = x.astype(jnp.float32)
+    parts = (x[:, g : g + GROUP].reshape(SEQ_PARTS * GROUP, ROWS) for g in range(0, LANE_CH, GROUP))
+    return [dot(tables["gather"][...], bf16(part)) for part in parts]
+
+
+def transformed(parts, tables):
     c, s = tables["cos"], tables["sin"]
-    x = x.astype(jnp.float32)
-    b = []
-    for g in range(0, LANE_CH, GROUP):
-        a = dot(tables["gather"][...], bf16(x[:, g : g + GROUP].reshape(SEQ_PARTS * GROUP, ROWS)))
-        b.append(jnp.concatenate(turned(a[:LINES], a[LINES:], c, s), 1))
+    b = [jnp.concatenate(turned(a[:LINES], a[LINES:], c, s), 1) for a in parts]
     spec = dot(jnp.concatenate(b, 0), tables["turn"][...])
     return spec[:, :ROWS], spec[:, ROWS:]
+
+
+def forward(x, tables):
+    return transformed(gathered(x, tables), tables)
 
 
 def inverse(real, imag, tables):
@@ -118,65 +124,69 @@
     out[:, LANE_CH:, :] = chunks((taps[...] + jnp.where(first, skip[...], 0.0)).T)
 
 
-def project_kernel(where, weight, grad, out, blocks, sems):
+def project_kernel(first, where, weight, grad, out, blocks, sems):
+    n = out.shape[0]
 
     def copy(i):
-        return pltpu.make_async_copy(weight.at[2 * i + where[1]], blocks.at[i], sems.at[i])
-
-    @pl.loop(0, AHEAD)
+        block = 2 * ((where[0] + first + i) & 3) + where[1]
+        return pltpu.make_async_copy(weight.at[block], blocks.at[i], sems.at[i])
+
+    @pl.loop(0, min(n, AHEAD))
     def _(i):
         copy(i).start()
 
-    @pl.loop(0, 4)
+    @pl.loop(0, n)
     def _(i):
         copy(i).wait()
 
-        @pl.when(i + AHEAD < 4)
+        @pl.when(i + AHEAD < n)
         def _():
             copy(i + AHEAD).start()
 
-        out[(i - where[0]) & 3] = bf16(dot(blocks[i], grad[...], ((1,), (1,))))
-
-
-def add_kernel(where, kept, other, *outs):
-    ahead = 1 + 2 * where[1]
-    for slot, out in zip((2, 4 - ahead, ahead, 0), outs):
-        out[...] = bf16(kept[slot].astype(jnp.float32) + other[slot].astype(jnp.float32))
-
-
-def add_two_kernel(ahead, passed, own, back, out, total):
-    out[...] = bf16(ahead[...].astype(jnp.float32) + passed[...].astype(jnp.float32))
-    total[...] = own[...].astype(jnp.float32) + back[...].astype(jnp.float32)
-
-
-def turn_kernel(outer, after, out):
-    out[...] = bf16(outer[...].astype(jnp.float32).T)
+        out[i] = bf16(dot(blocks[i], grad[...], ((1,), (1,))))
+
+
+def add_kernel(first, kept, other, *outs):
+    for i, out in enumerate(outs):
+        out[...] = bf16(kept[i].astype(jnp.float32) + other[first + i].astype(jnp.float32))
+
+
+def sum_kernel(own, passed, total):
+    total[...] = own[...].astype(jnp.float32) + passed[...].astype(jnp.float32)
 
 
 def first_kernel(go, got, *refs):
-    (sr, si, tr, ti), kept, sems = refs[5:9], refs[9:14], refs[14]
+    (sr, si, tr, ti), kept, (sems, parts) = refs[5:9], refs[9:14], refs[14:]
     fetch = Fetch(refs[:5], kept, sems)
 
     @pl.when(go[0] >= 0)
     def _():
         fetch.start(*TABLES)
-        fetch.wait("gather", "cos", "sin", "turn")
+        fetch.wait("gather")
 
     @pl.when(go[0] >= 0)
     def _():
-        sr[...], si[...] = forward(got[:, :LANE_CH, :], fetch.near)
-        tr[...], ti[...] = forward(got[:, LANE_CH:, :], fetch.near)
+        halves = (got[:, :LANE_CH, :], got[:, LANE_CH:, :])
+        for i, part in enumerate(p for half in halves for p in gathered(half, fetch.near)):
+            parts[i] = part
+        fetch.wait("cos", "sin", "turn")
+
+    @pl.when(go[0] >= 0)
+    def _():
+        sr[...], si[...] = transformed([parts[0], parts[1]], fetch.near)
+        tr[...], ti[...] = transformed([parts[2], parts[3]], fetch.near)
         fetch.wait("spread")
 
 
 def conv_kernel(sr, si, tr, ti, *refs):
-    tables, conv = dict(zip(TABLES, refs)), refs[-1]
+    tables, (outer, conv, outer_t) = dict(zip(TABLES, refs)), refs[-3:]
+    outer_t[...] = bf16(outer[...].astype(jnp.float32).T)
     x_real, x_imag, t_real, t_imag = sr[...], si[...], tr[...], ti[...]
     conv[...] = inverse(x_real * t_real - x_imag * t_imag, x_real * t_imag + x_imag * t_real, tables)
 
 
-def middle_kernel(own, last, outer_t, conv, out, hidden_grad_t):
-    total = own[...] + last[...].astype(jnp.float32)
+def middle_kernel(own, a, b, outer_t, conv, out, hidden_grad_t):
+    total = own[...] + (a[...].astype(jnp.float32) + b[...].astype(jnp.float32))
     hidden_grad_t[...] = total
     out[:, :LANE_CH, :] = chunks(total * outer_t[...].astype(jnp.float32))
     out[:, LANE_CH:, :] = conv[...]
@@ -286,15 +296,15 @@
     return pltpu.with_memory_space_constraint(a, pltpu.VMEM)
 
 
-def project(where, weight, grad, cost):
+def project(first, count, where, weight, grad, cost):
     return local(
-        project_kernel,
-        (inside((4, WIDTH, ROWS), jnp.bfloat16),),
+        lambda *refs: project_kernel(first, *refs),
+        (inside((count, WIDTH, ROWS), jnp.bfloat16),),
         where,
         weight,
         grad,
         specs=[SMEM, HBM, VMEM],
-        scratch=[pltpu.VMEM((4, WIDTH, COLUMNS), jnp.bfloat16), pltpu.SemaphoreType.DMA((4,))],
+        scratch=[pltpu.VMEM((count, WIDTH, COLUMNS), jnp.bfloat16), pltpu.SemaphoreType.DMA((count,))],
         cost=cost,
     )[0]
 
@@ -325,6 +335,10 @@
     return lax.ppermute(a, "ch", pairs)
 
 
+def shifted(a, rows):
+    return lax.ppermute(a, "ch", [(i, (i + 2 * rows) % 8) for i in range(8)])
+
+
 def on_device(outer_gate, inner_gate, values, filter_taps, skip_scale, out_weight, out_grad):
     tables = [far_memory(transform_tables()[i]) for i in (0, 3, 4, 2, 1)]
     me = lax.axis_index("ch").astype(jnp.int32)
@@ -346,19 +360,29 @@
     )[0]
     sent, far_half, near_half = lax.optimization_barrier((sent, far_half, near_half))
     got = near_memory(exchange(sent))
-    given = project(far_half, weight, out_grad, COSTS[0])
+    given = project(2, 4, far_half, weight, out_grad, COSTS[0])
     given, near_half = lax.optimization_barrier((given, near_half))
-    kept = project(near_half, weight, out_grad, COSTS[1])
-    across, back, ahead, own = local(
-        add_kernel,
-        (inside(block, jnp.bfloat16),) * 3 + (outside(block, jnp.bfloat16),),
-        near_half,
+    kept = project(2, 1, near_half, weight, out_grad, COSTS[1])
+    other = near_memory(to_partner(given))
+    across = local(
+        lambda *refs: add_kernel(0, *refs), (inside(block, jnp.bfloat16),), kept, other
+    )[0]
+    across, near_half = lax.optimization_barrier((across, near_half))
+    kept = project(3, 3, near_half, weight, out_grad, COSTS[1])
+    back, own, ahead = local(
+        lambda *refs: add_kernel(1, *refs),
+        (inside(block, jnp.bfloat16), outside(block, jnp.bfloat16), inside(block, jnp.bfloat16)),
         kept,
-        to_partner(given),
-        specs=[SMEM, VMEM, VMEM],
-    )
-    passed = along(across, 1)
-    back = along(back, -1)
+        other,
+    )
+    total = local(
+        sum_kernel,
+        (inside(block, jnp.float32),),
+        far_memory(own),
+        shifted(across, 2),
+        hold=(got,),
+    )[0]
+    sums = [near_memory(total), shifted(ahead, 1), shifted(back, 3)]
 
     spectrum = inside((SLOTS * LANE_CH, ROWS), jnp.float32)
     kept = local(
@@ -368,33 +392,20 @@
         got,
         *tables,
         specs=[SMEM, VMEM] + [HBM] * len(tables),
-        scratch=[pltpu.SemaphoreType.DMA((len(tables),))],
+        scratch=[
+            pltpu.SemaphoreType.DMA((len(tables),)),
+            pltpu.VMEM((4, 2 * LINES, ROWS), jnp.float32),
+        ],
+        hold=(total,),
         cost=COSTS[6],
     )
-    ahead, total = local(
-        add_two_kernel,
-        (inside(block, jnp.bfloat16), inside(block, jnp.float32)),
-        ahead,
-        passed,
-        far_memory(own),
-        back,
-        hold=kept[:1],
-    )
-    conv = local(
+    conv, outer_t = local(
         conv_kernel,
-        (inside((SEQ_PARTS, LANE_CH, ROWS), jnp.bfloat16),),
+        (inside((SEQ_PARTS, LANE_CH, ROWS), jnp.bfloat16), inside(block, jnp.bfloat16)),
         *map(near_memory, kept),
-        hold=(ahead,),
+        outer_gate,
         cost=COSTS[7],
-    )[0]
-    outer_t = local(
-        turn_kernel,
-        (inside(block, jnp.bfloat16),),
-        far_memory(outer_gate),
-        ahead,
-        cost=COSTS[5],
-    )[0]
-    sums = [near_memory(total), along(ahead, 1)]
+    )
     sent, hidden_grad_t = local(
         middle_kernel,
         (inside(sending, jnp.bfloat16), inside(block, jnp.float32)),

time: 98.3 us -> 92.4 us (0.940)
  waiting for transfers between devices: 16.7 us -> 11.9 us
  blocking collectives: 23.7 us -> 22.1 us
  Pallas kernels: 30.4 us -> 29.2 us
  starting transfers between devices: 26 us -> 27 us
    ppermute x0 -> x3, starting transfers between devices: none -> 6.52 us  [shifted(): return lax.ppermute(a, 'ch', [(i, (i + 2 * rows) % 8) for i in range(8)])]
    ppermute x6 -> x3, starting transfers between devices: 8.29 us -> 3.8 us  [along(): return lax.ppermute(a, 'ch', pairs)]
    ppermute x6 -> x3, waiting for transfers between devices: 6.68 us -> 3.17 us  [along(): return lax.ppermute(a, 'ch', pairs)]
    all_to_all x1, blocking collectives: 23.7 us -> 22.1 us  [exchange(): return lax.all_to_all(a, 'seq', split_axis=0, concat_axis=0, tiled=True)]
    all_to_all x2, waiting for transfers between devices: 10 us -> 8.69 us  [exchange(): return lax.all_to_all(a, 'seq', split_axis=0, concat_axis=0, tiled=True)]
    pallas_call x16 -> x17, Pallas kernels: 30.4 us -> 29.2 us  [local(): pl.pallas_call(body, out_shape=outs, in_specs=list(specs or [VMEM] * n) +...]
    ppermute x5, starting transfers between devices: 1.68 us -> 0.61 us  [to_partner(): return lax.ppermute(a, 'ch', [(i, i ^ 1) for i in range(8)])]
  transfers between devices with their start and end apart: 13 -> 13, of which waited for: 4 -> 3; matrix products, arithmetic and copies ran while one was open for 0% -> 0% of each run, Pallas kernels for 25% -> 23%
where the time goes in v3:
time: 92.4 us; the launch traced here: 91.9 us
  Pallas kernels  29.2 us (32%)
  starting transfers between devices  27 us (29%)
  blocking collectives  22.1 us (24%)
  waiting for transfers between devices  11.9 us (13%)
    pallas_call x17, Pallas kernels, local(): pl.pallas_call(body, out_shape=outs, in_specs=list(specs or [VMEM] * n) +...  29.2 us
    all_to_all x1, blocking collectives, exchange(): return lax.all_to_all(a, 'seq', split_axis=0, concat_axis=0, tiled=True)  22.1 us
    all_to_all x2, starting transfers between devices, exchange(): return lax.all_to_all(a, 'seq', split_axis=0, concat_axis=0, tiled=True)  16 us
    all_to_all x2, waiting for transfers between devices, exchange(): return lax.all_to_all(a, 'seq', split_axis=0, concat_axis=0, tiled=True)  8.69 us
    ppermute x3, starting transfers between devices, shifted(): return lax.ppermute(a, 'ch', [(i, (i + 2 * rows) % 8) for i in range(8)])  6.52 us
    ppermute x3, starting transfers between devices, along(): return lax.ppermute(a, 'ch', pairs)  3.8 us
    ppermute x3, waiting for transfers between devices, along(): return lax.ppermute(a, 'ch', pairs)  3.17 us
  transfers between devices with their start and end apart: 13, of which 3 were waited for; matrix products, arithmetic and copies ran while one was open for 0% of the time, Pallas kernels for 23%

profile of v3, /device:TPU:32, one launch (start us, length us, event | category | flops | bytes accessed | tf_op | source)
XLA Modules:
  0.0 91.9 jit_solution(15272075371202293679)
XLA Ops:
  0.7 0.1 pad_add_fusion
  0.8 1.5 %shard_map.155 = bf16[32,32,256]{2,1,0:T(8,128)(2,1)S(1)} custom-call(bf16[256,512]{1,0:T(8,128)(2,1)} %refs_1_.3, bf16[256,512]{1,0:T(8,128)(2,1)} %refs_2_.11, f32[256,512]{1,0:T(8,128)} %refs_2_.6, f32[1,512]{1,0:T(1,128)S(1)} %bitcast.5), custom_call_target="tpu_custom_call" | custom-call | flops 23000000512 | bytes 65536 | tf_op jit(solution)/shard_map/pallas_call | solution.py:280
  2.2 0.8 copy-done.2
  3.0 3.7 %shard_map.156 = bf16[4,512,256]{2,1,0:T(8,128)(2,1)S(1)} custom-call(s32[2]{0:T(128)S(1)} %get-tuple-element.35.refs_0_, bf16[8,512,1024]{2,1,0:T(8,128)(2,1)} %bitcast.6, bf16[256,1024]{1,0:T(8,128)(2,1)S(1)} %copy-done.1), custom_call_target="tpu_custom_call" | custom-call | bytes 65536 | tf_op jit(solution)/shard_map/pallas_call | solution.py:280
  6.7 0.1 collective-permute-start
  6.8 11.2 %all-to-all-start = ((bf16[32,32,256]{2,1,0:T(8,128)(2,1)}), bf16[32,32,256]{2,1,0:T(8,128)(2,1)S(1)}, u32[]{:S(2)}, u32[]{:S(2)}) async-start(bf16[32,32,256]{2,1,0:T(8,128)(2,1)} %copy-done.2), calls=%async_computation | async-start | bytes 1048576 | tf_op jit(solution)/shard_map/all_to_all | solution.py:326
  18.1 2.3 %shard_map.157.refs_0_ = bf16[1,512,256]{2,1,0:T(8,128)(2,1)S(1)} custom-call(s32[2]{0:T(128)S(1)} %get-tuple-element.39.refs_0_, bf16[8,512,1024]{2,1,0:T(8,128)(2,1)} %bitcast.7, bf16[256,1024]{1,0:T(8,128)(2,1)S(1)} %copy-done.1), custom_call_target="tpu_custom_call" | custom-call | flops 11500000256 | bytes 65536 | tf_op jit(solution)/shard_map/pallas_call | solution.py:280
  20.3 0.1 shard_map.158
  20.4 3.3 %collective-permute-start.1 = (bf16[512,256]{1,0:T(8,128)(2,1)S(1)}, bf16[512,256]{1,0:T(8,128)(2,1)S(1)}, u32[]{:S(2)}, u32[]{:S(2)}) collective-permute-start(bf16[512,256]{1,0:T(8,128)(2,1)S(1)} %shard_map.158), channel_id=1, source_target_pairs={{0,4},{1,5},{2,6},{3,7},{4,0},{5,1},{6,2},{7,3},{8,12},{9,13},{10,... | collective-permute-start | bytes 786440 | tf_op jit(solution)/shard_map/ppermute | solution.py:339
  23.7 3.2 %shard_map.159.refs_0_ = bf16[3,512,256]{2,1,0:T(8,128)(2,1)S(1)} custom-call(s32[2]{0:T(128)S(1)} %get-tuple-element.39.refs_0_, bf16[8,512,1024]{2,1,0:T(8,128)(2,1)} %bitcast.8, bf16[256,1024]{1,0:T(8,128)(2,1)S(1)} %copy-done.1), custom_call_target="tpu_custom_call" | custom-call | flops 11500000256 | bytes 65536 | tf_op jit(solution)/shard_map/pallas_call | solution.py:280
  26.9 0.8 shard_map.160
  27.7 0.7 collective-permute-start.2
  28.4 2.6 %collective-permute-start.3 = (bf16[512,256]{1,0:T(8,128)(2,1)S(1)}, bf16[512,256]{1,0:T(8,128)(2,1)S(1)}, u32[]{:S(2)}, u32[]{:S(2)}) collective-permute-start(bf16[512,256]{1,0:T(8,128)(2,1)S(1)} %get-tuple-element.44), channel_id=1, source_target_pairs={{0,6},{1,7},{2,0},{3,1},{4,2},{5,3},{6,4},{7,5},{8,14},{9,15},{10,... | collective-permute-start | bytes 786440 | tf_op jit(solution)/shard_map/ppermute | solution.py:339
  31.0 5.4 %all-to-all-done.refs_2_.refs_1_ = bf16[32,32,256]{2,1,0:T(8,128)(2,1)S(1)} async-done(((bf16[32,32,256]{2,1,0:T(8,128)(2,1)}), bf16[32,32,256]{2,1,0:T(8,128)(2,1)S(1)}, u32[]{:S(2)}, u32[]{:S(2)}) %all-to-all-start) | async-done | bytes 524320 | tf_op jit(solution)/shard_map/all_to_all | solution.py:326
  36.3 1.0 %shard_map.161.refs_7_.refs_0_ = f32[512,256]{1,0:T(8,128)S(1)} custom-call(bf16[512,256]{1,0:T(8,128)(2,1)} %get-tuple-element.40.refs_0_, bf16[512,256]{1,0:T(8,128)(2,1)S(1)} %collective-permute-done.1.refs_1_, bf16[32,32,256]{2,1,0:T(8,128)(2,1)S(1)} %all-to-all-done.refs_2_.refs_1_), custom_call_target="tpu_custom_call" | custom-call | bytes 65536 | tf_op jit(solution)/shard_map/pallas_call | solution.py:280
  37.3 2.7 %shard_map.162 = (f32[512,256]{1,0:T(8,128)S(1)}, f32[512,256]{1,0:T(8,128)S(1)}, f32[512,256]{1,0:T(8,128)S(1)}, f32[512,256]{1,0:T(8,128)S(1)}, bf16[512,256]{...) custom-call(s32[2]{0:T(128)S(1)} %get-tuple-element.39.refs_0_, ...), custom_call_target="tpu_custom_call" | custom-call | bytes 65536 | tf_op jit(solution)/shard_map/pallas_call | solution.py:280
  40.1 0.7 shard_map.163
  40.8 0.1 shard_map.164
  41.0 22.1 %all_to_all.15.refs_1_.refs_0_ = bf16[32,32,256]{2,1,0:T(8,128)(2,1)S(1)} all-to-all(bf16[32,32,256]{2,1,0:T(8,128)(2,1)S(1)} %get-tuple-element.56), channel_id=1, replica_groups=mesh['seq'=32,'ch'=8] {'seq'}, dimensions={0} | all-to-all | bytes 1048576 | tf_op jit(solution)/shard_map/all_to_all | solution.py:326
  63.1 1.4 %shard_map.165 = (bf16[256,512]{1,0:T(8,128)(2,1)S(1)}, bf16[256,512]{1,0:T(8,128)(2,1)}) custom-call(s32[2]{0:T(128)S(1)} %get-tuple-element.39.refs_0_, bf16[32,32,256]{2,1,0:T(8,128)(2,1)S(1)} %all_to_all.15.refs_1_.refs_0_, bf16[256,512]{1,0:T(8,128)(2,1)S(1)} %copy-done, f32[512,256]{1,0:T(8,128)S(1)} %get-tuple-element.57.refs_3_, ...), custom_call_target="tpu_custom_call" | custom-call | bytes 65536 | tf_op jit(solution)/shard_map/pallas_call | solution.py:280
  64.5 1.7 %collective-permute-start.4 = (bf16[256,512]{1,0:T(8,128)(2,1)S(1)}, bf16[256,512]{1,0:T(8,128)(2,1)S(1)}, u32[]{:S(2)}, u32[]{:S(2)}) collective-permute-start(bf16[256,512]{1,0:T(8,128)(2,1)S(1)} %get-tuple-element.58.refs_10_.refs_1_.refs_2_.refs_8_), channel_id=1, source_target_pairs={{0,2},{1,7},{2,4},{3,1},{4,6},{5,3},{6,0},{7,5},{8,10},{9,15},{10,... | collective-permute-start | bytes 786440 | tf_op jit(solution)/shard_map/ppermute | solution.py:335
  66.2 1.6 %collective-permute-start.7 = (bf16[256,512]{1,0:T(8,128)(2,1)S(1)}, bf16[256,512]{1,0:T(8,128)(2,1)S(1)}, u32[]{:S(2)}, u32[]{:S(2)}) collective-permute-start(bf16[256,512]{1,0:T(8,128)(2,1)S(1)} %get-tuple-element.58.refs_10_.refs_1_.refs_2_.refs_8_), channel_id=1, source_target_pairs={{0,6},{1,3},{2,0},{3,5},{4,2},{5,7},{6,4},{7,1},{8,14},{9,11},{10,... | collective-permute-start | bytes 786440 | tf_op jit(solution)/shard_map/ppermute | solution.py:335
  67.8 2.6 %shard_map.166.refs_0_.refs_2_ = bf16[32,32,256]{2,1,0:T(8,128)(2,1)} custom-call(bf16[32,32,256]{2,1,0:T(8,128)(2,1)S(1)} %all_to_all.15.refs_1_.refs_0_, f32[512,256]{1,0:T(8,128)S(1)} %get-tuple-element.45.refs_0_.refs_5_.refs_4_.refs_1_, f32[512,256]{1,0:T(8,128)S(1)} %get-tuple-element.46.refs_1_.refs_6_.refs_5_.refs_2_, ...), custom_call_target="tpu_custom_call" | custom-call | bytes 65536 | tf_op jit(solution)/shard_map/pallas_call | solution.py:280
  70.4 4.8 %all-to-all-start.2 = ((bf16[32,32,256]{2,1,0:T(8,128)(2,1)}), bf16[32,32,256]{2,1,0:T(8,128)(2,1)S(1)}, u32[]{:S(2)}, u32[]{:S(2)}) async-start(bf16[32,32,256]{2,1,0:T(8,128)(2,1)} %shard_map.166.refs_0_.refs_2_), calls=%async_computation.2 | async-start | bytes 1048576 | tf_op jit(solution)/shard_map/all_to_all | solution.py:326
  75.3 0.5 collective-permute-start.5
  75.8 0.5 collective-permute-start.10
  76.3 3.5 %shard_map.168.refs_1_ = bf16[8,512,1024]{2,1,0:T(8,128)(2,1)S(1)} custom-call(bf16[8,512,1024]{2,1,0:T(8,128)(2,1)} %bitcast.9, bf16[8,128]{1,0:T(8,128)(2,1)S(1)} %shard_map.167.refs_1_, bf16[32,32,256]{2,1,0:T(8,128)(2,1)} %shard_map.166.refs_0_.refs_2_), custom_call_target="tpu_custom_call" | custom-call | flops 2300000000 | bytes 65536 | tf_op jit(solution)/shard_map/pallas_call | solution.py:280
  79.8 3.2 %collective-permute-done.5.refs_2_ = bf16[256,512]{1,0:T(8,128)(2,1)S(1)} collective-permute-done((bf16[256,512]{1,0:T(8,128)(2,1)S(1)}, bf16[256,512]{1,0:T(8,128)(2,1)S(1)}, u32[]{:S(2)}, u32[]{:S(2)}) %collective-permute-start.5) | collective-permute-done | bytes 262176 | tf_op jit(solution)/shard_map/ppermute | solution.py:335
  83.0 2.3 %shard_map.169.refs_4_ = f32[256,1024]{1,0:T(8,128)S(1)} custom-call(s32[2]{0:T(128)S(1)} %get-tuple-element.39.refs_0_, bf16[8,512,1024]{2,1,0:T(8,128)(2,1)S(1)} %shard_map.168.refs_1_, bf16[256,512]{1,0:T(8,128)(2,1)S(1)} %get-tuple-element.58.refs_10_.refs_1_.refs_2_.refs_8_, bf16[256,512]{1,0:T(8,128)(2,1)S(1)} %collective-permute-done.7.refs_3_, ...), custom_call_target="tpu_custom_call" | custom-call | flops 5750000128 | bytes 65536 | tf_op jit(solution)/shard_map/pallas_call | solution.py:280
  85.3 2.1 %shard_map.170 = bf16[256,1024]{1,0:T(8,128)(2,1)} custom-call(s32[2]{0:T(128)S(1)} %get-tuple-element.39.refs_0_, bf16[8,512,1024]{2,1,0:T(8,128)(2,1)S(1)} %shard_map.168.refs_1_, bf16[256,512]{1,0:T(8,128)(2,1)S(1)} %collective-permute-done.5.refs_2_, bf16[256,512]{1,0:T(8,128)(2,1)S(1)} %collective-permute-done.6.refs_3_, f32[256,1024]{1,0:T(8,128)S(1)} %shard_map.169.refs_4_), custom_call_target="tpu_custom_call" | custom-call | bytes 65536 | tf_op jit(solution)/shard_map/pallas_call | solution.py:280
  87.4 3.3 %all-to-all-done.2.refs_0_ = bf16[32,32,256]{2,1,0:T(8,128)(2,1)S(1)} async-done(((bf16[32,32,256]{2,1,0:T(8,128)(2,1)}), bf16[32,32,256]{2,1,0:T(8,128)(2,1)S(1)}, u32[]{:S(2)}, u32[]{:S(2)}) %all-to-all-start.2) | async-done | bytes 524320 | tf_op jit(solution)/shard_map/all_to_all | solution.py:326
  90.8 1.1 %shard_map.171 = (bf16[256,512]{1,0:T(8,128)(2,1)}, bf16[256,512]{1,0:T(8,128)(2,1)}, f32[256,512]{1,0:T(8,128)}) custom-call(bf16[32,32,256]{2,1,0:T(8,128)(2,1)S(1)} %all-to-all-done.2.refs_0_, bf16[256,512]{1,0:T(8,128)(2,1)S(1)} %copy-done.3, bf16[256,512]{1,0:T(8,128)(2,1)S(1)} %copy-done.4), custom_call_target="tpu_custom_call" | custom-call | bytes 65536 | tf_op jit(solution)/shard_map/pallas_call | solution.py:280
  (24 shorter events, 0.1 us)
Async XLA Ops:
  0.8 2.3 %copy-start.1 = (bf16[256,1024]{1,0:T(8,128)(2,1)S(1)}, bf16[256,1024]{1,0:T(8,128)(2,1)}, u32[]{:S(2)}) copy-start(bf16[256,1024]{1,0:T(8,128)(2,1)} %refs_2_.9) | copy-start | bytes 1572868
  2.2 0.8 copy-start.2
  6.7 13.6 %collective-permute-start = (bf16[4,512,256]{2,1,0:T(8,128)(2,1)S(1)}, bf16[4,512,256]{2,1,0:T(8,128)(2,1)S(1)}, u32[]{:S(2)}, u32[]{:S(2)}) collective-permute-start(bf16[4,512,256]{2,1,0:T(8,128)(2,1)S(1)} %shard_map.156), channel_id=1, source_target_pairs={{0,1},{1,0},{2,3},{3,2},{4,5},{5,4},{6,7},{7,6},{8,9},{9,8},{10,11... | collective-permute-start | bytes 3145736 | tf_op jit(solution)/shard_map/ppermute | solution.py:330
  6.8 29.5 %all-to-all-start = ((bf16[32,32,256]{2,1,0:T(8,128)(2,1)}), bf16[32,32,256]{2,1,0:T(8,128)(2,1)S(1)}, u32[]{:S(2)}, u32[]{:S(2)}) async-start(bf16[32,32,256]{2,1,0:T(8,128)(2,1)} %copy-done.2), calls=%async_computation | async-start | bytes 1048576 | tf_op jit(solution)/shard_map/all_to_all | solution.py:326
  20.4 19.7 %copy-start = (bf16[256,512]{1,0:T(8,128)(2,1)S(1)}, bf16[256,512]{1,0:T(8,128)(2,1)}, u32[]{:S(2)}) copy-start(bf16[256,512]{1,0:T(8,128)(2,1)} %refs_2_.10) | copy-start | bytes 786436
  20.4 15.9 %collective-permute-start.1 = (bf16[512,256]{1,0:T(8,128)(2,1)S(1)}, bf16[512,256]{1,0:T(8,128)(2,1)S(1)}, u32[]{:S(2)}, u32[]{:S(2)}) collective-permute-start(bf16[512,256]{1,0:T(8,128)(2,1)S(1)} %shard_map.158), channel_id=1, source_target_pairs={{0,4},{1,5},{2,6},{3,7},{4,0},{5,1},{6,2},{7,3},{8,12},{9,13},{10,... | collective-permute-start | bytes 786440 | tf_op jit(solution)/shard_map/ppermute | solution.py:339
  27.7 13.1 %collective-permute-start.2 = (bf16[512,256]{1,0:T(8,128)(2,1)S(1)}, bf16[512,256]{1,0:T(8,128)(2,1)S(1)}, u32[]{:S(2)}, u32[]{:S(2)}) collective-permute-start(bf16[512,256]{1,0:T(8,128)(2,1)S(1)} %get-tuple-element.43), channel_id=1, source_target_pairs={{0,2},{1,3},{2,4},{3,5},{4,6},{5,7},{6,0},{7,1},{8,10},{9,11},{10,... | collective-permute-start | bytes 786440 | tf_op jit(solution)/shard_map/ppermute | solution.py:339
  28.4 12.4 %collective-permute-start.3 = (bf16[512,256]{1,0:T(8,128)(2,1)S(1)}, bf16[512,256]{1,0:T(8,128)(2,1)S(1)}, u32[]{:S(2)}, u32[]{:S(2)}) collective-permute-start(bf16[512,256]{1,0:T(8,128)(2,1)S(1)} %get-tuple-element.44), channel_id=1, source_target_pairs={{0,6},{1,7},{2,0},{3,1},{4,2},{5,3},{6,4},{7,5},{8,14},{9,15},{10,... | collective-permute-start | bytes 786440 | tf_op jit(solution)/shard_map/ppermute | solution.py:339
  64.5 10.8 %collective-permute-start.4 = (bf16[256,512]{1,0:T(8,128)(2,1)S(1)}, bf16[256,512]{1,0:T(8,128)(2,1)S(1)}, u32[]{:S(2)}, u32[]{:S(2)}) collective-permute-start(bf16[256,512]{1,0:T(8,128)(2,1)S(1)} %get-tuple-element.58.refs_10_.refs_1_.refs_2_.refs_8_), channel_id=1, source_target_pairs={{0,2},{1,7},{2,4},{3,1},{4,6},{5,3},{6,0},{7,5},{8,10},{9,15},{10,... | collective-permute-start | bytes 786440 | tf_op jit(solution)/shard_map/ppermute | solution.py:335
  66.2 10.1 %collective-permute-start.7 = (bf16[256,512]{1,0:T(8,128)(2,1)S(1)}, bf16[256,512]{1,0:T(8,128)(2,1)S(1)}, u32[]{:S(2)}, u32[]{:S(2)}) collective-permute-start(bf16[256,512]{1,0:T(8,128)(2,1)S(1)} %get-tuple-element.58.refs_10_.refs_1_.refs_2_.refs_8_), channel_id=1, source_target_pairs={{0,6},{1,3},{2,0},{3,5},{4,2},{5,7},{6,4},{7,1},{8,14},{9,11},{10,... | collective-permute-start | bytes 786440 | tf_op jit(solution)/shard_map/ppermute | solution.py:335
  70.4 20.4 %all-to-all-start.2 = ((bf16[32,32,256]{2,1,0:T(8,128)(2,1)}), bf16[32,32,256]{2,1,0:T(8,128)(2,1)S(1)}, u32[]{:S(2)}, u32[]{:S(2)}) async-start(bf16[32,32,256]{2,1,0:T(8,128)(2,1)} %shard_map.166.refs_0_.refs_2_), calls=%async_computation.2 | async-start | bytes 1048576 | tf_op jit(solution)/shard_map/all_to_all | solution.py:326
  75.3 7.7 %collective-permute-start.5 = (bf16[256,512]{1,0:T(8,128)(2,1)S(1)}, bf16[256,512]{1,0:T(8,128)(2,1)S(1)}, u32[]{:S(2)}, u32[]{:S(2)}) collective-permute-start(bf16[256,512]{1,0:T(8,128)(2,1)S(1)} %collective-permute-done.4.refs_4_), channel_id=1, source_target_pairs={{0,2},{1,7},{2,4},{3,1},{4,6},{5,3},{6,0},{7,5},{8,10},{9,15},{10,... | collective-permute-start | bytes 786440 | tf_op jit(solution)/shard_map/ppermute | solution.py:335
  75.8 7.2 %collective-permute-start.8 = (bf16[256,512]{1,0:T(8,128)(2,1)S(1)}, bf16[256,512]{1,0:T(8,128)(2,1)S(1)}, u32[]{:S(2)}, u32[]{:S(2)}) collective-permute-start(bf16[256,512]{1,0:T(8,128)(2,1)S(1)} %get-tuple-element.58.refs_10_.refs_1_.refs_2_.refs_8_), channel_id=1, source_target_pairs={{0,1},{1,0},{2,3},{3,2},{4,5},{5,4},{6,7},{7,6},{8,9},{9,8},{10,11... | collective-permute-start | bytes 786440 | tf_op jit(solution)/shard_map/ppermute | solution.py:330
  75.8 7.2 %collective-permute-start.10 = (bf16[256,512]{1,0:T(8,128)(2,1)S(1)}, bf16[256,512]{1,0:T(8,128)(2,1)S(1)}, u32[]{:S(2)}, u32[]{:S(2)}) collective-permute-start(bf16[256,512]{1,0:T(8,128)(2,1)S(1)} %collective-permute-done.4.refs_4_), channel_id=1, source_target_pairs={{0,1},{1,0},{2,3},{3,2},{4,5},{5,4},{6,7},{7,6},{8,9},{9,8},{10,11... | collective-permute-start | bytes 786440 | tf_op jit(solution)/shard_map/ppermute | solution.py:330
  76.3 6.7 %collective-permute-start.9 = (bf16[256,512]{1,0:T(8,128)(2,1)S(1)}, bf16[256,512]{1,0:T(8,128)(2,1)S(1)}, u32[]{:S(2)}, u32[]{:S(2)}) collective-permute-start(bf16[256,512]{1,0:T(8,128)(2,1)S(1)} %collective-permute-done.7.refs_3_), channel_id=1, source_target_pairs={{0,1},{1,0},{2,3},{3,2},{4,5},{5,4},{6,7},{7,6},{8,9},{9,8},{10,11... | collective-permute-start | bytes 786440 | tf_op jit(solution)/shard_map/ppermute | solution.py:330
  83.0 2.4 %collective-permute-start.6 = (bf16[256,512]{1,0:T(8,128)(2,1)S(1)}, bf16[256,512]{1,0:T(8,128)(2,1)S(1)}, u32[]{:S(2)}, u32[]{:S(2)}) collective-permute-start(bf16[256,512]{1,0:T(8,128)(2,1)S(1)} %collective-permute-done.5.refs_2_), channel_id=1, source_target_pairs={{0,1},{1,0},{2,3},{3,2},{4,5},{5,4},{6,7},{7,6},{8,9},{9,8},{10,11... | collective-permute-start | bytes 786440 | tf_op jit(solution)/shard_map/ppermute | solution.py:330
  85.3 5.5 %copy-start.3 = (bf16[256,512]{1,0:T(8,128)(2,1)S(1)}, bf16[256,512]{1,0:T(8,128)(2,1)}, u32[]{:S(2)}) copy-start(bf16[256,512]{1,0:T(8,128)(2,1)} %refs_1_.3) | copy-start | bytes 786436
  85.3 5.5 %copy-start.4 = (bf16[256,512]{1,0:T(8,128)(2,1)S(1)}, bf16[256,512]{1,0:T(8,128)(2,1)}, u32[]{:S(2)}) copy-start(bf16[256,512]{1,0:T(8,128)(2,1)} %refs_2_.11) | copy-start | bytes 786436

commit v4 on v3

--- a/solution.py
+++ b/solution.py
@@ -151,17 +151,16 @@
         out[...] = bf16(kept[i].astype(jnp.float32) + other[first + i].astype(jnp.float32))
 
 
-def sum_kernel(own, passed, total):
-    total[...] = own[...].astype(jnp.float32) + passed[...].astype(jnp.float32)
-
-
 def first_kernel(go, got, *refs):
-    (sr, si, tr, ti), kept, (sems, parts) = refs[5:9], refs[9:14], refs[14:]
-    fetch = Fetch(refs[:5], kept, sems)
+    far, own, (sr, si, tr, ti) = refs[:5], refs[5], refs[6:10]
+    kept, own_near, (sems, parts) = refs[10:15], refs[15], refs[16:]
+    fetch = Fetch(far, kept, sems)
+    fetch_own = pltpu.make_async_copy(own, own_near, sems.at[len(TABLES)])
 
     @pl.when(go[0] >= 0)
     def _():
         fetch.start(*TABLES)
+        fetch_own.start()
         fetch.wait("gather")
 
     @pl.when(go[0] >= 0)
@@ -176,6 +175,7 @@
         sr[...], si[...] = transformed([parts[0], parts[1]], fetch.near)
         tr[...], ti[...] = transformed([parts[2], parts[3]], fetch.near)
         fetch.wait("spread")
+        fetch_own.wait()
 
 
 def conv_kernel(sr, si, tr, ti, *refs):
@@ -185,15 +185,18 @@
     conv[...] = inverse(x_real * t_real - x_imag * t_imag, x_real * t_imag + x_imag * t_real, tables)
 
 
-def middle_kernel(own, a, b, outer_t, conv, out, hidden_grad_t):
-    total = own[...] + (a[...].astype(jnp.float32) + b[...].astype(jnp.float32))
+def middle_kernel(own, a, b, c, outer_t, conv, out, hidden_grad_t):
+    total = (own[...].astype(jnp.float32) + a[...].astype(jnp.float32)) + (
+        b[...].astype(jnp.float32) + c[...].astype(jnp.float32)
+    )
     hidden_grad_t[...] = total
     out[:, :LANE_CH, :] = chunks(total * outer_t[...].astype(jnp.float32))
     out[:, LANE_CH:, :] = conv[...]
 
 
-def second_kernel(got, sr, si, tr, ti, *refs):
-    tables, out = dict(zip(TABLES, refs)), refs[-1]
+def second_kernel(got, gated, sr, si, tr, ti, *refs):
+    tables, (out, outer_grad) = dict(zip(TABLES, refs)), refs[-2:]
+    outer_grad[...] = gated[...]
     g_real, g_imag = forward(got[:, :LANE_CH, :], tables)
     t_real, t_imag = tr[...], ti[...]
     out[:, :LANE_CH, :] = inverse(
@@ -205,17 +208,10 @@
     )
 
 
-def gate_kernel(where, got, outer, hidden_grad_t, hidden, outer_grad, staged, sem):
-    copy = pltpu.make_async_copy(staged, outer_grad, sem)
+def gate_kernel(got, outer, hidden_grad_t, hidden, gated):
     mixed_pre = flat(got[:, LANE_CH:, :]).astype(jnp.float32)
-
-    @pl.when(where[0] >= 0)
-    def _():
-        staged[...] = bf16((hidden_grad_t[...] * mixed_pre).T)
-        copy.start()
-
     hidden[...] = bf16(outer[...].astype(jnp.float32) * mixed_pre.T)
-    copy.wait()
+    gated[...] = bf16((hidden_grad_t[...] * mixed_pre).T)
 
 
 def final_kernel(got, inner, values, inner_grad, values_grad, taps_grad):
@@ -375,28 +371,27 @@
         kept,
         other,
     )
-    total = local(
-        sum_kernel,
-        (inside(block, jnp.float32),),
-        far_memory(own),
-        shifted(across, 2),
-        hold=(got,),
-    )[0]
-    sums = [near_memory(total), shifted(ahead, 1), shifted(back, 3)]
+    across = near_memory(shifted(across, 2))
+    sums = [across, shifted(ahead, 1), shifted(back, 3)]
 
     spectrum = inside((SLOTS * LANE_CH, ROWS), jnp.float32)
-    kept = local(
+    *kept, own = local(
         first_kernel,
-        (*(spectrum,) * 4, *(inside(t.shape, t.dtype) for t in tables)),
+        (
+            *(spectrum,) * 4,
+            *(inside(t.shape, t.dtype) for t in tables),
+            inside(block, jnp.bfloat16),
+        ),
         near_half,
         got,
         *tables,
-        specs=[SMEM, VMEM] + [HBM] * len(tables),
+        far_memory(own),
+        specs=[SMEM, VMEM] + [HBM] * (len(tables) + 1),
         scratch=[
-            pltpu.SemaphoreType.DMA((len(tables),)),
+            pltpu.SemaphoreType.DMA((len(tables) + 1,)),
             pltpu.VMEM((4, 2 * LINES, ROWS), jnp.float32),
         ],
-        hold=(total,),
+        hold=(across,),
         cost=COSTS[6],
     )
     conv, outer_t = local(
@@ -409,31 +404,28 @@
     sent, hidden_grad_t = local(
         middle_kernel,
         (inside(sending, jnp.bfloat16), inside(block, jnp.float32)),
+        near_memory(own),
         *sums,
         outer_t,
         conv,
         hold=kept,
     )
     got = near_memory(exchange(sent))
-    hidden, outer_grad = local(
+    hidden, gated = local(
         gate_kernel,
-        (inside(block_row, jnp.bfloat16), outside(block_row, jnp.bfloat16)),
-        near_half,
+        (inside(block_row, jnp.bfloat16), inside(block_row, jnp.bfloat16)),
         got,
         outer_gate,
         near_memory(hidden_grad_t),
-        specs=[SMEM, VMEM, VMEM, VMEM],
-        out_specs=(VMEM, HBM),
-        scratch=[pltpu.VMEM(block_row, jnp.bfloat16), pltpu.SemaphoreType.DMA],
         hold=kept,
     )
-    sent = local(
+    sent, outer_grad = local(
         second_kernel,
-        (outside(sending, jnp.bfloat16),),
+        (outside(sending, jnp.bfloat16), outside(block_row, jnp.bfloat16)),
         got,
-        *map(near_memory, kept),
+        *map(near_memory, (gated, *kept)),
         hold=(hidden,),
-    )[0]
+    )
     returned = near_memory(exchange(sent))
     before = along(hidden, 1)
     if LATE:

time: 92.4 us -> 91.3 us (0.988)
  Pallas kernels: 29.2 us -> 27.4 us
    pallas_call x17 -> x16, Pallas kernels: 29.2 us -> 27.4 us  [local(): pl.pallas_call(body, out_shape=outs, in_specs=list(specs or [VMEM] * n) +...]
where the time goes in v4:
time: 91.3 us; the launch traced here: 90.5 us
  Pallas kernels  27.4 us (30%)
  starting transfers between devices  27 us (30%)
  blocking collectives  22.9 us (25%)
  waiting for transfers between devices  11.4 us (12%)
    pallas_call x16, Pallas kernels, local(): pl.pallas_call(body, out_shape=outs, in_specs=list(specs or [VMEM] * n) +...  27.4 us
    all_to_all x1, blocking collectives, exchange(): return lax.all_to_all(a, 'seq', split_axis=0, concat_axis=0, tiled=True)  22.9 us
    all_to_all x2, starting transfers between devices, exchange(): return lax.all_to_all(a, 'seq', split_axis=0, concat_axis=0, tiled=True)  16 us
    all_to_all x2, waiting for transfers between devices, exchange(): return lax.all_to_all(a, 'seq', split_axis=0, concat_axis=0, tiled=True)  8.26 us
    ppermute x3, starting transfers between devices, shifted(): return lax.ppermute(a, 'ch', [(i, (i + 2 * rows) % 8) for i in range(8)])  6.52 us
    ppermute x3, starting transfers between devices, along(): return lax.ppermute(a, 'ch', pairs)  3.81 us
    ppermute x3, waiting for transfers between devices, along(): return lax.ppermute(a, 'ch', pairs)  3.16 us
  transfers between devices with their start and end apart: 13, of which 3 were waited for; matrix products, arithmetic and copies ran while one was open for 0% of the time, Pallas kernels for 23%

profile of v4, /device:TPU:32, one launch (start us, length us, event | category | flops | bytes accessed | tf_op | source)
XLA Modules:
  0.0 90.5 jit_solution(8920420935219120910)
XLA Ops:
  0.7 0.1 pad_add_fusion
  0.8 1.5 %shard_map.155 = bf16[32,32,256]{2,1,0:T(8,128)(2,1)S(1)} custom-call(bf16[256,512]{1,0:T(8,128)(2,1)} %refs_1_.5, bf16[256,512]{1,0:T(8,128)(2,1)} %refs_2_.9, f32[256,512]{1,0:T(8,128)} %refs_2_.5, f32[1,512]{1,0:T(1,128)S(1)} %bitcast.5), custom_call_target="tpu_custom_call" | custom-call | flops 23000000512 | bytes 65536 | tf_op jit(solution)/shard_map/pallas_call | solution.py:276
  2.2 0.0 copy-start.2
  2.2 0.8 copy-done.2
  3.0 3.7 %shard_map.156 = bf16[4,512,256]{2,1,0:T(8,128)(2,1)S(1)} custom-call(s32[2]{0:T(128)S(1)} %get-tuple-element.38.refs_0_, bf16[8,512,1024]{2,1,0:T(8,128)(2,1)} %bitcast.6, bf16[256,1024]{1,0:T(8,128)(2,1)S(1)} %copy-done.1), custom_call_target="tpu_custom_call" | custom-call | bytes 65536 | tf_op jit(solution)/shard_map/pallas_call | solution.py:276
  6.7 0.1 collective-permute-start
  6.8 11.2 %all-to-all-start = ((bf16[32,32,256]{2,1,0:T(8,128)(2,1)}), bf16[32,32,256]{2,1,0:T(8,128)(2,1)S(1)}, u32[]{:S(2)}, u32[]{:S(2)}) async-start(bf16[32,32,256]{2,1,0:T(8,128)(2,1)} %copy-done.2), calls=%async_computation | async-start | bytes 1048576 | tf_op jit(solution)/shard_map/all_to_all | solution.py:322
  18.1 2.3 %shard_map.157.refs_0_ = bf16[1,512,256]{2,1,0:T(8,128)(2,1)S(1)} custom-call(s32[2]{0:T(128)S(1)} %get-tuple-element.42.refs_0_, bf16[8,512,1024]{2,1,0:T(8,128)(2,1)} %bitcast.7, bf16[256,1024]{1,0:T(8,128)(2,1)S(1)} %copy-done.1), custom_call_target="tpu_custom_call" | custom-call | flops 11500000256 | bytes 65536 | tf_op jit(solution)/shard_map/pallas_call | solution.py:276
  20.3 0.1 shard_map.158
  20.4 3.3 %collective-permute-start.1 = (bf16[512,256]{1,0:T(8,128)(2,1)S(1)}, bf16[512,256]{1,0:T(8,128)(2,1)S(1)}, u32[]{:S(2)}, u32[]{:S(2)}) collective-permute-start(bf16[512,256]{1,0:T(8,128)(2,1)S(1)} %shard_map.158), channel_id=1, source_target_pairs={{0,4},{1,5},{2,6},{3,7},{4,0},{5,1},{6,2},{7,3},{8,12},{9,13},{10,... | collective-permute-start | bytes 786440 | tf_op jit(solution)/shard_map/ppermute | solution.py:335
  23.7 3.2 %shard_map.159.refs_0_ = bf16[3,512,256]{2,1,0:T(8,128)(2,1)S(1)} custom-call(s32[2]{0:T(128)S(1)} %get-tuple-element.42.refs_0_, bf16[8,512,1024]{2,1,0:T(8,128)(2,1)} %bitcast.8, bf16[256,1024]{1,0:T(8,128)(2,1)S(1)} %copy-done.1), custom_call_target="tpu_custom_call" | custom-call | flops 11500000256 | bytes 65536 | tf_op jit(solution)/shard_map/pallas_call | solution.py:276
  26.9 0.8 shard_map.160
  27.7 0.7 collective-permute-start.2
  28.4 2.6 %collective-permute-start.3 = (bf16[512,256]{1,0:T(8,128)(2,1)S(1)}, bf16[512,256]{1,0:T(8,128)(2,1)S(1)}, u32[]{:S(2)}, u32[]{:S(2)}) collective-permute-start(bf16[512,256]{1,0:T(8,128)(2,1)S(1)} %get-tuple-element.48), channel_id=1, source_target_pairs={{0,6},{1,7},{2,0},{3,1},{4,2},{5,3},{6,4},{7,5},{8,14},{9,15},{10,... | collective-permute-start | bytes 786440 | tf_op jit(solution)/shard_map/ppermute | solution.py:335
  31.0 5.4 %all-to-all-done.refs_1_ = bf16[32,32,256]{2,1,0:T(8,128)(2,1)S(1)} async-done(((bf16[32,32,256]{2,1,0:T(8,128)(2,1)}), bf16[32,32,256]{2,1,0:T(8,128)(2,1)S(1)}, u32[]{:S(2)}, u32[]{:S(2)}) %all-to-all-start) | async-done | bytes 524320 | tf_op jit(solution)/shard_map/all_to_all | solution.py:322
  36.3 2.8 %shard_map.161 = (f32[512,256]{1,0:T(8,128)S(1)}, f32[512,256]{1,0:T(8,128)S(1)}, f32[512,256]{1,0:T(8,128)S(1)}, f32[512,256]{1,0:T(8,128)S(1)}, bf16[512,256]{...) custom-call(s32[2]{0:T(128)S(1)} %get-tuple-element.42.refs_0_, ...), custom_call_target="tpu_custom_call" | custom-call | bytes 65536 | tf_op jit(solution)/shard_map/pallas_call | solution.py:276
  39.2 0.8 shard_map.162
  40.0 0.2 shard_map.163
  40.2 22.9 %all_to_all.15.refs_0_ = bf16[32,32,256]{2,1,0:T(8,128)(2,1)S(1)} all-to-all(bf16[32,32,256]{2,1,0:T(8,128)(2,1)S(1)} %get-tuple-element.60), channel_id=1, replica_groups=mesh['seq'=32,'ch'=8] {'seq'}, dimensions={0} | all-to-all | bytes 1048576 | tf_op jit(solution)/shard_map/all_to_all | solution.py:322
  63.1 0.2 shard_map.164
  63.3 1.7 %collective-permute-start.4 = (bf16[256,512]{1,0:T(8,128)(2,1)S(1)}, bf16[256,512]{1,0:T(8,128)(2,1)S(1)}, u32[]{:S(2)}, u32[]{:S(2)}) collective-permute-start(bf16[256,512]{1,0:T(8,128)(2,1)S(1)} %get-tuple-element.62.refs_11_.refs_1_.refs_2_.refs_8_), channel_id=1, source_target_pairs={{0,2},{1,7},{2,4},{3,1},{4,6},{5,3},{6,0},{7,5},{8,10},{9,15},{10,... | collective-permute-start | bytes 786440 | tf_op jit(solution)/shard_map/ppermute | solution.py:331
  65.0 1.6 %collective-permute-start.7 = (bf16[256,512]{1,0:T(8,128)(2,1)S(1)}, bf16[256,512]{1,0:T(8,128)(2,1)S(1)}, u32[]{:S(2)}, u32[]{:S(2)}) collective-permute-start(bf16[256,512]{1,0:T(8,128)(2,1)S(1)} %get-tuple-element.62.refs_11_.refs_1_.refs_2_.refs_8_), channel_id=1, source_target_pairs={{0,6},{1,3},{2,0},{3,5},{4,2},{5,7},{6,4},{7,1},{8,14},{9,11},{10,... | collective-permute-start | bytes 786440 | tf_op jit(solution)/shard_map/ppermute | solution.py:331
  66.6 2.8 %shard_map.165 = (bf16[32,32,256]{2,1,0:T(8,128)(2,1)}, bf16[256,512]{1,0:T(8,128)(2,1)}) custom-call(bf16[32,32,256]{2,1,0:T(8,128)(2,1)S(1)} %all_to_all.15.refs_0_, bf16[256,512]{1,0:T(8,128)(2,1)S(1)} %get-tuple-element.63.refs_1_, f32[512,256]{1,0:T(8,128)S(1)} %get-tuple-element.49.refs_0_.refs_6_.refs_3_.refs_2_, ...), custom_call_target="tpu_custom_call" | custom-call | bytes 65536 | tf_op jit(solution)/shard_map/pallas_call | solution.py:276
  69.4 4.8 %all-to-all-start.2 = ((bf16[32,32,256]{2,1,0:T(8,128)(2,1)}), bf16[32,32,256]{2,1,0:T(8,128)(2,1)S(1)}, u32[]{:S(2)}, u32[]{:S(2)}) async-start(bf16[32,32,256]{2,1,0:T(8,128)(2,1)} %get-tuple-element.64.refs_0_.refs_2_), calls=%async_computation.2 | async-start | bytes 1048576 | tf_op jit(solution)/shard_map/all_to_all | solution.py:322
  74.3 0.5 collective-permute-start.5
  74.8 0.5 collective-permute-start.10
  75.3 3.5 %shard_map.167.refs_1_ = bf16[8,512,1024]{2,1,0:T(8,128)(2,1)S(1)} custom-call(bf16[8,512,1024]{2,1,0:T(8,128)(2,1)} %bitcast.9, bf16[8,128]{1,0:T(8,128)(2,1)S(1)} %shard_map.166.refs_1_, bf16[32,32,256]{2,1,0:T(8,128)(2,1)} %get-tuple-element.64.refs_0_.refs_2_), custom_call_target="tpu_custom_call" | custom-call | flops 2300000000 | bytes 65536 | tf_op jit(solution)/shard_map/pallas_call | solution.py:276
  78.8 3.2 %collective-permute-done.5.refs_2_ = bf16[256,512]{1,0:T(8,128)(2,1)S(1)} collective-permute-done((bf16[256,512]{1,0:T(8,128)(2,1)S(1)}, bf16[256,512]{1,0:T(8,128)(2,1)S(1)}, u32[]{:S(2)}, u32[]{:S(2)}) %collective-permute-start.5) | collective-permute-done | bytes 262176 | tf_op jit(solution)/shard_map/ppermute | solution.py:331
  82.0 2.4 %shard_map.168.refs_4_ = f32[256,1024]{1,0:T(8,128)S(1)} custom-call(s32[2]{0:T(128)S(1)} %get-tuple-element.42.refs_0_, bf16[8,512,1024]{2,1,0:T(8,128)(2,1)S(1)} %shard_map.167.refs_1_, bf16[256,512]{1,0:T(8,128)(2,1)S(1)} %get-tuple-element.62.refs_11_.refs_1_.refs_2_.refs_8_, bf16[256,512]{1,0:T(8,128)(2,1)S(1)} %collective-permute-done.7.refs_3_, ...), custom_call_target="tpu_custom_call" | custom-call | flops 5750000128 | bytes 65536 | tf_op jit(solution)/shard_map/pallas_call | solution.py:276
  84.4 2.1 %shard_map.169 = bf16[256,1024]{1,0:T(8,128)(2,1)} custom-call(s32[2]{0:T(128)S(1)} %get-tuple-element.42.refs_0_, bf16[8,512,1024]{2,1,0:T(8,128)(2,1)S(1)} %shard_map.167.refs_1_, bf16[256,512]{1,0:T(8,128)(2,1)S(1)} %collective-permute-done.5.refs_2_, bf16[256,512]{1,0:T(8,128)(2,1)S(1)} %collective-permute-done.6.refs_3_, f32[256,1024]{1,0:T(8,128)S(1)} %shard_map.168.refs_4_), custom_call_target="tpu_custom_call" | custom-call | bytes 65536 | tf_op jit(solution)/shard_map/pallas_call | solution.py:276
  86.5 2.9 %all-to-all-done.2.refs_0_ = bf16[32,32,256]{2,1,0:T(8,128)(2,1)S(1)} async-done(((bf16[32,32,256]{2,1,0:T(8,128)(2,1)}), bf16[32,32,256]{2,1,0:T(8,128)(2,1)S(1)}, u32[]{:S(2)}, u32[]{:S(2)}) %all-to-all-start.2) | async-done | bytes 524320 | tf_op jit(solution)/shard_map/all_to_all | solution.py:322
  89.4 1.1 %shard_map.170 = (bf16[256,512]{1,0:T(8,128)(2,1)}, bf16[256,512]{1,0:T(8,128)(2,1)}, f32[256,512]{1,0:T(8,128)}) custom-call(bf16[32,32,256]{2,1,0:T(8,128)(2,1)S(1)} %all-to-all-done.2.refs_0_, bf16[256,512]{1,0:T(8,128)(2,1)S(1)} %copy-done.3, bf16[256,512]{1,0:T(8,128)(2,1)S(1)} %copy-done.4), custom_call_target="tpu_custom_call" | custom-call | bytes 65536 | tf_op jit(solution)/shard_map/pallas_call | solution.py:276
  (23 shorter events, 0.1 us)
Async XLA Ops:
  0.8 2.3 %copy-start.1 = (bf16[256,1024]{1,0:T(8,128)(2,1)S(1)}, bf16[256,1024]{1,0:T(8,128)(2,1)}, u32[]{:S(2)}) copy-start(bf16[256,1024]{1,0:T(8,128)(2,1)} %refs_2_.8) | copy-start | bytes 1572868
  2.2 0.8 copy-start.2
  6.7 13.6 %collective-permute-start = (bf16[4,512,256]{2,1,0:T(8,128)(2,1)S(1)}, bf16[4,512,256]{2,1,0:T(8,128)(2,1)S(1)}, u32[]{:S(2)}, u32[]{:S(2)}) collective-permute-start(bf16[4,512,256]{2,1,0:T(8,128)(2,1)S(1)} %shard_map.156), channel_id=1, source_target_pairs={{0,1},{1,0},{2,3},{3,2},{4,5},{5,4},{6,7},{7,6},{8,9},{9,8},{10,11... | collective-permute-start | bytes 3145736 | tf_op jit(solution)/shard_map/ppermute | solution.py:326
  6.8 29.5 %all-to-all-start = ((bf16[32,32,256]{2,1,0:T(8,128)(2,1)}), bf16[32,32,256]{2,1,0:T(8,128)(2,1)S(1)}, u32[]{:S(2)}, u32[]{:S(2)}) async-start(bf16[32,32,256]{2,1,0:T(8,128)(2,1)} %copy-done.2), calls=%async_computation | async-start | bytes 1048576 | tf_op jit(solution)/shard_map/all_to_all | solution.py:322
  20.4 18.8 %copy-start = (bf16[256,512]{1,0:T(8,128)(2,1)S(1)}, bf16[256,512]{1,0:T(8,128)(2,1)}, u32[]{:S(2)}) copy-start(bf16[256,512]{1,0:T(8,128)(2,1)} %refs_1_.4) | copy-start | bytes 786436
  20.4 15.9 %collective-permute-start.1 = (bf16[512,256]{1,0:T(8,128)(2,1)S(1)}, bf16[512,256]{1,0:T(8,128)(2,1)S(1)}, u32[]{:S(2)}, u32[]{:S(2)}) collective-permute-start(bf16[512,256]{1,0:T(8,128)(2,1)S(1)} %shard_map.158), channel_id=1, source_target_pairs={{0,4},{1,5},{2,6},{3,7},{4,0},{5,1},{6,2},{7,3},{8,12},{9,13},{10,... | collective-permute-start | bytes 786440 | tf_op jit(solution)/shard_map/ppermute | solution.py:335
  27.7 12.3 %collective-permute-start.2 = (bf16[512,256]{1,0:T(8,128)(2,1)S(1)}, bf16[512,256]{1,0:T(8,128)(2,1)S(1)}, u32[]{:S(2)}, u32[]{:S(2)}) collective-permute-start(bf16[512,256]{1,0:T(8,128)(2,1)S(1)} %get-tuple-element.47), channel_id=1, source_target_pairs={{0,2},{1,3},{2,4},{3,5},{4,6},{5,7},{6,0},{7,1},{8,10},{9,11},{10,... | collective-permute-start | bytes 786440 | tf_op jit(solution)/shard_map/ppermute | solution.py:335
  28.4 11.6 %collective-permute-start.3 = (bf16[512,256]{1,0:T(8,128)(2,1)S(1)}, bf16[512,256]{1,0:T(8,128)(2,1)S(1)}, u32[]{:S(2)}, u32[]{:S(2)}) collective-permute-start(bf16[512,256]{1,0:T(8,128)(2,1)S(1)} %get-tuple-element.48), channel_id=1, source_target_pairs={{0,6},{1,7},{2,0},{3,1},{4,2},{5,3},{6,4},{7,5},{8,14},{9,15},{10,... | collective-permute-start | bytes 786440 | tf_op jit(solution)/shard_map/ppermute | solution.py:335
  63.3 11.0 %collective-permute-start.4 = (bf16[256,512]{1,0:T(8,128)(2,1)S(1)}, bf16[256,512]{1,0:T(8,128)(2,1)S(1)}, u32[]{:S(2)}, u32[]{:S(2)}) collective-permute-start(bf16[256,512]{1,0:T(8,128)(2,1)S(1)} %get-tuple-element.62.refs_11_.refs_1_.refs_2_.refs_8_), channel_id=1, source_target_pairs={{0,2},{1,7},{2,4},{3,1},{4,6},{5,3},{6,0},{7,5},{8,10},{9,15},{10,... | collective-permute-start | bytes 786440 | tf_op jit(solution)/shard_map/ppermute | solution.py:331
  65.0 10.3 %collective-permute-start.7 = (bf16[256,512]{1,0:T(8,128)(2,1)S(1)}, bf16[256,512]{1,0:T(8,128)(2,1)S(1)}, u32[]{:S(2)}, u32[]{:S(2)}) collective-permute-start(bf16[256,512]{1,0:T(8,128)(2,1)S(1)} %get-tuple-element.62.refs_11_.refs_1_.refs_2_.refs_8_), channel_id=1, source_target_pairs={{0,6},{1,3},{2,0},{3,5},{4,2},{5,7},{6,4},{7,1},{8,14},{9,11},{10,... | collective-permute-start | bytes 786440 | tf_op jit(solution)/shard_map/ppermute | solution.py:331
  69.4 20.0 %all-to-all-start.2 = ((bf16[32,32,256]{2,1,0:T(8,128)(2,1)}), bf16[32,32,256]{2,1,0:T(8,128)(2,1)S(1)}, u32[]{:S(2)}, u32[]{:S(2)}) async-start(bf16[32,32,256]{2,1,0:T(8,128)(2,1)} %get-tuple-element.64.refs_0_.refs_2_), calls=%async_computation.2 | async-start | bytes 1048576 | tf_op jit(solution)/shard_map/all_to_all | solution.py:322
  74.3 7.7 %collective-permute-start.5 = (bf16[256,512]{1,0:T(8,128)(2,1)S(1)}, bf16[256,512]{1,0:T(8,128)(2,1)S(1)}, u32[]{:S(2)}, u32[]{:S(2)}) collective-permute-start(bf16[256,512]{1,0:T(8,128)(2,1)S(1)} %collective-permute-done.4.refs_4_), channel_id=1, source_target_pairs={{0,2},{1,7},{2,4},{3,1},{4,6},{5,3},{6,0},{7,5},{8,10},{9,15},{10,... | collective-permute-start | bytes 786440 | tf_op jit(solution)/shard_map/ppermute | solution.py:331
  74.8 7.2 %collective-permute-start.8 = (bf16[256,512]{1,0:T(8,128)(2,1)S(1)}, bf16[256,512]{1,0:T(8,128)(2,1)S(1)}, u32[]{:S(2)}, u32[]{:S(2)}) collective-permute-start(bf16[256,512]{1,0:T(8,128)(2,1)S(1)} %get-tuple-element.62.refs_11_.refs_1_.refs_2_.refs_8_), channel_id=1, source_target_pairs={{0,1},{1,0},{2,3},{3,2},{4,5},{5,4},{6,7},{7,6},{8,9},{9,8},{10,11... | collective-permute-start | bytes 786440 | tf_op jit(solution)/shard_map/ppermute | solution.py:326
  74.8 7.2 %collective-permute-start.10 = (bf16[256,512]{1,0:T(8,128)(2,1)S(1)}, bf16[256,512]{1,0:T(8,128)(2,1)S(1)}, u32[]{:S(2)}, u32[]{:S(2)}) collective-permute-start(bf16[256,512]{1,0:T(8,128)(2,1)S(1)} %collective-permute-done.4.refs_4_), channel_id=1, source_target_pairs={{0,1},{1,0},{2,3},{3,2},{4,5},{5,4},{6,7},{7,6},{8,9},{9,8},{10,11... | collective-permute-start | bytes 786440 | tf_op jit(solution)/shard_map/ppermute | solution.py:326
  75.3 6.7 %collective-permute-start.9 = (bf16[256,512]{1,0:T(8,128)(2,1)S(1)}, bf16[256,512]{1,0:T(8,128)(2,1)S(1)}, u32[]{:S(2)}, u32[]{:S(2)}) collective-permute-start(bf16[256,512]{1,0:T(8,128)(2,1)S(1)} %collective-permute-done.7.refs_3_), channel_id=1, source_target_pairs={{0,1},{1,0},{2,3},{3,2},{4,5},{5,4},{6,7},{7,6},{8,9},{9,8},{10,11... | collective-permute-start | bytes 786440 | tf_op jit(solution)/shard_map/ppermute | solution.py:326
  81.9 2.5 %collective-permute-start.6 = (bf16[256,512]{1,0:T(8,128)(2,1)S(1)}, bf16[256,512]{1,0:T(8,128)(2,1)S(1)}, u32[]{:S(2)}, u32[]{:S(2)}) collective-permute-start(bf16[256,512]{1,0:T(8,128)(2,1)S(1)} %collective-permute-done.5.refs_2_), channel_id=1, source_target_pairs={{0,1},{1,0},{2,3},{3,2},{4,5},{5,4},{6,7},{7,6},{8,9},{9,8},{10,11... | collective-permute-start | bytes 786440 | tf_op jit(solution)/shard_map/ppermute | solution.py:326
  84.4 5.0 %copy-start.3 = (bf16[256,512]{1,0:T(8,128)(2,1)S(1)}, bf16[256,512]{1,0:T(8,128)(2,1)}, u32[]{:S(2)}) copy-start(bf16[256,512]{1,0:T(8,128)(2,1)} %refs_1_.5) | copy-start | bytes 786436
  84.4 5.0 %copy-start.4 = (bf16[256,512]{1,0:T(8,128)(2,1)S(1)}, bf16[256,512]{1,0:T(8,128)(2,1)}, u32[]{:S(2)}) copy-start(bf16[256,512]{1,0:T(8,128)(2,1)} %refs_2_.9) | copy-start | bytes 786436

commit v5 on v4

--- a/solution.py
+++ b/solution.py
@@ -222,7 +222,7 @@
 
 
 def token_kernel(sent, hidden, out):
-    out[...] = hidden[:8, :128]
+    out[...] = hidden[:16, :128]
 
 
 def fetch_kernel(weight, hidden, sent, out, sems):
@@ -434,7 +434,7 @@
         after = along(hidden, -1)
     token = local(
         token_kernel,
-        (inside((8, 128), jnp.bfloat16),),
+        (inside((16, 128), jnp.bfloat16),),
         far_memory(sent),
         hidden,
         specs=[HBM, VMEM],

time: 91.3 us -> 91.3 us (level)
  no operation moved by 1% of the time
where the time goes in v5:
time: 91.3 us; the launch traced here: 90.5 us
  Pallas kernels  27.4 us (30%)
  starting transfers between devices  27 us (30%)
  blocking collectives  22.9 us (25%)
  waiting for transfers between devices  11.4 us (12%)
    pallas_call x16, Pallas kernels, local(): pl.pallas_call(body, out_shape=outs, in_specs=list(specs or [VMEM] * n) +...  27.4 us
    all_to_all x1, blocking collectives, exchange(): return lax.all_to_all(a, 'seq', split_axis=0, concat_axis=0, tiled=True)  22.9 us
    all_to_all x2, starting transfers between devices, exchange(): return lax.all_to_all(a, 'seq', split_axis=0, concat_axis=0, tiled=True)  16 us
    all_to_all x2, waiting for transfers between devices, exchange(): return lax.all_to_all(a, 'seq', split_axis=0, concat_axis=0, tiled=True)  8.26 us
    ppermute x3, starting transfers between devices, shifted(): return lax.ppermute(a, 'ch', [(i, (i + 2 * rows) % 8) for i in range(8)])  6.52 us
    ppermute x3, starting transfers between devices, along(): return lax.ppermute(a, 'ch', pairs)  3.81 us
    ppermute x3, waiting for transfers between devices, along(): return lax.ppermute(a, 'ch', pairs)  3.16 us
  transfers between devices with their start and end apart: 13, of which 3 were waited for; matrix products, arithmetic and copies ran while one was open for 0% of the time, Pallas kernels for 23%

profile of v5, /device:TPU:32, one launch (start us, length us, event | category | flops | bytes accessed | tf_op | source)
XLA Modules:
  0.0 90.5 jit_solution(10526961090807748342)
XLA Ops:
  0.7 0.1 pad_add_fusion
  0.8 1.5 %shard_map.155 = bf16[32,32,256]{2,1,0:T(8,128)(2,1)S(1)} custom-call(bf16[256,512]{1,0:T(8,128)(2,1)} %refs_1_.5, bf16[256,512]{1,0:T(8,128)(2,1)} %refs_2_.9, f32[256,512]{1,0:T(8,128)} %refs_2_.5, f32[1,512]{1,0:T(1,128)S(1)} %bitcast.5), custom_call_target="tpu_custom_call" | custom-call | flops 23000000512 | bytes 65536 | tf_op jit(solution)/shard_map/pallas_call | solution.py:276
  2.2 0.0 copy-start.2
  2.2 0.8 copy-done.2
  3.0 3.7 %shard_map.156 = bf16[4,512,256]{2,1,0:T(8,128)(2,1)S(1)} custom-call(s32[2]{0:T(128)S(1)} %get-tuple-element.38.refs_0_, bf16[8,512,1024]{2,1,0:T(8,128)(2,1)} %bitcast.6, bf16[256,1024]{1,0:T(8,128)(2,1)S(1)} %copy-done.1), custom_call_target="tpu_custom_call" | custom-call | bytes 65536 | tf_op jit(solution)/shard_map/pallas_call | solution.py:276
  6.7 0.1 collective-permute-start
  6.8 11.2 %all-to-all-start = ((bf16[32,32,256]{2,1,0:T(8,128)(2,1)}), bf16[32,32,256]{2,1,0:T(8,128)(2,1)S(1)}, u32[]{:S(2)}, u32[]{:S(2)}) async-start(bf16[32,32,256]{2,1,0:T(8,128)(2,1)} %copy-done.2), calls=%async_computation | async-start | bytes 1048576 | tf_op jit(solution)/shard_map/all_to_all | solution.py:322
  18.1 2.3 %shard_map.157.refs_0_ = bf16[1,512,256]{2,1,0:T(8,128)(2,1)S(1)} custom-call(s32[2]{0:T(128)S(1)} %get-tuple-element.42.refs_0_, bf16[8,512,1024]{2,1,0:T(8,128)(2,1)} %bitcast.7, bf16[256,1024]{1,0:T(8,128)(2,1)S(1)} %copy-done.1), custom_call_target="tpu_custom_call" | custom-call | flops 11500000256 | bytes 65536 | tf_op jit(solution)/shard_map/pallas_call | solution.py:276
  20.3 0.1 shard_map.158
  20.4 3.3 %collective-permute-start.1 = (bf16[512,256]{1,0:T(8,128)(2,1)S(1)}, bf16[512,256]{1,0:T(8,128)(2,1)S(1)}, u32[]{:S(2)}, u32[]{:S(2)}) collective-permute-start(bf16[512,256]{1,0:T(8,128)(2,1)S(1)} %shard_map.158), channel_id=1, source_target_pairs={{0,4},{1,5},{2,6},{3,7},{4,0},{5,1},{6,2},{7,3},{8,12},{9,13},{10,... | collective-permute-start | bytes 786440 | tf_op jit(solution)/shard_map/ppermute | solution.py:335
  23.7 3.2 %shard_map.159.refs_0_ = bf16[3,512,256]{2,1,0:T(8,128)(2,1)S(1)} custom-call(s32[2]{0:T(128)S(1)} %get-tuple-element.42.refs_0_, bf16[8,512,1024]{2,1,0:T(8,128)(2,1)} %bitcast.8, bf16[256,1024]{1,0:T(8,128)(2,1)S(1)} %copy-done.1), custom_call_target="tpu_custom_call" | custom-call | flops 11500000256 | bytes 65536 | tf_op jit(solution)/shard_map/pallas_call | solution.py:276
  26.9 0.8 shard_map.160
  27.7 0.7 collective-permute-start.2
  28.4 2.6 %collective-permute-start.3 = (bf16[512,256]{1,0:T(8,128)(2,1)S(1)}, bf16[512,256]{1,0:T(8,128)(2,1)S(1)}, u32[]{:S(2)}, u32[]{:S(2)}) collective-permute-start(bf16[512,256]{1,0:T(8,128)(2,1)S(1)} %get-tuple-element.48), channel_id=1, source_target_pairs={{0,6},{1,7},{2,0},{3,1},{4,2},{5,3},{6,4},{7,5},{8,14},{9,15},{10,... | collective-permute-start | bytes 786440 | tf_op jit(solution)/shard_map/ppermute | solution.py:335
  31.0 5.4 %all-to-all-done.refs_1_ = bf16[32,32,256]{2,1,0:T(8,128)(2,1)S(1)} async-done(((bf16[32,32,256]{2,1,0:T(8,128)(2,1)}), bf16[32,32,256]{2,1,0:T(8,128)(2,1)S(1)}, u32[]{:S(2)}, u32[]{:S(2)}) %all-to-all-start) | async-done | bytes 524320 | tf_op jit(solution)/shard_map/all_to_all | solution.py:322
  36.3 2.8 %shard_map.161 = (f32[512,256]{1,0:T(8,128)S(1)}, f32[512,256]{1,0:T(8,128)S(1)}, f32[512,256]{1,0:T(8,128)S(1)}, f32[512,256]{1,0:T(8,128)S(1)}, bf16[512,256]{...) custom-call(s32[2]{0:T(128)S(1)} %get-tuple-element.42.refs_0_, ...), custom_call_target="tpu_custom_call" | custom-call | bytes 65536 | tf_op jit(solution)/shard_map/pallas_call | solution.py:276
  39.2 0.8 shard_map.162
  40.0 0.2 shard_map.163
  40.2 22.9 %all_to_all.15.refs_0_ = bf16[32,32,256]{2,1,0:T(8,128)(2,1)S(1)} all-to-all(bf16[32,32,256]{2,1,0:T(8,128)(2,1)S(1)} %get-tuple-element.60), channel_id=1, replica_groups=mesh['seq'=32,'ch'=8] {'seq'}, dimensions={0} | all-to-all | bytes 1048576 | tf_op jit(solution)/shard_map/all_to_all | solution.py:322
  63.1 0.2 shard_map.164
  63.3 1.7 %collective-permute-start.4 = (bf16[256,512]{1,0:T(8,128)(2,1)S(1)}, bf16[256,512]{1,0:T(8,128)(2,1)S(1)}, u32[]{:S(2)}, u32[]{:S(2)}) collective-permute-start(bf16[256,512]{1,0:T(8,128)(2,1)S(1)} %get-tuple-element.62.refs_11_.refs_1_.refs_2_.refs_8_), channel_id=1, source_target_pairs={{0,2},{1,7},{2,4},{3,1},{4,6},{5,3},{6,0},{7,5},{8,10},{9,15},{10,... | collective-permute-start | bytes 786440 | tf_op jit(solution)/shard_map/ppermute | solution.py:331
  65.0 1.6 %collective-permute-start.7 = (bf16[256,512]{1,0:T(8,128)(2,1)S(1)}, bf16[256,512]{1,0:T(8,128)(2,1)S(1)}, u32[]{:S(2)}, u32[]{:S(2)}) collective-permute-start(bf16[256,512]{1,0:T(8,128)(2,1)S(1)} %get-tuple-element.62.refs_11_.refs_1_.refs_2_.refs_8_), channel_id=1, source_target_pairs={{0,6},{1,3},{2,0},{3,5},{4,2},{5,7},{6,4},{7,1},{8,14},{9,11},{10,... | collective-permute-start | bytes 786440 | tf_op jit(solution)/shard_map/ppermute | solution.py:331
  66.6 2.8 %shard_map.165 = (bf16[32,32,256]{2,1,0:T(8,128)(2,1)}, bf16[256,512]{1,0:T(8,128)(2,1)}) custom-call(bf16[32,32,256]{2,1,0:T(8,128)(2,1)S(1)} %all_to_all.15.refs_0_, bf16[256,512]{1,0:T(8,128)(2,1)S(1)} %get-tuple-element.63.refs_1_, f32[512,256]{1,0:T(8,128)S(1)} %get-tuple-element.49.refs_0_.refs_6_.refs_3_.refs_2_, ...), custom_call_target="tpu_custom_call" | custom-call | bytes 65536 | tf_op jit(solution)/shard_map/pallas_call | solution.py:276
  69.4 4.8 %all-to-all-start.2 = ((bf16[32,32,256]{2,1,0:T(8,128)(2,1)}), bf16[32,32,256]{2,1,0:T(8,128)(2,1)S(1)}, u32[]{:S(2)}, u32[]{:S(2)}) async-start(bf16[32,32,256]{2,1,0:T(8,128)(2,1)} %get-tuple-element.64.refs_0_.refs_2_), calls=%async_computation.2 | async-start | bytes 1048576 | tf_op jit(solution)/shard_map/all_to_all | solution.py:322
  74.3 0.5 collective-permute-start.5
  74.8 0.5 collective-permute-start.10
  75.3 3.5 %shard_map.167.refs_1_ = bf16[8,512,1024]{2,1,0:T(8,128)(2,1)S(1)} custom-call(bf16[8,512,1024]{2,1,0:T(8,128)(2,1)} %bitcast.9, bf16[16,128]{1,0:T(8,128)(2,1)S(1)} %shard_map.166.refs_1_, bf16[32,32,256]{2,1,0:T(8,128)(2,1)} %get-tuple-element.64.refs_0_.refs_2_), custom_call_target="tpu_custom_call" | custom-call | flops 2300000000 | bytes 65536 | tf_op jit(solution)/shard_map/pallas_call | solution.py:276
  78.8 3.2 %collective-permute-done.5.refs_2_ = bf16[256,512]{1,0:T(8,128)(2,1)S(1)} collective-permute-done((bf16[256,512]{1,0:T(8,128)(2,1)S(1)}, bf16[256,512]{1,0:T(8,128)(2,1)S(1)}, u32[]{:S(2)}, u32[]{:S(2)}) %collective-permute-start.5) | collective-permute-done | bytes 262176 | tf_op jit(solution)/shard_map/ppermute | solution.py:331
  82.0 2.4 %shard_map.168.refs_4_ = f32[256,1024]{1,0:T(8,128)S(1)} custom-call(s32[2]{0:T(128)S(1)} %get-tuple-element.42.refs_0_, bf16[8,512,1024]{2,1,0:T(8,128)(2,1)S(1)} %shard_map.167.refs_1_, bf16[256,512]{1,0:T(8,128)(2,1)S(1)} %get-tuple-element.62.refs_11_.refs_1_.refs_2_.refs_8_, bf16[256,512]{1,0:T(8,128)(2,1)S(1)} %collective-permute-done.7.refs_3_, ...), custom_call_target="tpu_custom_call" | custom-call | flops 5750000128 | bytes 65536 | tf_op jit(solution)/shard_map/pallas_call | solution.py:276
  84.4 2.1 %shard_map.169 = bf16[256,1024]{1,0:T(8,128)(2,1)} custom-call(s32[2]{0:T(128)S(1)} %get-tuple-element.42.refs_0_, bf16[8,512,1024]{2,1,0:T(8,128)(2,1)S(1)} %shard_map.167.refs_1_, bf16[256,512]{1,0:T(8,128)(2,1)S(1)} %collective-permute-done.5.refs_2_, bf16[256,512]{1,0:T(8,128)(2,1)S(1)} %collective-permute-done.6.refs_3_, f32[256,1024]{1,0:T(8,128)S(1)} %shard_map.168.refs_4_), custom_call_target="tpu_custom_call" | custom-call | bytes 65536 | tf_op jit(solution)/shard_map/pallas_call | solution.py:276
  86.5 2.9 %all-to-all-done.2.refs_0_ = bf16[32,32,256]{2,1,0:T(8,128)(2,1)S(1)} async-done(((bf16[32,32,256]{2,1,0:T(8,128)(2,1)}), bf16[32,32,256]{2,1,0:T(8,128)(2,1)S(1)}, u32[]{:S(2)}, u32[]{:S(2)}) %all-to-all-start.2) | async-done | bytes 524320 | tf_op jit(solution)/shard_map/all_to_all | solution.py:322
  89.4 1.1 %shard_map.170 = (bf16[256,512]{1,0:T(8,128)(2,1)}, bf16[256,512]{1,0:T(8,128)(2,1)}, f32[256,512]{1,0:T(8,128)}) custom-call(bf16[32,32,256]{2,1,0:T(8,128)(2,1)S(1)} %all-to-all-done.2.refs_0_, bf16[256,512]{1,0:T(8,128)(2,1)S(1)} %copy-done.3, bf16[256,512]{1,0:T(8,128)(2,1)S(1)} %copy-done.4), custom_call_target="tpu_custom_call" | custom-call | bytes 65536 | tf_op jit(solution)/shard_map/pallas_call | solution.py:276
  (23 shorter events, 0.1 us)
Async XLA Ops:
  0.8 2.3 %copy-start.1 = (bf16[256,1024]{1,0:T(8,128)(2,1)S(1)}, bf16[256,1024]{1,0:T(8,128)(2,1)}, u32[]{:S(2)}) copy-start(bf16[256,1024]{1,0:T(8,128)(2,1)} %refs_2_.8) | copy-start | bytes 1572868
  2.2 0.8 copy-start.2
  6.7 13.6 %collective-permute-start = (bf16[4,512,256]{2,1,0:T(8,128)(2,1)S(1)}, bf16[4,512,256]{2,1,0:T(8,128)(2,1)S(1)}, u32[]{:S(2)}, u32[]{:S(2)}) collective-permute-start(bf16[4,512,256]{2,1,0:T(8,128)(2,1)S(1)} %shard_map.156), channel_id=1, source_target_pairs={{0,1},{1,0},{2,3},{3,2},{4,5},{5,4},{6,7},{7,6},{8,9},{9,8},{10,11... | collective-permute-start | bytes 3145736 | tf_op jit(solution)/shard_map/ppermute | solution.py:326
  6.8 29.5 %all-to-all-start = ((bf16[32,32,256]{2,1,0:T(8,128)(2,1)}), bf16[32,32,256]{2,1,0:T(8,128)(2,1)S(1)}, u32[]{:S(2)}, u32[]{:S(2)}) async-start(bf16[32,32,256]{2,1,0:T(8,128)(2,1)} %copy-done.2), calls=%async_computation | async-start | bytes 1048576 | tf_op jit(solution)/shard_map/all_to_all | solution.py:322
  20.4 18.8 %copy-start = (bf16[256,512]{1,0:T(8,128)(2,1)S(1)}, bf16[256,512]{1,0:T(8,128)(2,1)}, u32[]{:S(2)}) copy-start(bf16[256,512]{1,0:T(8,128)(2,1)} %refs_1_.4) | copy-start | bytes 786436
  20.4 15.9 %collective-permute-start.1 = (bf16[512,256]{1,0:T(8,128)(2,1)S(1)}, bf16[512,256]{1,0:T(8,128)(2,1)S(1)}, u32[]{:S(2)}, u32[]{:S(2)}) collective-permute-start(bf16[512,256]{1,0:T(8,128)(2,1)S(1)} %shard_map.158), channel_id=1, source_target_pairs={{0,4},{1,5},{2,6},{3,7},{4,0},{5,1},{6,2},{7,3},{8,12},{9,13},{10,... | collective-permute-start | bytes 786440 | tf_op jit(solution)/shard_map/ppermute | solution.py:335
  27.7 12.3 %collective-permute-start.2 = (bf16[512,256]{1,0:T(8,128)(2,1)S(1)}, bf16[512,256]{1,0:T(8,128)(2,1)S(1)}, u32[]{:S(2)}, u32[]{:S(2)}) collective-permute-start(bf16[512,256]{1,0:T(8,128)(2,1)S(1)} %get-tuple-element.47), channel_id=1, source_target_pairs={{0,2},{1,3},{2,4},{3,5},{4,6},{5,7},{6,0},{7,1},{8,10},{9,11},{10,... | collective-permute-start | bytes 786440 | tf_op jit(solution)/shard_map/ppermute | solution.py:335
  28.4 11.6 %collective-permute-start.3 = (bf16[512,256]{1,0:T(8,128)(2,1)S(1)}, bf16[512,256]{1,0:T(8,128)(2,1)S(1)}, u32[]{:S(2)}, u32[]{:S(2)}) collective-permute-start(bf16[512,256]{1,0:T(8,128)(2,1)S(1)} %get-tuple-element.48), channel_id=1, source_target_pairs={{0,6},{1,7},{2,0},{3,1},{4,2},{5,3},{6,4},{7,5},{8,14},{9,15},{10,... | collective-permute-start | bytes 786440 | tf_op jit(solution)/shard_map/ppermute | solution.py:335
  63.3 11.0 %collective-permute-start.4 = (bf16[256,512]{1,0:T(8,128)(2,1)S(1)}, bf16[256,512]{1,0:T(8,128)(2,1)S(1)}, u32[]{:S(2)}, u32[]{:S(2)}) collective-permute-start(bf16[256,512]{1,0:T(8,128)(2,1)S(1)} %get-tuple-element.62.refs_11_.refs_1_.refs_2_.refs_8_), channel_id=1, source_target_pairs={{0,2},{1,7},{2,4},{3,1},{4,6},{5,3},{6,0},{7,5},{8,10},{9,15},{10,... | collective-permute-start | bytes 786440 | tf_op jit(solution)/shard_map/ppermute | solution.py:331
  65.0 10.3 %collective-permute-start.7 = (bf16[256,512]{1,0:T(8,128)(2,1)S(1)}, bf16[256,512]{1,0:T(8,128)(2,1)S(1)}, u32[]{:S(2)}, u32[]{:S(2)}) collective-permute-start(bf16[256,512]{1,0:T(8,128)(2,1)S(1)} %get-tuple-element.62.refs_11_.refs_1_.refs_2_.refs_8_), channel_id=1, source_target_pairs={{0,6},{1,3},{2,0},{3,5},{4,2},{5,7},{6,4},{7,1},{8,14},{9,11},{10,... | collective-permute-start | bytes 786440 | tf_op jit(solution)/shard_map/ppermute | solution.py:331
  69.4 20.0 %all-to-all-start.2 = ((bf16[32,32,256]{2,1,0:T(8,128)(2,1)}), bf16[32,32,256]{2,1,0:T(8,128)(2,1)S(1)}, u32[]{:S(2)}, u32[]{:S(2)}) async-start(bf16[32,32,256]{2,1,0:T(8,128)(2,1)} %get-tuple-element.64.refs_0_.refs_2_), calls=%async_computation.2 | async-start | bytes 1048576 | tf_op jit(solution)/shard_map/all_to_all | solution.py:322
  74.3 7.7 %collective-permute-start.5 = (bf16[256,512]{1,0:T(8,128)(2,1)S(1)}, bf16[256,512]{1,0:T(8,128)(2,1)S(1)}, u32[]{:S(2)}, u32[]{:S(2)}) collective-permute-start(bf16[256,512]{1,0:T(8,128)(2,1)S(1)} %collective-permute-done.4.refs_4_), channel_id=1, source_target_pairs={{0,2},{1,7},{2,4},{3,1},{4,6},{5,3},{6,0},{7,5},{8,10},{9,15},{10,... | collective-permute-start | bytes 786440 | tf_op jit(solution)/shard_map/ppermute | solution.py:331
  74.8 7.2 %collective-permute-start.8 = (bf16[256,512]{1,0:T(8,128)(2,1)S(1)}, bf16[256,512]{1,0:T(8,128)(2,1)S(1)}, u32[]{:S(2)}, u32[]{:S(2)}) collective-permute-start(bf16[256,512]{1,0:T(8,128)(2,1)S(1)} %get-tuple-element.62.refs_11_.refs_1_.refs_2_.refs_8_), channel_id=1, source_target_pairs={{0,1},{1,0},{2,3},{3,2},{4,5},{5,4},{6,7},{7,6},{8,9},{9,8},{10,11... | collective-permute-start | bytes 786440 | tf_op jit(solution)/shard_map/ppermute | solution.py:326
  74.8 7.2 %collective-permute-start.10 = (bf16[256,512]{1,0:T(8,128)(2,1)S(1)}, bf16[256,512]{1,0:T(8,128)(2,1)S(1)}, u32[]{:S(2)}, u32[]{:S(2)}) collective-permute-start(bf16[256,512]{1,0:T(8,128)(2,1)S(1)} %collective-permute-done.4.refs_4_), channel_id=1, source_target_pairs={{0,1},{1,0},{2,3},{3,2},{4,5},{5,4},{6,7},{7,6},{8,9},{9,8},{10,11... | collective-permute-start | bytes 786440 | tf_op jit(solution)/shard_map/ppermute | solution.py:326
  75.3 6.7 %collective-permute-start.9 = (bf16[256,512]{1,0:T(8,128)(2,1)S(1)}, bf16[256,512]{1,0:T(8,128)(2,1)S(1)}, u32[]{:S(2)}, u32[]{:S(2)}) collective-permute-start(bf16[256,512]{1,0:T(8,128)(2,1)S(1)} %collective-permute-done.7.refs_3_), channel_id=1, source_target_pairs={{0,1},{1,0},{2,3},{3,2},{4,5},{5,4},{6,7},{7,6},{8,9},{9,8},{10,11... | collective-permute-start | bytes 786440 | tf_op jit(solution)/shard_map/ppermute | solution.py:326
  81.9 2.5 %collective-permute-start.6 = (bf16[256,512]{1,0:T(8,128)(2,1)S(1)}, bf16[256,512]{1,0:T(8,128)(2,1)S(1)}, u32[]{:S(2)}, u32[]{:S(2)}) collective-permute-start(bf16[256,512]{1,0:T(8,128)(2,1)S(1)} %collective-permute-done.5.refs_2_), channel_id=1, source_target_pairs={{0,1},{1,0},{2,3},{3,2},{4,5},{5,4},{6,7},{7,6},{8,9},{9,8},{10,11... | collective-permute-start | bytes 786440 | tf_op jit(solution)/shard_map/ppermute | solution.py:326
  84.4 5.0 %copy-start.3 = (bf16[256,512]{1,0:T(8,128)(2,1)S(1)}, bf16[256,512]{1,0:T(8,128)(2,1)}, u32[]{:S(2)}) copy-start(bf16[256,512]{1,0:T(8,128)(2,1)} %refs_1_.5) | copy-start | bytes 786436
  84.4 5.0 %copy-start.4 = (bf16[256,512]{1,0:T(8,128)(2,1)S(1)}, bf16[256,512]{1,0:T(8,128)(2,1)}, u32[]{:S(2)}) copy-start(bf16[256,512]{1,0:T(8,128)(2,1)} %refs_2_.9) | copy-start | bytes 786436

commit v6 on v5

--- a/solution.py
+++ b/solution.py
@@ -225,29 +225,54 @@
     out[...] = hidden[:16, :128]
 
 
-def fetch_kernel(weight, hidden, sent, out, sems):
-    @pl.loop(0, 8)
-    def _(i):
-        pltpu.make_async_copy(weight.at[i], out.at[i], sems.at[i]).start()
-
-    @pl.loop(0, 8)
-    def _(i):
-        pltpu.make_async_copy(weight.at[i], out.at[i], sems.at[i]).wait()
-
-
-def mixed_kernel(where, weight, *refs):
-    parts, base, out = refs[:-2], refs[-2], refs[-1]
-    blocks = (0, 1 - 2 * where[1], 2 * where[1] - 1) if len(parts) == 6 else (2,)
-    blocks = [2 * ((where[0] + b) & 3) + where[1] for b in blocks]
-    mirror = (0, 2 * where[1] - 1, 1 - 2 * where[1]) if len(parts) == 6 else (2,)
-    blocks += [2 * ((where[0] + b) & 3) + 1 - where[1] for b in mirror]
+def block_ids(where):
+    row, core, turn = where[0], where[1], 2 * where[1] - 1
+    near = [2 * (r & 3) + core for r in (row, row - turn, row + turn)]
+    far = [2 * (r & 3) + 1 - core for r in (row, row + turn, row - turn)]
+    return near + far, [2 * ((row + 2) & 3) + core, 2 * ((row + 2) & 3) + 1 - core]
+
+
+def fetch_kernel(where, weight, token, sent, out, sems):
+    copies = [
+        pltpu.make_async_copy(weight.at[block], out.at[i], sems.at[i])
+        for i, block in enumerate(block_ids(where)[0])
+    ]
+    for copy in copies:
+        copy.start()
+    for copy in copies:
+        copy.wait()
+
+
+def near_mixed_kernel(where, weight, kept, *refs):
+    parts, (out, rest, sems) = refs[:6], refs[6:]
+    copies = [
+        pltpu.make_async_copy(weight.at[block], rest.at[i], sems.at[i])
+        for i, block in enumerate(block_ids(where)[1])
+    ]
+
+    @pl.when(where[0] >= 0)
+    def _():
+        for copy in copies:
+            copy.start()
+
+    @pl.when(where[0] >= 0)
+    def _():
+        for c in range(0, COLUMNS, 256):
+            columns = slice(c, c + 256)
+            total = dot(parts[0][...], kept[0, :, columns])
+            for i in range(1, 6):
+                total += dot(parts[i][...], kept[i, :, columns])
+            out[:, columns] = total
+
+    for copy in copies:
+        copy.wait()
+
+
+def far_mixed_kernel(rest, near, far, base, out):
     for c in range(0, COLUMNS, 256):
         columns = slice(c, c + 256)
-        total = base[:, columns] if len(parts) == 2 else None
-        for part, block in zip(parts, blocks):
-            term = dot(part[...], weight[block, :, columns])
-            total = term if total is None else total + term
-        out[:, columns] = total.astype(out.dtype)
+        total = base[:, columns] + dot(near[...], rest[0, :, columns])
+        out[:, columns] = bf16(total + dot(far[...], rest[1, :, columns]))
 
 
 def shape(dims, dtype):
@@ -302,19 +327,6 @@
         specs=[SMEM, HBM, VMEM],
         scratch=[pltpu.VMEM((count, WIDTH, COLUMNS), jnp.bfloat16), pltpu.SemaphoreType.DMA((count,))],
         cost=cost,
-    )[0]
-
-
-def mix(where, weight, parts, base, out):
-    return local(
-        mixed_kernel,
-        (out((ROWS, COLUMNS), jnp.float32 if out is inside else jnp.bfloat16),),
-        where,
-        weight,
-        *parts,
-        base,
-        specs=[SMEM] + [VMEM] * (2 + len(parts)),
-        cost=COSTS[3] if out is inside else COSTS[4],
     )[0]
 
 
@@ -444,19 +456,39 @@
         after = along(turned_back, -1)
     kept_weight = local(
         fetch_kernel,
-        (inside(weight.shape, weight.dtype),),
+        (inside((6, WIDTH, COLUMNS), weight.dtype),),
+        near_half,
         weight,
         token,
         far_memory(sent),
-        specs=[HBM, VMEM, HBM],
-        scratch=[pltpu.SemaphoreType.DMA((8,))],
+        specs=[SMEM, HBM, VMEM, HBM],
+        scratch=[pltpu.SemaphoreType.DMA((6,))],
         cost=COSTS[2],
     )[0]
     across = along(passed, 1)
     near = [hidden, after, before]
     far = [to_partner(a) for a in near]
-    part = mix(near_half, kept_weight, near + far, hidden, inside)
-    mixed = mix(near_half, kept_weight, [across, to_partner(across)], part, outside)
+    part, rest = local(
+        near_mixed_kernel,
+        (inside((ROWS, COLUMNS), jnp.float32), inside((2, WIDTH, COLUMNS), weight.dtype)),
+        near_half,
+        weight,
+        kept_weight,
+        *near,
+        *far,
+        specs=[SMEM, HBM] + [VMEM] * 7,
+        scratch=[pltpu.SemaphoreType.DMA((2,))],
+        cost=COSTS[3],
+    )
+    mixed = local(
+        far_mixed_kernel,
+        (outside((ROWS, COLUMNS), jnp.bfloat16),),
+        rest,
+        across,
+        to_partner(across),
+        part,
+        cost=COSTS[4],
+    )[0]
     inner_grad, values_grad, taps_grad = local(
         final_kernel,
         (

time: 91.3 us -> 91.3 us (level)
  transfers between devices with their start and end apart: 13 -> 13, of which waited for: 3 -> 3; matrix products, arithmetic and copies ran while one was open for 0% -> 0% of each run, Pallas kernels for 23% -> 22%
where the time goes in v6:
time: 91.3 us; the launch traced here: 90.5 us
  starting transfers between devices  27 us (30%)
  Pallas kernels  26.8 us (29%)
  blocking collectives  22.9 us (25%)
  waiting for transfers between devices  12 us (13%)
    pallas_call x16, Pallas kernels, local(): pl.pallas_call(body, out_shape=outs, in_specs=list(specs or [VMEM] * n) +...  26.8 us
    all_to_all x1, blocking collectives, exchange(): return lax.all_to_all(a, 'seq', split_axis=0, concat_axis=0, tiled=True)  22.9 us
    all_to_all x2, starting transfers between devices, exchange(): return lax.all_to_all(a, 'seq', split_axis=0, concat_axis=0, tiled=True)  16 us
    all_to_all x2, waiting for transfers between devices, exchange(): return lax.all_to_all(a, 'seq', split_axis=0, concat_axis=0, tiled=True)  8.82 us
    ppermute x3, starting transfers between devices, shifted(): return lax.ppermute(a, 'ch', [(i, (i + 2 * rows) % 8) for i in range(8)])  6.52 us
    ppermute x3, starting transfers between devices, along(): return lax.ppermute(a, 'ch', pairs)  3.81 us
    ppermute x3, waiting for transfers between devices, along(): return lax.ppermute(a, 'ch', pairs)  3.19 us
  transfers between devices with their start and end apart: 13, of which 3 were waited for; matrix products, arithmetic and copies ran while one was open for 0% of the time, Pallas kernels for 22%

profile of v6, /device:TPU:32, one launch (start us, length us, event | category | flops | bytes accessed | tf_op | source)
XLA Modules:
  0.0 90.5 jit_solution(16058822847090057154)
XLA Ops:
  0.7 0.1 pad_add_fusion
  0.8 1.5 %shard_map.155 = bf16[32,32,256]{2,1,0:T(8,128)(2,1)S(1)} custom-call(bf16[256,512]{1,0:T(8,128)(2,1)} %refs_1_.5, bf16[256,512]{1,0:T(8,128)(2,1)} %refs_2_.9, f32[256,512]{1,0:T(8,128)} %refs_2_.5, f32[1,512]{1,0:T(1,128)S(1)} %bitcast.5), custom_call_target="tpu_custom_call" | custom-call | flops 23000000512 | bytes 65536 | tf_op jit(solution)/shard_map/pallas_call | solution.py:301
  2.2 0.8 copy-done.2
  3.0 3.7 %shard_map.156 = bf16[4,512,256]{2,1,0:T(8,128)(2,1)S(1)} custom-call(s32[2]{0:T(128)S(1)} %get-tuple-element.40.refs_0_, bf16[8,512,1024]{2,1,0:T(8,128)(2,1)} %bitcast.6, bf16[256,1024]{1,0:T(8,128)(2,1)S(1)} %copy-done.1), custom_call_target="tpu_custom_call" | custom-call | bytes 65536 | tf_op jit(solution)/shard_map/pallas_call | solution.py:301
  6.7 0.1 collective-permute-start
  6.8 11.2 %all-to-all-start = ((bf16[32,32,256]{2,1,0:T(8,128)(2,1)}), bf16[32,32,256]{2,1,0:T(8,128)(2,1)S(1)}, u32[]{:S(2)}, u32[]{:S(2)}) async-start(bf16[32,32,256]{2,1,0:T(8,128)(2,1)} %copy-done.2), calls=%async_computation | async-start | bytes 1048576 | tf_op jit(solution)/shard_map/all_to_all | solution.py:334
  18.1 2.3 %shard_map.157.refs_0_ = bf16[1,512,256]{2,1,0:T(8,128)(2,1)S(1)} custom-call(s32[2]{0:T(128)S(1)} %get-tuple-element.44.refs_0_, bf16[8,512,1024]{2,1,0:T(8,128)(2,1)} %bitcast.7, bf16[256,1024]{1,0:T(8,128)(2,1)S(1)} %copy-done.1), custom_call_target="tpu_custom_call" | custom-call | flops 11500000256 | bytes 65536 | tf_op jit(solution)/shard_map/pallas_call | solution.py:301
  20.3 0.1 shard_map.158
  20.4 3.3 %collective-permute-start.1 = (bf16[512,256]{1,0:T(8,128)(2,1)S(1)}, bf16[512,256]{1,0:T(8,128)(2,1)S(1)}, u32[]{:S(2)}, u32[]{:S(2)}) collective-permute-start(bf16[512,256]{1,0:T(8,128)(2,1)S(1)} %shard_map.158), channel_id=1, source_target_pairs={{0,4},{1,5},{2,6},{3,7},{4,0},{5,1},{6,2},{7,3},{8,12},{9,13},{10,... | collective-permute-start | bytes 786440 | tf_op jit(solution)/shard_map/ppermute | solution.py:347
  23.7 3.2 %shard_map.159.refs_0_ = bf16[3,512,256]{2,1,0:T(8,128)(2,1)S(1)} custom-call(s32[2]{0:T(128)S(1)} %get-tuple-element.44.refs_0_, bf16[8,512,1024]{2,1,0:T(8,128)(2,1)} %bitcast.8, bf16[256,1024]{1,0:T(8,128)(2,1)S(1)} %copy-done.1), custom_call_target="tpu_custom_call" | custom-call | flops 11500000256 | bytes 65536 | tf_op jit(solution)/shard_map/pallas_call | solution.py:301
  26.9 0.8 shard_map.160
  27.7 0.7 collective-permute-start.2
  28.4 2.6 %collective-permute-start.3 = (bf16[512,256]{1,0:T(8,128)(2,1)S(1)}, bf16[512,256]{1,0:T(8,128)(2,1)S(1)}, u32[]{:S(2)}, u32[]{:S(2)}) collective-permute-start(bf16[512,256]{1,0:T(8,128)(2,1)S(1)} %get-tuple-element.50), channel_id=1, source_target_pairs={{0,6},{1,7},{2,0},{3,1},{4,2},{5,3},{6,4},{7,5},{8,14},{9,15},{10,... | collective-permute-start | bytes 786440 | tf_op jit(solution)/shard_map/ppermute | solution.py:347
  31.0 5.4 %all-to-all-done.refs_1_ = bf16[32,32,256]{2,1,0:T(8,128)(2,1)S(1)} async-done(((bf16[32,32,256]{2,1,0:T(8,128)(2,1)}), bf16[32,32,256]{2,1,0:T(8,128)(2,1)S(1)}, u32[]{:S(2)}, u32[]{:S(2)}) %all-to-all-start) | async-done | bytes 524320 | tf_op jit(solution)/shard_map/all_to_all | solution.py:334
  36.3 2.8 %shard_map.161 = (f32[512,256]{1,0:T(8,128)S(1)}, f32[512,256]{1,0:T(8,128)S(1)}, f32[512,256]{1,0:T(8,128)S(1)}, f32[512,256]{1,0:T(8,128)S(1)}, bf16[512,256]{...) custom-call(s32[2]{0:T(128)S(1)} %get-tuple-element.44.refs_0_, ...), custom_call_target="tpu_custom_call" | custom-call | bytes 65536 | tf_op jit(solution)/shard_map/pallas_call | solution.py:301
  39.2 0.8 shard_map.162
  40.0 0.2 shard_map.163
  40.2 22.9 %all_to_all.15.refs_0_ = bf16[32,32,256]{2,1,0:T(8,128)(2,1)S(1)} all-to-all(bf16[32,32,256]{2,1,0:T(8,128)(2,1)S(1)} %get-tuple-element.62), channel_id=1, replica_groups=mesh['seq'=32,'ch'=8] {'seq'}, dimensions={0} | all-to-all | bytes 1048576 | tf_op jit(solution)/shard_map/all_to_all | solution.py:334
  63.1 0.2 shard_map.164
  63.3 1.7 %collective-permute-start.4 = (bf16[256,512]{1,0:T(8,128)(2,1)S(1)}, bf16[256,512]{1,0:T(8,128)(2,1)S(1)}, u32[]{:S(2)}, u32[]{:S(2)}) collective-permute-start(bf16[256,512]{1,0:T(8,128)(2,1)S(1)} %get-tuple-element.64.refs_11_.refs_1_.refs_3_), channel_id=1, source_target_pairs={{0,2},{1,7},{2,4},{3,1},{4,6},{5,3},{6,0},{7,5},{8,10},{9,15},{10,... | collective-permute-start | bytes 786440 | tf_op jit(solution)/shard_map/ppermute | solution.py:343
  65.0 1.6 %collective-permute-start.5 = (bf16[256,512]{1,0:T(8,128)(2,1)S(1)}, bf16[256,512]{1,0:T(8,128)(2,1)S(1)}, u32[]{:S(2)}, u32[]{:S(2)}) collective-permute-start(bf16[256,512]{1,0:T(8,128)(2,1)S(1)} %get-tuple-element.64.refs_11_.refs_1_.refs_3_), channel_id=1, source_target_pairs={{0,6},{1,3},{2,0},{3,5},{4,2},{5,7},{6,4},{7,1},{8,14},{9,11},{10,... | collective-permute-start | bytes 786440 | tf_op jit(solution)/shard_map/ppermute | solution.py:343
  66.6 2.8 %shard_map.165 = (bf16[32,32,256]{2,1,0:T(8,128)(2,1)}, bf16[256,512]{1,0:T(8,128)(2,1)}) custom-call(bf16[32,32,256]{2,1,0:T(8,128)(2,1)S(1)} %all_to_all.15.refs_0_, bf16[256,512]{1,0:T(8,128)(2,1)S(1)} %get-tuple-element.65.refs_1_, f32[512,256]{1,0:T(8,128)S(1)} %get-tuple-element.51.refs_0_.refs_6_.refs_3_.refs_2_, ...), custom_call_target="tpu_custom_call" | custom-call | bytes 65536 | tf_op jit(solution)/shard_map/pallas_call | solution.py:301
  69.4 4.8 %all-to-all-start.2 = ((bf16[32,32,256]{2,1,0:T(8,128)(2,1)}), bf16[32,32,256]{2,1,0:T(8,128)(2,1)S(1)}, u32[]{:S(2)}, u32[]{:S(2)}) async-start(bf16[32,32,256]{2,1,0:T(8,128)(2,1)} %get-tuple-element.66.refs_0_.refs_3_), calls=%async_computation.2 | async-start | bytes 1048576 | tf_op jit(solution)/shard_map/all_to_all | solution.py:334
  74.3 0.5 collective-permute-start.9
  74.8 0.5 collective-permute-start.7
  75.3 0.0 collective-permute-start.8
  75.3 3.4 %shard_map.167.refs_2_ = bf16[6,512,1024]{2,1,0:T(8,128)(2,1)S(1)} custom-call(s32[2]{0:T(128)S(1)} %get-tuple-element.44.refs_0_, bf16[8,512,1024]{2,1,0:T(8,128)(2,1)} %bitcast.9, bf16[16,128]{1,0:T(8,128)(2,1)S(1)} %shard_map.166.refs_2_, bf16[32,32,256]{2,1,0:T(8,128)(2,1)} %get-tuple-element.66.refs_0_.refs_3_), custom_call_target="tpu_custom_call" | custom-call | flops 2300000000 | bytes 65536 | tf_op jit(solution)/shard_map/pallas_call | solution.py:301
  78.8 3.2 %collective-permute-done.9.refs_1_ = bf16[256,512]{1,0:T(8,128)(2,1)S(1)} collective-permute-done((bf16[256,512]{1,0:T(8,128)(2,1)S(1)}, bf16[256,512]{1,0:T(8,128)(2,1)S(1)}, u32[]{:S(2)}, u32[]{:S(2)}) %collective-permute-start.9) | collective-permute-done | bytes 262176 | tf_op jit(solution)/shard_map/ppermute | solution.py:343
  82.0 2.4 %shard_map.168 = (f32[256,1024]{1,0:T(8,128)S(1)}, bf16[2,512,1024]{2,1,0:T(8,128)(2,1)S(1)}) custom-call(s32[2]{0:T(128)S(1)} %get-tuple-element.44.refs_0_, bf16[8,512,1024]{2,1,0:T(8,128)(2,1)} %bitcast.10, bf16[6,512,1024]{2,1,0:T(8,128)(2,1)S(1)} %shard_map.167.refs_2_, bf16[256,512]{1,0:T(8,128)(2,1)S(1)} %get-tuple-element.64.refs_11_.refs_1_.refs_3_, ...), custom_call_target="tpu_custom_call" | custom-call | flops 5750000128 | bytes 65536 | tf_op jit(solution)/shard_map/pallas_call | solution.py:301
  84.4 1.5 %shard_map.169 = bf16[256,1024]{1,0:T(8,128)(2,1)} custom-call(bf16[2,512,1024]{2,1,0:T(8,128)(2,1)S(1)} %get-tuple-element.68.refs_0_, bf16[256,512]{1,0:T(8,128)(2,1)S(1)} %collective-permute-done.9.refs_1_, bf16[256,512]{1,0:T(8,128)(2,1)S(1)} %collective-permute-done.10.refs_2_, f32[256,1024]{1,0:T(8,128)S(1)} %get-tuple-element.70.refs_3_), custom_call_target="tpu_custom_call" | custom-call | bytes 65536 | tf_op jit(solution)/shard_map/pallas_call | solution.py:301
  85.9 3.5 %all-to-all-done.2.refs_0_ = bf16[32,32,256]{2,1,0:T(8,128)(2,1)S(1)} async-done(((bf16[32,32,256]{2,1,0:T(8,128)(2,1)}), bf16[32,32,256]{2,1,0:T(8,128)(2,1)S(1)}, u32[]{:S(2)}, u32[]{:S(2)}) %all-to-all-start.2) | async-done | bytes 524320 | tf_op jit(solution)/shard_map/all_to_all | solution.py:334
  89.4 1.1 %shard_map.170 = (bf16[256,512]{1,0:T(8,128)(2,1)}, bf16[256,512]{1,0:T(8,128)(2,1)}, f32[256,512]{1,0:T(8,128)}) custom-call(bf16[32,32,256]{2,1,0:T(8,128)(2,1)S(1)} %all-to-all-done.2.refs_0_, bf16[256,512]{1,0:T(8,128)(2,1)S(1)} %copy-done.3, bf16[256,512]{1,0:T(8,128)(2,1)S(1)} %copy-done.4), custom_call_target="tpu_custom_call" | custom-call | bytes 65536 | tf_op jit(solution)/shard_map/pallas_call | solution.py:301
  (23 shorter events, 0.1 us)
Async XLA Ops:
  0.8 2.3 %copy-start.1 = (bf16[256,1024]{1,0:T(8,128)(2,1)S(1)}, bf16[256,1024]{1,0:T(8,128)(2,1)}, u32[]{:S(2)}) copy-start(bf16[256,1024]{1,0:T(8,128)(2,1)} %refs_2_.8) | copy-start | bytes 1572868
  2.2 0.8 copy-start.2
  6.7 13.6 %collective-permute-start = (bf16[4,512,256]{2,1,0:T(8,128)(2,1)S(1)}, bf16[4,512,256]{2,1,0:T(8,128)(2,1)S(1)}, u32[]{:S(2)}, u32[]{:S(2)}) collective-permute-start(bf16[4,512,256]{2,1,0:T(8,128)(2,1)S(1)} %shard_map.156), channel_id=1, source_target_pairs={{0,1},{1,0},{2,3},{3,2},{4,5},{5,4},{6,7},{7,6},{8,9},{9,8},{10,11... | collective-permute-start | bytes 3145736 | tf_op jit(solution)/shard_map/ppermute | solution.py:338
  6.8 29.5 %all-to-all-start = ((bf16[32,32,256]{2,1,0:T(8,128)(2,1)}), bf16[32,32,256]{2,1,0:T(8,128)(2,1)S(1)}, u32[]{:S(2)}, u32[]{:S(2)}) async-start(bf16[32,32,256]{2,1,0:T(8,128)(2,1)} %copy-done.2), calls=%async_computation | async-start | bytes 1048576 | tf_op jit(solution)/shard_map/all_to_all | solution.py:334
  20.4 18.8 %copy-start = (bf16[256,512]{1,0:T(8,128)(2,1)S(1)}, bf16[256,512]{1,0:T(8,128)(2,1)}, u32[]{:S(2)}) copy-start(bf16[256,512]{1,0:T(8,128)(2,1)} %refs_1_.4) | copy-start | bytes 786436
  20.4 15.9 %collective-permute-start.1 = (bf16[512,256]{1,0:T(8,128)(2,1)S(1)}, bf16[512,256]{1,0:T(8,128)(2,1)S(1)}, u32[]{:S(2)}, u32[]{:S(2)}) collective-permute-start(bf16[512,256]{1,0:T(8,128)(2,1)S(1)} %shard_map.158), channel_id=1, source_target_pairs={{0,4},{1,5},{2,6},{3,7},{4,0},{5,1},{6,2},{7,3},{8,12},{9,13},{10,... | collective-permute-start | bytes 786440 | tf_op jit(solution)/shard_map/ppermute | solution.py:347
  27.7 12.3 %collective-permute-start.2 = (bf16[512,256]{1,0:T(8,128)(2,1)S(1)}, bf16[512,256]{1,0:T(8,128)(2,1)S(1)}, u32[]{:S(2)}, u32[]{:S(2)}) collective-permute-start(bf16[512,256]{1,0:T(8,128)(2,1)S(1)} %get-tuple-element.49), channel_id=1, source_target_pairs={{0,2},{1,3},{2,4},{3,5},{4,6},{5,7},{6,0},{7,1},{8,10},{9,11},{10,... | collective-permute-start | bytes 786440 | tf_op jit(solution)/shard_map/ppermute | solution.py:347
  28.4 11.6 %collective-permute-start.3 = (bf16[512,256]{1,0:T(8,128)(2,1)S(1)}, bf16[512,256]{1,0:T(8,128)(2,1)S(1)}, u32[]{:S(2)}, u32[]{:S(2)}) collective-permute-start(bf16[512,256]{1,0:T(8,128)(2,1)S(1)} %get-tuple-element.50), channel_id=1, source_target_pairs={{0,6},{1,7},{2,0},{3,1},{4,2},{5,3},{6,4},{7,5},{8,14},{9,15},{10,... | collective-permute-start | bytes 786440 | tf_op jit(solution)/shard_map/ppermute | solution.py:347
  63.3 11.0 %collective-permute-start.4 = (bf16[256,512]{1,0:T(8,128)(2,1)S(1)}, bf16[256,512]{1,0:T(8,128)(2,1)S(1)}, u32[]{:S(2)}, u32[]{:S(2)}) collective-permute-start(bf16[256,512]{1,0:T(8,128)(2,1)S(1)} %get-tuple-element.64.refs_11_.refs_1_.refs_3_), channel_id=1, source_target_pairs={{0,2},{1,7},{2,4},{3,1},{4,6},{5,3},{6,0},{7,5},{8,10},{9,15},{10,... | collective-permute-start | bytes 786440 | tf_op jit(solution)/shard_map/ppermute | solution.py:343
  65.0 9.8 %collective-permute-start.5 = (bf16[256,512]{1,0:T(8,128)(2,1)S(1)}, bf16[256,512]{1,0:T(8,128)(2,1)S(1)}, u32[]{:S(2)}, u32[]{:S(2)}) collective-permute-start(bf16[256,512]{1,0:T(8,128)(2,1)S(1)} %get-tuple-element.64.refs_11_.refs_1_.refs_3_), channel_id=1, source_target_pairs={{0,6},{1,3},{2,0},{3,5},{4,2},{5,7},{6,4},{7,1},{8,14},{9,11},{10,... | collective-permute-start | bytes 786440 | tf_op jit(solution)/shard_map/ppermute | solution.py:343
  69.4 20.0 %all-to-all-start.2 = ((bf16[32,32,256]{2,1,0:T(8,128)(2,1)}), bf16[32,32,256]{2,1,0:T(8,128)(2,1)S(1)}, u32[]{:S(2)}, u32[]{:S(2)}) async-start(bf16[32,32,256]{2,1,0:T(8,128)(2,1)} %get-tuple-element.66.refs_0_.refs_3_), calls=%async_computation.2 | async-start | bytes 1048576 | tf_op jit(solution)/shard_map/all_to_all | solution.py:334
  74.3 7.7 %collective-permute-start.9 = (bf16[256,512]{1,0:T(8,128)(2,1)S(1)}, bf16[256,512]{1,0:T(8,128)(2,1)S(1)}, u32[]{:S(2)}, u32[]{:S(2)}) collective-permute-start(bf16[256,512]{1,0:T(8,128)(2,1)S(1)} %collective-permute-done.4.refs_5_), channel_id=1, source_target_pairs={{0,2},{1,7},{2,4},{3,1},{4,6},{5,3},{6,0},{7,5},{8,10},{9,15},{10,... | collective-permute-start | bytes 786440 | tf_op jit(solution)/shard_map/ppermute | solution.py:343
  74.8 7.2 %collective-permute-start.6 = (bf16[256,512]{1,0:T(8,128)(2,1)S(1)}, bf16[256,512]{1,0:T(8,128)(2,1)S(1)}, u32[]{:S(2)}, u32[]{:S(2)}) collective-permute-start(bf16[256,512]{1,0:T(8,128)(2,1)S(1)} %get-tuple-element.64.refs_11_.refs_1_.refs_3_), channel_id=1, source_target_pairs={{0,1},{1,0},{2,3},{3,2},{4,5},{5,4},{6,7},{7,6},{8,9},{9,8},{10,11... | collective-permute-start | bytes 786440 | tf_op jit(solution)/shard_map/ppermute | solution.py:338
  74.8 7.2 %collective-permute-start.7 = (bf16[256,512]{1,0:T(8,128)(2,1)S(1)}, bf16[256,512]{1,0:T(8,128)(2,1)S(1)}, u32[]{:S(2)}, u32[]{:S(2)}) collective-permute-start(bf16[256,512]{1,0:T(8,128)(2,1)S(1)} %collective-permute-done.5.refs_4_), channel_id=1, source_target_pairs={{0,1},{1,0},{2,3},{3,2},{4,5},{5,4},{6,7},{7,6},{8,9},{9,8},{10,11... | collective-permute-start | bytes 786440 | tf_op jit(solution)/shard_map/ppermute | solution.py:338
  75.3 6.7 %collective-permute-start.8 = (bf16[256,512]{1,0:T(8,128)(2,1)S(1)}, bf16[256,512]{1,0:T(8,128)(2,1)S(1)}, u32[]{:S(2)}, u32[]{:S(2)}) collective-permute-start(bf16[256,512]{1,0:T(8,128)(2,1)S(1)} %collective-permute-done.4.refs_5_), channel_id=1, source_target_pairs={{0,1},{1,0},{2,3},{3,2},{4,5},{5,4},{6,7},{7,6},{8,9},{9,8},{10,11... | collective-permute-start | bytes 786440 | tf_op jit(solution)/shard_map/ppermute | solution.py:338
  78.7 10.6 %copy-start.3 = (bf16[256,512]{1,0:T(8,128)(2,1)S(1)}, bf16[256,512]{1,0:T(8,128)(2,1)}, u32[]{:S(2)}) copy-start(bf16[256,512]{1,0:T(8,128)(2,1)} %refs_1_.5) | copy-start | bytes 786436
  78.7 10.6 %copy-start.4 = (bf16[256,512]{1,0:T(8,128)(2,1)S(1)}, bf16[256,512]{1,0:T(8,128)(2,1)}, u32[]{:S(2)}) copy-start(bf16[256,512]{1,0:T(8,128)(2,1)} %refs_2_.9) | copy-start | bytes 786436
  81.9 2.4 %collective-permute-start.10 = (bf16[256,512]{1,0:T(8,128)(2,1)S(1)}, bf16[256,512]{1,0:T(8,128)(2,1)S(1)}, u32[]{:S(2)}, u32[]{:S(2)}) collective-permute-start(bf16[256,512]{1,0:T(8,128)(2,1)S(1)} %collective-permute-done.9.refs_1_), channel_id=1, source_target_pairs={{0,1},{1,0},{2,3},{3,2},{4,5},{5,4},{6,7},{7,6},{8,9},{9,8},{10,11... | collective-permute-start | bytes 786440 | tf_op jit(solution)/shard_map/ppermute | solution.py:338
